TPU v7x, 128 devices: a whole 4x4x4 slice. The times are simulated.
128 devices in a mesh: dp: 16 (over z, x), ctx: 8 (over y, core).
Axes of the slice: x: 4, y: 4, z: 4, core: 2. Of those that a mesh axis runs over, the one named last changes fastest.
Arguments:
- grad_query: bfloat16 [128, 1536, 6144], P(('dp', 'ctx')), may hold values from -6 to 6
- grad_key: bfloat16 [128, 512, 4096], P(('dp', 'ctx')), may hold values from -6 to 6
- query_weight: float32 [1536, 6144], P('ctx', 'dp'), may hold values from -1.25 to 1.25
- key_weight: float32 [512, 4096], P('ctx', 'dp'), may hold values from -1.25 to 1.25
- query_moment: float32 [1536, 6144], P('ctx', 'dp'), may hold values from -6 to 6
- key_moment: float32 [512, 4096], P('ctx', 'dp'), may hold values from -6 to 6
- max_logits: float32 [128, 32], P(('dp', 'ctx')), may hold values from 20 to 300, as said below
Outputs:
- new_query_weight: bfloat16 [1536, 6144], P('ctx')
- new_key_weight: bfloat16 [512, 4096], P('ctx')
- new_query_moment: float32 [1536, 6144], P('ctx', 'dp')
- new_key_moment: float32 [512, 4096], P('ctx', 'dp')
Inputs may be any that keep to these rules, and one draw needn't show every extreme that they name: `max_logits`: for every head one device holds a value clearly larger than all the others of that head.
All inputs are finite; a program needn't handle non-finite values.
Results may differ from a plain program's by a relative error of at most 0.014.
Values may be sent and summed in bfloat16 or wider, within the bound.
No kernel may reach another device: no remote copies, remote signals or barrier semaphores. Data moves between devices by JAX's collectives and lax.ppermute only.
A program may use at most 128 MiB of HBM per device.

v0:
```python
import math

import jax
import jax.numpy as jnp
from jax import lax
from jax.sharding import PartitionSpec as P

QL = 1536
KVL = 512
QH = 192
QROPE = 64
KH = 128
ITERS = 5


momentum_decay = 0.9
learn_rate = 0.2
weight_decay = 0.1
clip_limit = 100.0
norm_epsilon = 1e-07
coef_first = 3.4445
coef_second = -4.775
coef_third = 2.0315


def unchanged(first_value, second_value):
    return (first_value, second_value)


def iterate_blocks(blocks, gram):
    mixer = coef_second * gram + coef_third * jnp.einsum(
        "hij,hjk->hik", gram, gram, precision=lax.Precision.HIGHEST
    )
    return coef_first * blocks + jnp.einsum(
        "rhi,hij->rhj", blocks, mixer, precision=lax.Precision.HIGHEST
    )


def orthogonal_pair(query_part, key_part, total_norms, total_grams):
    query_blocks = query_part.reshape(query_part.shape[0], -1, QH)
    key_blocks = key_part.reshape(key_part.shape[0], -1, KH)
    query_norm, key_norm = total_norms(
        jnp.sum(query_blocks * query_blocks, axis=(0, 2)),
        jnp.sum(key_blocks * key_blocks, axis=(0, 2)),
    )
    query_blocks = query_blocks / (jnp.sqrt(query_norm) + norm_epsilon)[None, :, None]
    key_blocks = key_blocks / (jnp.sqrt(key_norm) + norm_epsilon)[None, :, None]
    for iteration in range(ITERS):
        query_gram = jnp.einsum(
            "rhi,rhj->hij", query_blocks, query_blocks, precision=lax.Precision.HIGHEST
        )
        key_gram = jnp.einsum(
            "rhi,rhj->hij", key_blocks, key_blocks, precision=lax.Precision.HIGHEST
        )
        query_gram, key_gram = total_grams(query_gram, key_gram)
        query_blocks = iterate_blocks(query_blocks, query_gram)
        key_blocks = iterate_blocks(key_blocks, key_gram)
    return (
        query_blocks.reshape(query_part.shape[0], -1),
        key_blocks.reshape(key_part.shape[0], -1),
    )


def head_factors(gamma, head_width, rope_width):
    position = jnp.arange(head_width)
    root = jnp.sqrt(gamma)
    table = jnp.where(position[None, :] < head_width - rope_width, root[:, None], gamma[:, None])
    return table.reshape(-1)


def on_device(grad_query, grad_key, query_weight, key_weight, query_moment, key_moment, max_logits):
    query_terms = grad_query[0]
    key_terms = grad_key[0]
    query_cols, key_cols = (
        lax.psum_scatter(query_terms, "dp", scatter_dimension=1, tiled=True).astype(jnp.float32),
        lax.psum_scatter(key_terms, "dp", scatter_dimension=1, tiled=True).astype(jnp.float32),
    )
    query_grad, key_grad = (
        lax.psum_scatter(query_cols, "ctx", scatter_dimension=0, tiled=True),
        lax.psum_scatter(key_cols, "ctx", scatter_dimension=0, tiled=True),
    )
    new_query_moment = momentum_decay * query_moment + query_grad
    new_key_moment = momentum_decay * key_moment + key_grad
    peak = lax.pmax(max_logits[0], ("dp", "ctx"))
    query_full, key_full = (
        lax.all_gather(new_query_moment, "ctx", axis=0, tiled=True),
        lax.all_gather(new_key_moment, "ctx", axis=0, tiled=True),
    )
    query_whole, key_whole = orthogonal_pair(query_full, key_full, unchanged, unchanged)
    context_index = lax.axis_index("ctx")
    query_ortho = lax.dynamic_slice_in_dim(
        query_whole, context_index * query_weight.shape[0], query_weight.shape[0], 0
    )
    key_ortho = lax.dynamic_slice_in_dim(
        key_whole, context_index * key_weight.shape[0], key_weight.shape[0], 0
    )
    local_heads = query_weight.shape[1] // QH
    gamma = jnp.minimum(1.0, clip_limit / peak)
    gamma_local = lax.dynamic_slice_in_dim(
        gamma, lax.axis_index("dp") * local_heads, local_heads, 0
    )
    query_scale = 0.2 * math.sqrt(max(QL, QH))
    key_scale = 0.2 * math.sqrt(max(KVL, KH))
    query_next = query_weight - learn_rate * (
        query_scale * query_ortho + weight_decay * query_weight
    )
    key_next = key_weight - learn_rate * (key_scale * key_ortho + weight_decay * key_weight)
    query_block = (query_next * head_factors(gamma_local, QH, QROPE)[None, :]).astype(jnp.bfloat16)
    key_block = (key_next * head_factors(gamma_local, KH, 0)[None, :]).astype(jnp.bfloat16)
    query_out, key_out = (
        lax.all_gather(query_block, "dp", axis=1, tiled=True),
        lax.all_gather(key_block, "dp", axis=1, tiled=True),
    )
    return (query_out, key_out, new_query_moment, new_key_moment)


def solution(mesh):
    in_specs = (
        P(("dp", "ctx"), None, None),
        P(("dp", "ctx"), None, None),
        P("ctx", "dp"),
        P("ctx", "dp"),
        P("ctx", "dp"),
        P("ctx", "dp"),
        P(("dp", "ctx"), None),
    )
    out_specs = (P("ctx", None), P("ctx", None), P("ctx", "dp"), P("ctx", "dp"))
    return jax.shard_map(
        on_device, mesh=mesh, in_specs=in_specs, out_specs=out_specs, check_vma=False
    )
```

profile of v0, /device:TPU:8, one launch (start us, length us, event | category | flops | bytes accessed | tf_op | source)
XLA Modules:
  0.0 447.6 jit_solution(6363278111768553981)
XLA Ops:
  7.2 24.7 %copy.103 = bf16[1536,6144]{0,1:T(8,128)(2,1)} copy(bf16[1536,6144]{1,0:T(8,128)(2,1)} %bitcast.108) | data formatting | bytes 37748736
  32.0 0.7 reduce-scatter.9.cloned.1.call-update
  32.7 122.9 %reduce-scatter.13.cloned.1.call-done = bf16[384,1536]{1,0:T(8,128)(2,1)} async-done(((bf16[6144,1536]{1,0:T(8,128)(2,1)}), bf16[384,1536]{1,0:T(8,128)(2,1)}) %reduce-scatter.13.cloned.1.call-update) | async-done | bytes 1179664
  155.6 1.7 copy.104
  157.3 1.6 convert_element_type.12
  158.9 77.4 %reduce-scatter.9.cloned.1.call-done = bf16[512,256]{1,0:T(8,128)(2,1)} async-done(((bf16[512,4096]{1,0:T(8,128)(2,1)}), bf16[512,256]{1,0:T(8,128)(2,1)}) %reduce-scatter.9.cloned.1.call-update) | async-done | bytes 262160 | tf_op jit(solution)/shard_map/reduce_scatter | solution.py:76
  236.3 1.8 convert_element_type.14
  238.2 31.4 %reduce-scatter.7.cloned.1.call-done = f32[192,384]{1,0:T(8,128)} async-done(((f32[1536,384]{1,0:T(8,128)}), f32[192,384]{1,0:T(8,128)}) %reduce-scatter.7.cloned.1.call-update) | async-done | bytes 294928 | tf_op jit(solution)/shard_map/reduce_scatter | solution.py:79
  269.5 1.7 multiply_add_fusion
  271.3 66.6 %pmax.7 = f32[32]{0:T(128)S(1)} all-reduce(f32[32]{0:T(128)S(1)} %bitcast.117), channel_id=1, replica_groups=mesh['dp'=16,'ctx'=8] {'dp','ctx'}, use_global_device_ids=true, to_apply=%region_4.0 | all-reduce | flops 32 | bytes 256 | tf_op jit(solution)/shard_map/pmax | solution.py:84
  338.3 0.9 multiply_add_fusion.1
  339.2 13.2 %all_gather.14 = f32[512,256]{1,0:T(8,128)S(1)} all-gather(f32[64,256]{1,0:T(8,128)S(1)} %multiply_add_fusion.1), channel_id=1, replica_groups=mesh['dp'=16,'ctx'=8] {'ctx'}, dimensions={0}, use_global_device_ids=true | all-gather | bytes 589824 | tf_op jit(solution)/shard_map/all_gather | solution.py:87
  352.5 2.1 multiply_reduce_fusion
  354.9 2.4 copy.59
  357.3 5.0 %fusion.20 = f32[2,192,192]{2,1,0:T(8,128)S(1)} fusion(f32[1536,2,192]{0,2,1:T(8,128)} %bitcast.111, f32[2]{0:T(128)S(1)} %sqrt_add_fusion.1), kind=kOutput, calls=%fused_computation.43 | convolution fusion | flops 1359544320 | bytes 2654216 | tf_op jit(solution)/shard_map/rhi,rhj->hij/dot_general | solution.py:49
  362.9 2.5 fusion.4
  365.4 2.3 fusion.23
  368.3 2.5 fusion.3
  370.8 2.5 fusion.24
  373.8 2.5 fusion.2
  376.3 2.3 fusion.25
  379.1 2.5 fusion.1
  381.6 2.3 fusion.26
  383.9 0.8 fusion.10
  384.7 2.5 fusion
  387.5 0.7 multiply_convert_fusion
  388.6 0.7 fusion.21
  389.6 0.7 fusion.5
  396.9 24.3 %all_gather.15 = bf16[64,4096]{1,0:T(8,128)(2,1)S(1)} all-gather(bf16[64,256]{1,0:T(8,128)(2,1)S(1)} %multiply_convert_fusion.1), channel_id=1, replica_groups=mesh['dp'=16,'ctx'=8] {'dp'}, dimensions={1}, use_global_device_ids=true | all-gather | bytes 557056 | tf_op jit(solution)/shard_map/all_gather | solution.py:112
  421.2 15.2 %all-gather.5.cloned.1.call-done = bf16[192,6144]{1,0:T(8,128)(2,1)} async-done(((bf16[192,384]{1,0:T(8,128)(2,1)}), bf16[192,6144]{1,0:T(8,128)(2,1)}) %all-gather.5.cloned.1.call-update) | async-done | bytes 2359312 | tf_op jit(solution)/shard_map/all_gather | solution.py:111
  436.4 3.3 copy.109
  439.7 0.8 copy.110
  (65 shorter events, 10.6 us)
Async XLA Ops:
  7.2 148.4 %reduce-scatter.13.cloned.1.call-start = ((), (), s32[]{:S(2)}) async-start(), calls=%async_computation.9 | async-start | bytes 20054016
  31.9 204.4 %reduce-scatter.9.cloned.1.call-start = ((), (), s32[]{:S(2)}) async-start(), calls=%async_computation.7 | async-start | bytes 4456448 | tf_op jit(solution)/shard_map/reduce_scatter | solution.py:76
  32.7 236.9 %reduce-scatter.7.cloned.1.call-start = ((), (), s32[]{:S(2)}) async-start(), calls=%async_computation.4 | async-start | bytes 2654208 | tf_op jit(solution)/shard_map/reduce_scatter | solution.py:79
  158.8 110.7 %copy-start.2 = (f32[192,384]{1,0:T(8,128)S(1)}, f32[192,384]{1,0:T(8,128)}, u32[]{:S(2)}) copy-start(f32[192,384]{1,0:T(8,128)} %param.11) | copy-start | bytes 884740
  158.8 112.5 %copy-start.7 = (f32[1,32]{1,0:T(1,128)S(1)}, f32[1,32]{1,0:T(1,128)}, u32[]{:S(2)}) copy-start(f32[1,32]{1,0:T(1,128)} %param.13) | copy-start | bytes 388
  158.8 179.5 %copy-start.5 = (f32[64,256]{1,0:T(8,128)S(1)}, f32[64,256]{1,0:T(8,128)}, u32[]{:S(2)}) copy-start(f32[64,256]{1,0:T(8,128)} %param.12) | copy-start | bytes 196612
  158.9 179.4 %reduce-scatter.11.cloned.1.call-start = ((), (), s32[]{:S(2)}) async-start(), calls=%async_computation.8 | async-start | bytes 589824 | tf_op jit(solution)/shard_map/reduce_scatter | solution.py:80
  238.1 114.4 %all-gather.3.cloned.1.call-start = ((), (), s32[]{:S(2)}) async-start(), calls=%async_computation.5 | async-start | bytes 2654208 | tf_op jit(solution)/shard_map/all_gather | solution.py:86
  271.3 165.1 %all-gather.5.cloned.1.call-start = ((), (), s32[]{:S(2)}) async-start(), calls=%async_computation.6 | async-start | bytes 2506752 | tf_op jit(solution)/shard_map/all_gather | solution.py:111
  339.2 18.1 %copy-start.4 = (f32[64,256]{1,0:T(8,128)}, f32[64,256]{1,0:T(8,128)S(1)}, u32[]{:S(2)}) copy-start(f32[64,256]{1,0:T(8,128)S(1)} %multiply_add_fusion.1) | copy-start | bytes 196612
  352.5 2.4 copy-start
  357.3 5.6 %copy-start.1 = (f32[1536,384]{0,1:T(8,128)S(1)}, f32[1536,384]{0,1:T(8,128)}, u32[]{:S(2)}) copy-start(f32[1536,384]{0,1:T(8,128)} %copy.59) | copy-start | bytes 7077892
  384.7 2.8 copy-start.3
  394.1 2.7 copy-start.6
Sparse Core Ops, SparseCore 0:
  32.0 123.4 reduce-scatter.12
  158.9 77.3 reduce-scatter.8
  239.5 30.0 reduce-scatter.6
  272.5 30.2 reduce-scatter.10
  304.8 26.2 all-gather.2
  388.4 47.9 all-gather.4
where the time goes:
time: 452 us; the launch traced here: 448 us
  waiting for transfers between devices  248 us (55%)
  blocking collectives  104 us (23%)
  matrix products  37.7 us (8%)
  local copies, waits for them, and re-layouts  33.9 us (8%)
  between operations  14.7 us (3%)
  other arithmetic  9.22 us (2%)
    unnamed x7, waiting for transfers between devices  124 us
    reduce_scatter x1, waiting for transfers between devices, on_device(): lax.psum_scatter(key_terms, 'dp', scatter_dimension=1, tiled=True)  77.4 us
    pmax x1, blocking collectives, on_device(): peak = lax.pmax(max_logits[0], ('dp', 'ctx'))  66.6 us
    reduce_scatter x1, waiting for transfers between devices, on_device(): lax.psum_scatter(query_cols, 'ctx', scatter_dimension=0, tiled=True)  31.4 us
    unnamed x22, local copies, waits for them, and re-layouts  30.8 us
    all_gather x1, blocking collectives, on_device(): lax.all_gather(key_block, 'dp', axis=1, tiled=True)  24.3 us
    dot_general x10, matrix products, iterate_blocks(): jnp.einsum('rhi,hij->rhj', blocks, mixer, precision=lax.Precision.HIGHEST)  15.7 us
    all_gather x1, waiting for transfers between devices, on_device(): lax.all_gather(query_block, 'dp', axis=1, tiled=True)  15.2 us
  transfers between devices with their start and end apart: 6, of which 4 were waited for; matrix products, arithmetic and copies ran while one was open for 4% of the time, Pallas kernels for 0%

commit v1 on v0

v1 whole, which is shorter than its diff:
```python
import functools
import math

import jax
import jax.numpy as jnp
from jax import lax
from jax.experimental import pallas as pl
from jax.experimental.pallas import tpu as pltpu
from jax.sharding import PartitionSpec as P

QL = 1536
KVL = 512
QH = 192
QROPE = 64
KH = 128
ITERS = 5

momentum_decay = 0.9
learn_rate = 0.2
weight_decay = 0.1
clip_limit = 100.0
norm_epsilon = 1e-07
coef_first = 3.4445
coef_second = -4.775
coef_third = 2.0315

N = 4
QC, KC = 384, 256
QR, KR = 192, 64
RA, RB, RC = 80, 80, 32
MC = RC * 3 + KR * 2
G_ROWS = 384
HQ, HK = QR // 2, KR // 2
H_ROWS = HQ * 3 + HK * 2

f32, bf16 = jnp.float32, jnp.bfloat16
AXES = ("dp", "ctx")
VMEM = pl.BlockSpec(memory_space=pltpu.VMEM)
SMEM = pl.BlockSpec(memory_space=pltpu.SMEM)
ANY = pl.BlockSpec(memory_space=pl.ANY)
HIGHEST = lax.Precision.HIGHEST


def place(z, x, y, c):
    return ((z % N) * N + x % N) * 2 * N + (y % N) * 2 + c


def send(array, target):
    pairs = [
        (place(z, x, y, c), place(*target(z, x, y, c)))
        for z in range(N)
        for x in range(N)
        for y in range(N)
        for c in range(2)
    ]
    return lax.ppermute(array, AXES, pairs)


def shift(array, axis, by):
    def target(z, x, y, c):
        return (z + by * (axis == "z"), x + by * (axis == "x"), y + by * (axis == "y"), c)

    return send(array, target)


def ring(array, axis):
    def target(z, x, y, c):
        by = 1 - 2 * c
        return (z + by * (axis == "z"), x + by * (axis == "x"), y + by * (axis == "y"), c)

    return send(array, target)


def swap(array):
    return send(array, lambda z, x, y, c: (z, x, y, 1 - c))


def exchange(array, axis, step):
    def target(z, x, y, c):
        return (
            z ^ (step * (axis == "z")),
            x ^ (step * (axis == "x")),
            y ^ (step * (axis == "y")),
            c,
        )

    return send(array, target)


def slice_copies(where, other, step, query, key, query_to, key_to, sems):
    z, x, y, core = where[0], where[1], where[2], where[3]
    if other:
        core = 1 - core
    ahead = (1 - 2 * core) * (N - step) + N
    block_a, block_b, block_c = (x + ahead) % N, (z + ahead) % N, (y + ahead) % N
    copies = ([], [], [])

    def add(part, source, to):
        number = sum(len(c) for c in copies)
        copies[part].append(pltpu.make_async_copy(source, to, sems.at[number]))

    def columns(zz, xx, width):
        return pl.ds(pl.multiple_of((zz * N + xx) * width, 128), width)

    for zz in range(N):
        add(
            0,
            query.at[:, core, pl.ds(0, RA), columns(zz, block_a, QC)],
            query_to.at[:, zz, pl.ds(0, RA), :],
        )
    for xx in range(N):
        add(
            1,
            query.at[:, core, pl.ds(RA, RB), columns(block_b, xx, QC)],
            query_to.at[xx, :, pl.ds(RA, RB), :],
        )
    for zz in range(N):
        for xx in range(N):
            add(
                2,
                query.at[block_c, core, pl.ds(RA + RB, RC), columns(zz, xx, QC)],
                query_to.at[zz, xx, pl.ds(RA + RB, RC), :],
            )
            add(2, key.at[block_c, core, :, columns(zz, xx, KC)], key_to.at[zz, xx])
    return copies


N_COPIES = 4 + 4 + 32


def slice_kernel(step, where, query, key, query_to, key_to, sems):
    copies = slice_copies(where, True, step, query, key, query_to, key_to, sems)
    for part in copies:
        for copy in part:
            copy.start()
    for part in copies:
        for copy in part:
            copy.wait()


def slice_other(step, where, query, key):
    return pl.pallas_call(
        functools.partial(slice_kernel, step),
        out_shape=(
            jax.ShapeDtypeStruct((N, N, QR, QC), bf16),
            jax.ShapeDtypeStruct((N, N, KR, KC), bf16),
        ),
        in_specs=[SMEM, ANY, ANY],
        out_specs=(ANY, ANY),
        scratch_shapes=[pltpu.SemaphoreType.DMA((N_COPIES,))],
        compiler_params=pltpu.CompilerParams(vmem_limit_bytes=4 << 20),
        name=f"slice_other_{step}",
    )(where, query, key)


def pre_kernel(step, where, query, key, query_from, key_from, a, b, c, own_q, own_k, sems):
    copies = slice_copies(where, False, step, query, key, own_q, own_k, sems)
    for part in copies:
        for copy in part:
            copy.start()

    def total(first, second):
        return (first.astype(f32) + second.astype(f32)).astype(bf16)

    def each(body):
        @pl.loop(0, N * N)
        def _(i):
            body(i // N, i % N)

    for copy in copies[0]:
        copy.wait()

    @each
    def _(i, j):
        rows = pl.ds(0, RA)
        a[i, j] = total(own_q[i, j, rows, :], query_from[i, j, rows, :])

    for copy in copies[1]:
        copy.wait()

    @each
    def _(i, j):
        rows = pl.ds(RA, RB)
        b[i, j] = total(own_q[i, j, rows, :], query_from[i, j, rows, :])

    for copy in copies[2]:
        copy.wait()

    @each
    def _(i, j):
        rows = pl.ds(RA + RB, RC)
        block = total(own_q[i, j, rows, :], query_from[i, j, rows, :])
        for lane in range(3):
            c[i, j, pl.ds(lane * RC, RC), :] = block[:, lane * 128 : (lane + 1) * 128]
        block = total(own_k[i, j], key_from[i, j])
        for lane in range(2):
            c[i, j, pl.ds(3 * RC + lane * KR, KR), :] = block[:, lane * 128 : (lane + 1) * 128]


def pre_sum(step, where, query, key, query_from, key_from):
    return pl.pallas_call(
        functools.partial(pre_kernel, step),
        out_shape=(
            jax.ShapeDtypeStruct((N, N, RA, QC), bf16),
            jax.ShapeDtypeStruct((N, N, RB, QC), bf16),
            jax.ShapeDtypeStruct((N, N, MC, 128), bf16),
        ),
        in_specs=[SMEM, ANY, ANY, VMEM, VMEM],
        out_specs=(VMEM, VMEM, VMEM),
        scratch_shapes=[
            pltpu.VMEM((N, N, QR, QC), bf16),
            pltpu.VMEM((N, N, KR, KC), bf16),
            pltpu.SemaphoreType.DMA((N_COPIES,)),
        ],
        compiler_params=pltpu.CompilerParams(vmem_limit_bytes=16 << 20),
        name=f"pre_sum_{step}",
    )(where, query, key, query_from, key_from)


def add(*terms):
    total = terms[0].astype(f32)
    for term in terms[1:]:
        total = total + term.astype(f32)
    return total.astype(bf16)


def block_of(array, index):
    return lax.dynamic_index_in_dim(array, index, 0, keepdims=False)


def scatter(array, axis, here):
    received = [shift(block_of(array, (here + by) % N), axis, by) for by in (1, 2, 3)]
    return [block_of(array, here)] + received


def moment_kernel(
    a0, a1, a2, a3, b0, b1, b2, b3, c0, c1, c2, c3, qm, km, qm_out, km_out, gram0, gram1
):
    def total(*refs):
        value = refs[0][...].astype(f32)
        for ref in refs[1:]:
            value = value + ref[...].astype(f32)
        return value

    part_c = total(c0, c1, c2, c3)
    qm_out[pl.ds(0, RA), :] = momentum_decay * qm[pl.ds(0, RA), :] + total(a0, a1, a2, a3)
    qm_out[pl.ds(RA, RB), :] = momentum_decay * qm[pl.ds(RA, RB), :] + total(b0, b1, b2, b3)
    for lane in range(3):
        lanes = pl.ds(lane * 128, 128)
        rows = pl.ds(RA + RB, RC)
        qm_out[rows, lanes] = (
            momentum_decay * qm[rows, lanes] + part_c[lane * RC : (lane + 1) * RC]
        )
    for lane in range(2):
        lanes = pl.ds(lane * 128, 128)
        start = 3 * RC + lane * KR
        km_out[:, lanes] = momentum_decay * km[:, lanes] + part_c[start : start + KR]

    def gram_of(value):
        return lax.dot_general(
            value, value, (((0,), (0,)), ((), ())), precision=HIGHEST, preferred_element_type=f32
        )

    full = qm_out[...]
    for head, out in enumerate((gram0, gram1)):
        wide = (full if head == 0 else pltpu.roll(full, QH, 1))[:, :256]
        gram = gram_of(wide)
        out[pl.ds(0, 192), :] = gram[:192, :128]
        out[pl.ds(192, 64), :] = gram[128:192, 128:]
        out[pl.ds(256, 128), :] = gram_of(km_out[:, pl.ds(head * KH, KH)])


def moments(parts_a, parts_b, parts_c, query_moment, key_moment):
    return pl.pallas_call(
        moment_kernel,
        out_shape=(
            jax.ShapeDtypeStruct((QR, QC), f32),
            jax.ShapeDtypeStruct((KR, KC), f32),
            jax.ShapeDtypeStruct((G_ROWS, 128), f32),
            jax.ShapeDtypeStruct((G_ROWS, 128), f32),
        ),
        in_specs=[VMEM] * 14,
        out_specs=(VMEM,) * 4,
        compiler_params=pltpu.CompilerParams(vmem_limit_bytes=16 << 20),
        name="moments",
    )(*parts_a, *parts_b, *parts_c, query_moment, key_moment)


def chain_kernel(g0, g1, g2, g3, out):
    packed = g0[...] + g1[...] + g2[...] + g3[...]
    top, side, corner = packed[:128], packed[128:192], packed[192:256]
    key_gram = packed[256:384]
    row = lax.broadcasted_iota(jnp.int32, (256, 256), 0)
    column = lax.broadcasted_iota(jnp.int32, (256, 256), 1)
    zeros = jnp.zeros((64, 128), f32)
    lower = jnp.concatenate([side, zeros], axis=0)
    query_gram = jnp.concatenate(
        [
            jnp.concatenate([top, lower.T], axis=1),
            jnp.concatenate([lower, jnp.concatenate([corner, zeros], axis=0)], axis=1),
        ],
        axis=0,
    )
    query_gram = jnp.where((row < QH) & (column < QH), query_gram, 0.0)
    query_eye = jnp.where((row == column) & (row < QH), 1.0, 0.0).astype(f32)
    key_eye = jnp.where(row == column, 1.0, 0.0).astype(f32)[:128, :128]

    def product(left, right):
        return jnp.dot(left, right, precision=HIGHEST, preferred_element_type=f32)

    def start(gram, eye):
        square = jnp.sum(jnp.sum(gram * eye, axis=1, keepdims=True), axis=0, keepdims=True)
        inverse = 1.0 / (jnp.sqrt(square) + norm_epsilon)
        return gram * inverse * inverse, inverse

    grams, inverses = zip(start(query_gram, query_eye), start(key_gram, key_eye))
    grams, eyes, totals = list(grams), (query_eye, key_eye), [None, None]
    for iteration in range(ITERS):
        mixers = []
        for i in range(2):
            square = product(grams[i], grams[i])
            mixers.append(coef_first * eyes[i] + coef_second * grams[i] + coef_third * square)
        if iteration < ITERS - 1:
            halves = [product(mixers[i], grams[i]) for i in range(2)]
        for i in range(2):
            totals[i] = mixers[i] if iteration == 0 else product(totals[i], mixers[i])
        if iteration < ITERS - 1:
            grams = [product(halves[i], mixers[i]) for i in range(2)]
    query_total, key_total = (totals[i] * inverses[i] for i in range(2))
    out[pl.ds(0, 192), :] = query_total[:192, :128]
    out[pl.ds(192, 192), :] = query_total[:192, 128:]
    out[pl.ds(384, 128), :] = key_total


def chain(grams):
    return pl.pallas_call(
        chain_kernel,
        out_shape=jax.ShapeDtypeStruct((512, 128), f32),
        in_specs=[VMEM] * 4,
        out_specs=VMEM,
        compiler_params=pltpu.CompilerParams(vmem_limit_bytes=16 << 20),
        name="newton_schulz_polynomial",
    )(*grams)


def update_kernel(where, own, other, qm, km, qw, kw, qf, kf, first, second):
    core = where[3]
    mine, theirs = own[...], other[...]
    packs = (jnp.where(core == 0, mine, theirs), jnp.where(core == 0, theirs, mine))

    def product(left, right):
        return jnp.dot(left, right, precision=HIGHEST, preferred_element_type=f32)

    full = qm[...]
    zeros = jnp.zeros((64, 256), f32)
    pad = jnp.zeros((QR, 128), f32)
    pieces = []
    for head in range(2):
        wide = (full if head == 0 else pltpu.roll(full, QH, 1))[:, :256]
        matrix = jnp.concatenate([packs[head][:192], packs[head][192:384]], axis=1)
        matrix = jnp.concatenate([matrix, zeros], axis=0)
        piece = jnp.concatenate([product(wide, matrix), pad], axis=1)
        pieces.append(piece if head == 0 else pltpu.roll(piece, QH, 1))
    query_ortho = pieces[0] + pieces[1]
    key_ortho = jnp.concatenate(
        [product(km[:, pl.ds(h * KH, KH)], packs[h][384:]) for h in range(2)], axis=1
    )
    query_scale = 0.2 * math.sqrt(max(QL, QH))
    key_scale = 0.2 * math.sqrt(max(KVL, KH))
    query_weight, key_weight = qw[...], kw[...]
    query_next = query_weight - learn_rate * (
        query_scale * query_ortho + weight_decay * query_weight
    )
    key_next = key_weight - learn_rate * (key_scale * key_ortho + weight_decay * key_weight)
    query_block = (query_next * qf[...]).astype(bf16)
    key_block = (key_next * kf[...]).astype(bf16)
    for half, out in enumerate((first, second)):
        for lane in range(3):
            out[pl.ds(lane * HQ, HQ), :] = query_block[
                half * HQ : (half + 1) * HQ, lane * 128 : (lane + 1) * 128
            ]
        for lane in range(2):
            out[pl.ds(3 * HQ + lane * HK, HK), :] = key_block[
                half * HK : (half + 1) * HK, lane * 128 : (lane + 1) * 128
            ]


def update(where, own, other, query_moment, key_moment, query_weight, key_weight, qf, kf):
    return pl.pallas_call(
        update_kernel,
        out_shape=(jax.ShapeDtypeStruct((H_ROWS, 128), bf16),) * 2,
        in_specs=[SMEM] + [VMEM] * 8,
        out_specs=(VMEM, VMEM),
        compiler_params=pltpu.CompilerParams(vmem_limit_bytes=16 << 20),
        name="update",
    )(where, own, other, query_moment, key_moment, query_weight, key_weight, qf, kf)


def assemble_kernel(where, *refs):
    z, x = where[0], where[1]
    inputs, (query_out, key_out) = refs[:8], refs[8:]
    for half in range(2):
        for far in range(N):
            stack = inputs[half * N + far]
            for near in range(N):
                if half == 0:
                    owner = ((z + N - near) % N) * N + (x + N - far) % N
                else:
                    owner = ((z + N - far) % N) * N + (x + N - near) % N
                for lane in range(3):
                    query_out[
                        pl.ds(half * HQ, HQ),
                        pl.ds(pl.multiple_of(owner * QC + lane * 128, 128), 128),
                    ] = stack[near, pl.ds(lane * HQ, HQ), :]
                for lane in range(2):
                    key_out[
                        pl.ds(half * HK, HK),
                        pl.ds(pl.multiple_of(owner * KC + lane * 128, 128), 128),
                    ] = stack[near, pl.ds(3 * HQ + lane * HK, HK), :]


def assemble(where, first, second):
    return pl.pallas_call(
        assemble_kernel,
        out_shape=(
            jax.ShapeDtypeStruct((QR, N * N * QC), bf16),
            jax.ShapeDtypeStruct((KR, N * N * KC), bf16),
        ),
        in_specs=[SMEM] + [VMEM] * 8,
        out_specs=(VMEM, VMEM),
        compiler_params=pltpu.CompilerParams(vmem_limit_bytes=20 << 20),
        name="assemble",
    )(where, *first, *second)


def gather(array, axis):
    return [array] + [shift(array, axis, by) for by in (1, 2, 3)]


def head_factors(gamma, head_width, rope_width):
    position = jnp.arange(head_width)
    root = jnp.sqrt(gamma)
    table = jnp.where(position[None, :] < head_width - rope_width, root[:, None], gamma[:, None])
    return table.reshape(1, -1)


def on_device(grad_query, grad_key, query_weight, key_weight, query_moment, key_moment, max_logits):
    dp, ctx = lax.axis_index("dp"), lax.axis_index("ctx")
    z, x, y, core = dp // N, dp % N, ctx // 2, ctx % 2
    where = jnp.stack([z, x, y, core]).astype(jnp.int32)
    query = grad_query.reshape(N, 2, QR, N * N * QC)
    key = grad_key.reshape(N, 2, KR, N * N * KC)

    pre = []
    for step in range(1, N + 1):
        query_part, key_part = slice_other(step, where, query, key)
        query_part, key_part = swap(query_part), swap(key_part)
        pre.append(pre_sum(step, where, query, key, query_part, key_part))

    sums = list(pre[0])
    for step in range(1, N):
        sums = [ring(part, axis) for part, axis in zip(sums, ("x", "z", "y"))]
        sums = [add(own, part) for own, part in zip(pre[step], sums)]

    peak = max_logits[0]
    peak = jnp.maximum(peak, swap(peak))
    for axis in ("x", "y", "z"):
        for step in (1, 2):
            peak = jnp.maximum(peak, exchange(peak, axis, step))
    gamma = jnp.minimum(1.0, clip_limit / peak)
    gamma = lax.dynamic_slice_in_dim(gamma, dp * 2, 2, 0)
    query_factor, key_factor = head_factors(gamma, QH, QROPE), head_factors(gamma, KH, 0)

    here = dict(z=z, x=x, y=y)
    second = [scatter(s, axis, here[axis]) for s, axis in zip(sums, ("y", "x", "z"))]
    sums = [add(*terms) for terms in second]
    third = [scatter(s, axis, here[axis]) for s, axis in zip(sums, ("z", "y", "x"))]
    new_query_moment, new_key_moment, gram0, gram1 = moments(*third, query_moment, key_moment)

    keep, give = jnp.where(core == 0, gram0, gram1), jnp.where(core == 0, gram1, gram0)
    gram = keep + swap(give)
    own = chain(gather(gram, "y"))
    first, last = update(
        where,
        own,
        swap(own),
        new_query_moment,
        new_key_moment,
        query_weight,
        key_weight,
        query_factor,
        key_factor,
    )
    first, last = jnp.stack(gather(first, "z")), jnp.stack(gather(last, "x"))
    first, last = gather(first, "x"), gather(last, "z")
    query_out, key_out = assemble(where, first, last)
    return (query_out, key_out, new_query_moment, new_key_moment)


def solution(mesh):
    in_specs = (
        P(("dp", "ctx"), None, None),
        P(("dp", "ctx"), None, None),
        P("ctx", "dp"),
        P("ctx", "dp"),
        P("ctx", "dp"),
        P("ctx", "dp"),
        P(("dp", "ctx"), None),
    )
    out_specs = (P("ctx", None), P("ctx", None), P("ctx", "dp"), P("ctx", "dp"))
    return jax.shard_map(
        on_device, mesh=mesh, in_specs=in_specs, out_specs=out_specs, check_vma=False
    )
```

time: 452 us -> 222 us (0.49)
  the two profiles are of different devices: /device:TPU:8 before, /device:TPU:66 now
where the time goes in v1:
time: 222 us; the launch traced here: 218 us
  starting transfers between devices  97.2 us (44%)
  waiting for transfers between devices  62.9 us (28%)
  Pallas kernels  29.8 us (13%)
  local copies, waits for them, and re-layouts  17.7 us (8%)
  other arithmetic  8.62 us (4%)
    ppermute x59, starting transfers between devices, send(): return lax.ppermute(array, AXES, pairs)  97.2 us
    ppermute x59, waiting for transfers between devices, send(): return lax.ppermute(array, AXES, pairs)  62.9 us
    unnamed x32, local copies, waits for them, and re-layouts  17.2 us
    pallas_call x4, Pallas kernels, pre_sum(): pl.pallas_call(functools.partial(pre_kernel, step), out_shape=(jax.ShapeD...  10.8 us
    convert_element_type x11, other arithmetic, add(): return total.astype(bf16)  8.22 us
    pallas_call x1, Pallas kernels, chain(): pl.pallas_call(chain_kernel, out_shape=jax.ShapeDtypeStruct((512, 128), f...  7.1 us
    pallas_call x4, Pallas kernels, slice_other(): pl.pallas_call(functools.partial(slice_kernel, step), out_shape=(jax.Shap...  6.82 us
  transfers between devices with their start and end apart: 59, of which 25 were waited for; matrix products, arithmetic and copies ran while one was open for 4% of the time, Pallas kernels for 8%

profile of v1, /device:TPU:66, one launch (start us, length us, event | category | flops | bytes accessed | tf_op | source)
XLA Modules:
  0.0 217.5 jit_solution(3062826639587696076)
XLA Ops:
  0.7 6.4 %copy-done = bf16[1,1536,6144]{2,1,0:T(8,128)(2,1)S(1)} copy-done((bf16[1,1536,6144]{2,1,0:T(8,128)(2,1)S(1)}, bf16[1,1536,6144]{2,1,0:T(8,128)(2,1)}, u32[]{:S(2)}) %copy-start) | copy-done | bytes 18874392
  15.0 4.5 %collective-permute-done.7.key_from = bf16[4,4,64,256]{3,2,1,0:T(8,128)(2,1)S(1)} collective-permute-done((bf16[4,4,64,256]{3,2,1,0:T(8,128)(2,1)S(1)}, bf16[4,4,64,256]{3,2,1,0:T(8,128)(2,1)S(1)}, u32[]{:S(2)}, u32[]{:S(2)}) %collective-permute-start.7) | collective-permute-done | bytes 524320 | tf_op jit(solution)/shard_map/ppermute | solution.py:56
  19.6 2.7 %pre_sum_1.1 = (bf16[4,4,80,384]{3,2,1,0:T(8,128)(2,1)S(1)}, bf16[4,4,80,384]{3,2,1,0:T(8,128)(2,1)S(1)}, bf16[4,4,224,128]{3,2,1,0:T(8,128)(2,1)S(1)}) custom-call(s32[4]{0:T(128)S(1)} %pad_add_fusion.where, bf16[4,2,192,6144]{3,2,1,0:T(8,128)(2,1)S(1)} %bitcast.73, bf16[4,2,64,4096]{3,2,1,0:T(8,128)(2,1)S(1)} %bitcast.81, ...), custom_call_target="tpu_custom_call" | custom-call | tf_op jit(solution)/shard_map/pre_sum_1/pallas_call | solution.py:201
  28.3 2.5 %slice_other_4.1 = (bf16[4,4,192,384]{3,2,1,0:T(8,128)(2,1)}, bf16[4,4,64,256]{3,2,1,0:T(8,128)(2,1)}) custom-call(s32[4]{0:T(128)S(1)} %pad_add_fusion.where, bf16[4,2,192,6144]{3,2,1,0:T(8,128)(2,1)S(1)} %bitcast.74, bf16[4,2,64,4096]{3,2,1,0:T(8,128)(2,1)S(1)} %bitcast.82), custom_call_target="tpu_custom_call" | custom-call | tf_op jit(solution)/shard_map/slice_other_4/pallas_call | solution.py:142
  30.9 2.7 %pre_sum_2.1 = (bf16[4,4,80,384]{3,2,1,0:T(8,128)(2,1)S(1)}, bf16[4,4,80,384]{3,2,1,0:T(8,128)(2,1)S(1)}, bf16[4,4,224,128]{3,2,1,0:T(8,128)(2,1)S(1)}) custom-call(s32[4]{0:T(128)S(1)} %pad_add_fusion.where, bf16[4,2,192,6144]{3,2,1,0:T(8,128)(2,1)S(1)} %bitcast.75, bf16[4,2,64,4096]{3,2,1,0:T(8,128)(2,1)S(1)} %bitcast.83, ...), custom_call_target="tpu_custom_call" | custom-call | tf_op jit(solution)/shard_map/pre_sum_2/pallas_call | solution.py:201
  33.6 3.4 %collective-permute-done.26 = bf16[4,4,224,128]{3,2,1,0:T(8,128)(2,1)S(1)} collective-permute-done((bf16[4,4,224,128]{3,2,1,0:T(8,128)(2,1)S(1)}, bf16[4,4,224,128]{3,2,1,0:T(8,128)(2,1)S(1)}, u32[]{:S(2)}, u32[]{:S(2)}) %collective-permute-start.26) | collective-permute-done | bytes 917536 | tf_op jit(solution)/shard_map/ppermute | solution.py:56
  44.3 2.7 %pre_sum_3.1 = (bf16[4,4,80,384]{3,2,1,0:T(8,128)(2,1)S(1)}, bf16[4,4,80,384]{3,2,1,0:T(8,128)(2,1)S(1)}, bf16[4,4,224,128]{3,2,1,0:T(8,128)(2,1)S(1)}) custom-call(s32[4]{0:T(128)S(1)} %pad_add_fusion.where, bf16[4,2,192,6144]{3,2,1,0:T(8,128)(2,1)S(1)} %bitcast.76, bf16[4,2,64,4096]{3,2,1,0:T(8,128)(2,1)S(1)} %bitcast.84, ...), custom_call_target="tpu_custom_call" | custom-call | tf_op jit(solution)/shard_map/pre_sum_3/pallas_call | solution.py:201
  47.0 6.9 %collective-permute-done.27 = bf16[4,4,224,128]{3,2,1,0:T(8,128)(2,1)S(1)} collective-permute-done((bf16[4,4,224,128]{3,2,1,0:T(8,128)(2,1)S(1)}, bf16[4,4,224,128]{3,2,1,0:T(8,128)(2,1)S(1)}, u32[]{:S(2)}, u32[]{:S(2)}) %collective-permute-start.27) | collective-permute-done | bytes 917536 | tf_op jit(solution)/shard_map/ppermute | solution.py:56
  64.7 6.4 %copy-done.1 = bf16[1,1536,6144]{2,1,0:T(8,128)(2,1)S(1)} copy-done((bf16[1,1536,6144]{2,1,0:T(8,128)(2,1)S(1)}, bf16[1,1536,6144]{2,1,0:T(8,128)(2,1)}, u32[]{:S(2)}) %copy-start.1) | copy-done | bytes 18874392
  73.3 2.7 %pre_sum_4.1 = (bf16[4,4,80,384]{3,2,1,0:T(8,128)(2,1)S(1)}, bf16[4,4,80,384]{3,2,1,0:T(8,128)(2,1)S(1)}, bf16[4,4,224,128]{3,2,1,0:T(8,128)(2,1)S(1)}) custom-call(s32[4]{0:T(128)S(1)} %pad_add_fusion.where, bf16[4,2,192,6144]{3,2,1,0:T(8,128)(2,1)S(1)} %bitcast.77, bf16[4,2,64,4096]{3,2,1,0:T(8,128)(2,1)S(1)} %bitcast.85, ...), custom_call_target="tpu_custom_call" | custom-call | tf_op jit(solution)/shard_map/pre_sum_4/pallas_call | solution.py:201
  79.6 3.9 %collective-permute-start.30 = (bf16[4,224,128]{2,1,0:T(8,128)(2,1)S(1)}, bf16[4,224,128]{2,1,0:T(8,128)(2,1)S(1)}, u32[]{:S(2)}, u32[]{:S(2)}) collective-permute-start(bf16[4,224,128]{2,1,0:T(8,128)(2,1)S(1)} %get-tuple-element.70), channel_id=1, source_target_pairs={{0,64},{1,65},{2,66},{3,67},{4,68},{5,69},{6,70},{7,71},{8,72},{9,... | collective-permute-start | bytes 688136 | tf_op jit(solution)/shard_map/ppermute | solution.py:56
  85.8 5.6 %collective-permute-start.22 = (bf16[4,80,384]{2,1,0:T(8,128)(2,1)S(1)}, bf16[4,80,384]{2,1,0:T(8,128)(2,1)S(1)}, u32[]{:S(2)}, u32[]{:S(2)}) collective-permute-start(bf16[4,80,384]{2,1,0:T(8,128)(2,1)S(1)} %get-tuple-element.63), channel_id=1, source_target_pairs={{0,24},{1,25},{2,26},{3,27},{4,28},{5,29},{6,30},{7,31},{8,0},{9,1... | collective-permute-start | bytes 737288 | tf_op jit(solution)/shard_map/ppermute | solution.py:56
  91.4 2.5 %collective-permute-start.21 = (bf16[4,80,384]{2,1,0:T(8,128)(2,1)S(1)}, bf16[4,80,384]{2,1,0:T(8,128)(2,1)S(1)}, u32[]{:S(2)}, u32[]{:S(2)}) collective-permute-start(bf16[4,80,384]{2,1,0:T(8,128)(2,1)S(1)} %get-tuple-element.64), channel_id=1, source_target_pairs={{0,16},{1,17},{2,18},{3,19},{4,20},{5,21},{6,22},{7,23},{8,24},{9,... | collective-permute-start | bytes 737288 | tf_op jit(solution)/shard_map/ppermute | solution.py:56
  94.7 2.6 %collective-permute-start.13 = (bf16[4,80,384]{2,1,0:T(8,128)(2,1)S(1)}, bf16[4,80,384]{2,1,0:T(8,128)(2,1)S(1)}, u32[]{:S(2)}, u32[]{:S(2)}) collective-permute-start(bf16[4,80,384]{2,1,0:T(8,128)(2,1)S(1)} %get-tuple-element.66), channel_id=1, source_target_pairs={{0,6},{1,7},{2,0},{3,1},{4,2},{5,3},{6,4},{7,5},{8,14},{9,15},{10,... | collective-permute-start | bytes 737288 | tf_op jit(solution)/shard_map/ppermute | solution.py:56
  98.7 3.0 %collective-permute-done.21 = bf16[4,80,384]{2,1,0:T(8,128)(2,1)S(1)} collective-permute-done((bf16[4,80,384]{2,1,0:T(8,128)(2,1)S(1)}, bf16[4,80,384]{2,1,0:T(8,128)(2,1)S(1)}, u32[]{:S(2)}, u32[]{:S(2)}) %collective-permute-start.21) | collective-permute-done | bytes 245792 | tf_op jit(solution)/shard_map/ppermute | solution.py:56
  102.8 2.7 %collective-permute-start.33 = (bf16[224,128]{1,0:T(8,128)(2,1)S(1)}, bf16[224,128]{1,0:T(8,128)(2,1)S(1)}, u32[]{:S(2)}, u32[]{:S(2)}) collective-permute-start(bf16[224,128]{1,0:T(8,128)(2,1)S(1)} %get-tuple-element.80), channel_id=1, source_target_pairs={{0,16},{1,17},{2,18},{3,19},{4,20},{5,21},{6,22},{7,23},{8,24},{9,... | collective-permute-start | bytes 172040 | tf_op jit(solution)/shard_map/ppermute | solution.py:56
  105.5 2.6 %collective-permute-start.32 = (bf16[224,128]{1,0:T(8,128)(2,1)S(1)}, bf16[224,128]{1,0:T(8,128)(2,1)S(1)}, u32[]{:S(2)}, u32[]{:S(2)}) collective-permute-start(bf16[224,128]{1,0:T(8,128)(2,1)S(1)} %get-tuple-element.81), channel_id=1, source_target_pairs={{0,8},{1,9},{2,10},{3,11},{4,12},{5,13},{6,14},{7,15},{8,16},{9,17... | collective-permute-start | bytes 172040 | tf_op jit(solution)/shard_map/ppermute | solution.py:56
  112.0 4.6 %collective-permute-start.15 = (bf16[80,384]{1,0:T(8,128)(2,1)S(1)}, bf16[80,384]{1,0:T(8,128)(2,1)S(1)}, u32[]{:S(2)}, u32[]{:S(2)}) collective-permute-start(bf16[80,384]{1,0:T(8,128)(2,1)S(1)} %get-tuple-element.76), channel_id=1, source_target_pairs={{0,64},{1,65},{2,66},{3,67},{4,68},{5,69},{6,70},{7,71},{8,72},{9,... | collective-permute-start | bytes 184328 | tf_op jit(solution)/shard_map/ppermute | solution.py:56
  116.6 2.5 %collective-permute-start.14 = (bf16[80,384]{1,0:T(8,128)(2,1)S(1)}, bf16[80,384]{1,0:T(8,128)(2,1)S(1)}, u32[]{:S(2)}, u32[]{:S(2)}) collective-permute-start(bf16[80,384]{1,0:T(8,128)(2,1)S(1)} %get-tuple-element.77), channel_id=1, source_target_pairs={{0,32},{1,33},{2,34},{3,35},{4,36},{5,37},{6,38},{7,39},{8,40},{9,... | collective-permute-start | bytes 184328 | tf_op jit(solution)/shard_map/ppermute | solution.py:56
  127.7 4.0 %collective-permute-start.44 = (f32[32]{0:T(128)S(1)}, f32[32]{0:T(128)S(1)}, u32[]{:S(2)}, u32[]{:S(2)}) collective-permute-start(f32[32]{0:T(128)S(1)} %max.24), channel_id=1, source_target_pairs={{0,4},{1,5},{2,6},{3,7},{4,0},{5,1},{6,2},{7,3},{8,12},{9,13},{10,... | collective-permute-start | bytes 392 | tf_op jit(solution)/shard_map/ppermute | solution.py:56
  133.8 3.0 %collective-permute-done.45 = f32[32]{0:T(128)S(1)} collective-permute-done((f32[32]{0:T(128)S(1)}, f32[32]{0:T(128)S(1)}, u32[]{:S(2)}, u32[]{:S(2)}) %collective-permute-start.45) | collective-permute-done | bytes 160 | tf_op jit(solution)/shard_map/ppermute | solution.py:56
  137.4 11.3 %collective-permute-start.38 = (f32[384,128]{1,0:T(8,128)S(1)}, f32[384,128]{1,0:T(8,128)S(1)}, u32[]{:S(2)}, u32[]{:S(2)}) collective-permute-start(f32[384,128]{1,0:T(8,128)S(1)} %select_add_fusion.g0), channel_id=1, source_target_pairs={{0,6},{1,7},{2,0},{3,1},{4,2},{5,3},{6,4},{7,5},{8,14},{9,15},{10,... | collective-permute-start | bytes 589832 | tf_op jit(solution)/shard_map/ppermute | solution.py:56
  152.9 3.1 %collective-permute-done.37.g2 = f32[384,128]{1,0:T(8,128)S(1)} collective-permute-done((f32[384,128]{1,0:T(8,128)S(1)}, f32[384,128]{1,0:T(8,128)S(1)}, u32[]{:S(2)}, u32[]{:S(2)}) %collective-permute-start.37) | collective-permute-done | bytes 196640 | tf_op jit(solution)/shard_map/ppermute | solution.py:56
  158.0 7.1 %newton_schulz_polynomial.1.own = f32[512,128]{1,0:T(8,128)S(1)} custom-call(f32[384,128]{1,0:T(8,128)S(1)} %select_add_fusion.g0, f32[384,128]{1,0:T(8,128)S(1)} %collective-permute-done.36.g1, f32[384,128]{1,0:T(8,128)S(1)} %collective-permute-done.37.g2, f32[384,128]{1,0:T(8,128)S(1)} %collective-permute-done.38.g3), custom_call_target="tpu_custom_call" | custom-call | tf_op jit(solution)/shard_map/newton_schulz_polynomial/pallas_call | solution.py:336
  168.7 2.8 %collective-permute-start.54 = (bf16[352,128]{1,0:T(8,128)(2,1)S(1)}, bf16[352,128]{1,0:T(8,128)(2,1)S(1)}, u32[]{:S(2)}, u32[]{:S(2)}) collective-permute-start(bf16[352,128]{1,0:T(8,128)(2,1)S(1)} %get-tuple-element.57), channel_id=1, source_target_pairs={{0,16},{1,17},{2,18},{3,19},{4,20},{5,21},{6,22},{7,23},{8,24},{9,... | collective-permute-start | bytes 270344 | tf_op jit(solution)/shard_map/ppermute | solution.py:56
  173.0 3.1 %collective-permute-done.54 = bf16[352,128]{1,0:T(8,128)(2,1)S(1)} collective-permute-done((bf16[352,128]{1,0:T(8,128)(2,1)S(1)}, bf16[352,128]{1,0:T(8,128)(2,1)S(1)}, u32[]{:S(2)}, u32[]{:S(2)}) %collective-permute-start.54) | collective-permute-done | bytes 90144 | tf_op jit(solution)/shard_map/ppermute | solution.py:56
  181.0 2.3 %collective-permute-start.47 = (bf16[352,128]{1,0:T(8,128)(2,1)S(1)}, bf16[352,128]{1,0:T(8,128)(2,1)S(1)}, u32[]{:S(2)}, u32[]{:S(2)}) collective-permute-start(bf16[352,128]{1,0:T(8,128)(2,1)S(1)} %get-tuple-element.56), channel_id=1, source_target_pairs={{0,32},{1,33},{2,34},{3,35},{4,36},{5,37},{6,38},{7,39},{8,40},{9,... | collective-permute-start | bytes 270344 | tf_op jit(solution)/shard_map/ppermute | solution.py:56
  183.7 6.5 %collective-permute-done.49 = bf16[352,128]{1,0:T(8,128)(2,1)S(1)} collective-permute-done((bf16[352,128]{1,0:T(8,128)(2,1)S(1)}, bf16[352,128]{1,0:T(8,128)(2,1)S(1)}, u32[]{:S(2)}, u32[]{:S(2)}) %collective-permute-start.49) | collective-permute-done | bytes 90144 | tf_op jit(solution)/shard_map/ppermute | solution.py:56
  190.2 10.8 %collective-permute-start.56 = (bf16[4,352,128]{2,1,0:T(8,128)(2,1)S(1)}, bf16[4,352,128]{2,1,0:T(8,128)(2,1)S(1)}, u32[]{:S(2)}, u32[]{:S(2)}) collective-permute-start(bf16[4,352,128]{2,1,0:T(8,128)(2,1)S(1)} %pad_maximum_fusion.1.refs_4_), channel_id=1, source_target_pairs={{0,32},{1,33},{2,34},{3,35},{4,36},{5,37},{6,38},{7,39},{8,40},{9,... | collective-permute-start | bytes 1081352 | tf_op jit(solution)/shard_map/ppermute | solution.py:56
  203.2 2.8 %collective-permute-done.56.refs_5_ = bf16[4,352,128]{2,1,0:T(8,128)(2,1)S(1)} collective-permute-done((bf16[4,352,128]{2,1,0:T(8,128)(2,1)S(1)}, bf16[4,352,128]{2,1,0:T(8,128)(2,1)S(1)}, u32[]{:S(2)}, u32[]{:S(2)}) %collective-permute-start.56) | collective-permute-done | bytes 360480 | tf_op jit(solution)/shard_map/ppermute | solution.py:56
  205.9 7.3 %collective-permute-done.52.refs_3_ = bf16[4,352,128]{2,1,0:T(8,128)(2,1)S(1)} collective-permute-done((bf16[4,352,128]{2,1,0:T(8,128)(2,1)S(1)}, bf16[4,352,128]{2,1,0:T(8,128)(2,1)S(1)}, u32[]{:S(2)}, u32[]{:S(2)}) %collective-permute-start.52) | collective-permute-done | bytes 360480 | tf_op jit(solution)/shard_map/ppermute | solution.py:56
  214.5 2.8 %assemble.1 = (bf16[192,6144]{1,0:T(8,128)(2,1)}, bf16[64,4096]{1,0:T(8,128)(2,1)}) custom-call(s32[4]{0:T(128)S(1)} %pad_add_fusion.where, bf16[4,352,128]{2,1,0:T(8,128)(2,1)S(1)} %pad_maximum_fusion.refs_0_, bf16[4,352,128]{2,1,0:T(8,128)(2,1)S(1)} %collective-permute-done.50.refs_1_, bf16[4,352,128]{2,1,0:T(8,128)(2,1)S(1)} %collective-permute-done.51.refs_2_, ...), custom_call_target="tpu_custom_call" | custom-call | tf_op jit(solution)/shard_map/assemble/pallas_call | solution.py:423
  (166 shorter events, 78.3 us)
Async XLA Ops:
  12.4 18.4 %collective-permute-start.4 = (bf16[4,4,192,384]{3,2,1,0:T(8,128)(2,1)S(1)}, bf16[4,4,192,384]{3,2,1,0:T(8,128)(2,1)S(1)}, u32[]{:S(2)}, u32[]{:S(2)}) collective-permute-start(bf16[4,4,192,384]{3,2,1,0:T(8,128)(2,1)S(1)} %get-tuple-element.38), channel_id=1, source_target_pairs={{0,1},{1,0},{2,3},{3,2},{4,5},{5,4},{6,7},{7,6},{8,9},{9,8},{10,11... | collective-permute-start | bytes 7077896 | tf_op jit(solution)/shard_map/ppermute | solution.py:56
  14.5 29.8 %collective-permute-start.2 = (bf16[4,4,192,384]{3,2,1,0:T(8,128)(2,1)S(1)}, bf16[4,4,192,384]{3,2,1,0:T(8,128)(2,1)S(1)}, u32[]{:S(2)}, u32[]{:S(2)}) collective-permute-start(bf16[4,4,192,384]{3,2,1,0:T(8,128)(2,1)S(1)} %get-tuple-element.35), channel_id=1, source_target_pairs={{0,1},{1,0},{2,3},{3,2},{4,5},{5,4},{6,7},{7,6},{8,9},{9,8},{10,11... | collective-permute-start | bytes 7077896 | tf_op jit(solution)/shard_map/ppermute | solution.py:56
  22.3 14.7 %collective-permute-start.26 = (bf16[4,4,224,128]{3,2,1,0:T(8,128)(2,1)S(1)}, bf16[4,4,224,128]{3,2,1,0:T(8,128)(2,1)S(1)}, u32[]{:S(2)}, u32[]{:S(2)}) collective-permute-start(bf16[4,4,224,128]{3,2,1,0:T(8,128)(2,1)S(1)} %get-tuple-element.51), channel_id=1, source_target_pairs={{0,2},{1,7},{2,4},{3,1},{4,6},{5,3},{6,0},{7,5},{8,10},{9,15},{10,... | collective-permute-start | bytes 2752520 | tf_op jit(solution)/shard_map/ppermute | solution.py:56
  25.2 14.1 %collective-permute-start.17 = (bf16[4,4,80,384]{3,2,1,0:T(8,128)(2,1)S(1)}, bf16[4,4,80,384]{3,2,1,0:T(8,128)(2,1)S(1)}, u32[]{:S(2)}, u32[]{:S(2)}) collective-permute-start(bf16[4,4,80,384]{3,2,1,0:T(8,128)(2,1)S(1)} %get-tuple-element.47), channel_id=1, source_target_pairs={{0,32},{1,97},{2,34},{3,99},{4,36},{5,101},{6,38},{7,103},{8,40},{... | collective-permute-start | bytes 2949128 | tf_op jit(solution)/shard_map/ppermute | solution.py:56
  26.8 14.1 %collective-permute-start.8 = (bf16[4,4,80,384]{3,2,1,0:T(8,128)(2,1)S(1)}, bf16[4,4,80,384]{3,2,1,0:T(8,128)(2,1)S(1)}, u32[]{:S(2)}, u32[]{:S(2)}) collective-permute-start(bf16[4,4,80,384]{3,2,1,0:T(8,128)(2,1)S(1)} %get-tuple-element.43), channel_id=1, source_target_pairs={{0,8},{1,25},{2,10},{3,27},{4,12},{5,29},{6,14},{7,31},{8,16},{9,1... | collective-permute-start | bytes 2949128 | tf_op jit(solution)/shard_map/ppermute | solution.py:56
  30.8 11.9 %collective-permute-start.3 = (bf16[4,4,64,256]{3,2,1,0:T(8,128)(2,1)S(1)}, bf16[4,4,64,256]{3,2,1,0:T(8,128)(2,1)S(1)}, u32[]{:S(2)}, u32[]{:S(2)}) collective-permute-start(bf16[4,4,64,256]{3,2,1,0:T(8,128)(2,1)S(1)} %get-tuple-element.36), channel_id=1, source_target_pairs={{0,1},{1,0},{2,3},{3,2},{4,5},{5,4},{6,7},{7,6},{8,9},{9,8},{10,11... | collective-permute-start | bytes 1572872 | tf_op jit(solution)/shard_map/ppermute | solution.py:56
  36.9 27.8 %collective-permute-start = (bf16[4,4,192,384]{3,2,1,0:T(8,128)(2,1)}, bf16[4,4,192,384]{3,2,1,0:T(8,128)(2,1)S(1)}, u32[]{:S(2)}, u32[]{:S(2)}) collective-permute-start(bf16[4,4,192,384]{3,2,1,0:T(8,128)(2,1)} %get-tuple-element.32), channel_id=1, source_target_pairs={{0,1},{1,0},{2,3},{3,2},{4,5},{5,4},{6,7},{7,6},{8,9},{9,8},{10,11... | collective-permute-start | bytes 7077896 | tf_op jit(solution)/shard_map/ppermute | solution.py:56
  39.3 14.6 %collective-permute-start.27 = (bf16[4,4,224,128]{3,2,1,0:T(8,128)(2,1)S(1)}, bf16[4,4,224,128]{3,2,1,0:T(8,128)(2,1)S(1)}, u32[]{:S(2)}, u32[]{:S(2)}) collective-permute-start(bf16[4,4,224,128]{3,2,1,0:T(8,128)(2,1)S(1)} %add_convert_fusion.8), channel_id=1, source_target_pairs={{0,2},{1,7},{2,4},{3,1},{4,6},{5,3},{6,0},{7,5},{8,10},{9,15},{10,... | collective-permute-start | bytes 2752520 | tf_op jit(solution)/shard_map/ppermute | solution.py:56
  40.9 14.2 %collective-permute-start.18 = (bf16[4,4,80,384]{3,2,1,0:T(8,128)(2,1)S(1)}, bf16[4,4,80,384]{3,2,1,0:T(8,128)(2,1)S(1)}, u32[]{:S(2)}, u32[]{:S(2)}) collective-permute-start(bf16[4,4,80,384]{3,2,1,0:T(8,128)(2,1)S(1)} %add_convert_fusion.2), channel_id=1, source_target_pairs={{0,32},{1,97},{2,34},{3,99},{4,36},{5,101},{6,38},{7,103},{8,40},{... | collective-permute-start | bytes 2949128 | tf_op jit(solution)/shard_map/ppermute | solution.py:56
  42.7 15.2 %collective-permute-start.9 = (bf16[4,4,80,384]{3,2,1,0:T(8,128)(2,1)S(1)}, bf16[4,4,80,384]{3,2,1,0:T(8,128)(2,1)S(1)}, u32[]{:S(2)}, u32[]{:S(2)}) collective-permute-start(bf16[4,4,80,384]{3,2,1,0:T(8,128)(2,1)S(1)} %add_convert_fusion.5), channel_id=1, source_target_pairs={{0,8},{1,25},{2,10},{3,27},{4,12},{5,29},{6,14},{7,31},{8,16},{9,1... | collective-permute-start | bytes 2949128 | tf_op jit(solution)/shard_map/ppermute | solution.py:56
  55.1 20.9 %collective-permute-start.28 = (bf16[4,4,224,128]{3,2,1,0:T(8,128)(2,1)}, bf16[4,4,224,128]{3,2,1,0:T(8,128)(2,1)}, u32[]{:S(2)}, u32[]{:S(2)}) collective-permute-start(bf16[4,4,224,128]{3,2,1,0:T(8,128)(2,1)} %add_convert_fusion.7), channel_id=1, source_target_pairs={{0,2},{1,7},{2,4},{3,1},{4,6},{5,3},{6,0},{7,5},{8,10},{9,15},{10,... | collective-permute-start | bytes 2752520 | tf_op jit(solution)/shard_map/ppermute | solution.py:56
  56.3 23.3 %collective-permute-start.19 = (bf16[4,4,80,384]{3,2,1,0:T(8,128)(2,1)}, bf16[4,4,80,384]{3,2,1,0:T(8,128)(2,1)}, u32[]{:S(2)}, u32[]{:S(2)}) collective-permute-start(bf16[4,4,80,384]{3,2,1,0:T(8,128)(2,1)} %add_convert_fusion.1), channel_id=1, source_target_pairs={{0,32},{1,97},{2,34},{3,99},{4,36},{5,101},{6,38},{7,103},{8,40},{... | collective-permute-start | bytes 2949128 | tf_op jit(solution)/shard_map/ppermute | solution.py:56
  59.2 24.4 %collective-permute-start.10 = (bf16[4,4,80,384]{3,2,1,0:T(8,128)(2,1)}, bf16[4,4,80,384]{3,2,1,0:T(8,128)(2,1)}, u32[]{:S(2)}, u32[]{:S(2)}) collective-permute-start(bf16[4,4,80,384]{3,2,1,0:T(8,128)(2,1)} %add_convert_fusion.4), channel_id=1, source_target_pairs={{0,8},{1,25},{2,10},{3,27},{4,12},{5,29},{6,14},{7,31},{8,16},{9,1... | collective-permute-start | bytes 2949128 | tf_op jit(solution)/shard_map/ppermute | solution.py:56
  64.2 45.2 %collective-permute-start.41 = (f32[32]{0:T(128)S(1)}, f32[32]{0:T(128)S(1)}, u32[]{:S(2)}, u32[]{:S(2)}) collective-permute-start(f32[32]{0:T(128)S(1)} %bitcast_maximum_fusion), channel_id=1, source_target_pairs={{0,8},{1,9},{2,10},{3,11},{4,12},{5,13},{6,14},{7,15},{8,0},{9,1},... | collective-permute-start | bytes 392 | tf_op jit(solution)/shard_map/ppermute | solution.py:56
  78.9 12.5 %collective-permute-start.31 = (bf16[4,224,128]{2,1,0:T(8,128)(2,1)S(1)}, bf16[4,224,128]{2,1,0:T(8,128)(2,1)S(1)}, u32[]{:S(2)}, u32[]{:S(2)}) collective-permute-start(bf16[4,224,128]{2,1,0:T(8,128)(2,1)S(1)} %get-tuple-element.69), channel_id=1, source_target_pairs={{0,96},{1,97},{2,98},{3,99},{4,100},{5,101},{6,102},{7,103},{8,104... | collective-permute-start | bytes 688136 | tf_op jit(solution)/shard_map/ppermute | solution.py:56
  79.6 14.3 %collective-permute-start.30 = (bf16[4,224,128]{2,1,0:T(8,128)(2,1)S(1)}, bf16[4,224,128]{2,1,0:T(8,128)(2,1)S(1)}, u32[]{:S(2)}, u32[]{:S(2)}) collective-permute-start(bf16[4,224,128]{2,1,0:T(8,128)(2,1)S(1)} %get-tuple-element.70), channel_id=1, source_target_pairs={{0,64},{1,65},{2,66},{3,67},{4,68},{5,69},{6,70},{7,71},{8,72},{9,... | collective-permute-start | bytes 688136 | tf_op jit(solution)/shard_map/ppermute | solution.py:56
  85.8 11.5 %collective-permute-start.22 = (bf16[4,80,384]{2,1,0:T(8,128)(2,1)S(1)}, bf16[4,80,384]{2,1,0:T(8,128)(2,1)S(1)}, u32[]{:S(2)}, u32[]{:S(2)}) collective-permute-start(bf16[4,80,384]{2,1,0:T(8,128)(2,1)S(1)} %get-tuple-element.63), channel_id=1, source_target_pairs={{0,24},{1,25},{2,26},{3,27},{4,28},{5,29},{6,30},{7,31},{8,0},{9,1... | collective-permute-start | bytes 737288 | tf_op jit(solution)/shard_map/ppermute | solution.py:56
  94.7 10.7 %collective-permute-start.13 = (bf16[4,80,384]{2,1,0:T(8,128)(2,1)S(1)}, bf16[4,80,384]{2,1,0:T(8,128)(2,1)S(1)}, u32[]{:S(2)}, u32[]{:S(2)}) collective-permute-start(bf16[4,80,384]{2,1,0:T(8,128)(2,1)S(1)} %get-tuple-element.66), channel_id=1, source_target_pairs={{0,6},{1,7},{2,0},{3,1},{4,2},{5,3},{6,4},{7,5},{8,14},{9,15},{10,... | collective-permute-start | bytes 737288 | tf_op jit(solution)/shard_map/ppermute | solution.py:56
  97.4 10.7 %collective-permute-start.12 = (bf16[4,80,384]{2,1,0:T(8,128)(2,1)S(1)}, bf16[4,80,384]{2,1,0:T(8,128)(2,1)S(1)}, u32[]{:S(2)}, u32[]{:S(2)}) collective-permute-start(bf16[4,80,384]{2,1,0:T(8,128)(2,1)S(1)} %get-tuple-element.67), channel_id=1, source_target_pairs={{0,4},{1,5},{2,6},{3,7},{4,0},{5,1},{6,2},{7,3},{8,12},{9,13},{10,... | collective-permute-start | bytes 737288 | tf_op jit(solution)/shard_map/ppermute | solution.py:56
  110.3 10.5 %collective-permute-start.23 = (bf16[80,384]{1,0:T(8,128)(2,1)S(1)}, bf16[80,384]{1,0:T(8,128)(2,1)S(1)}, u32[]{:S(2)}, u32[]{:S(2)}) collective-permute-start(bf16[80,384]{1,0:T(8,128)(2,1)S(1)} %get-tuple-element.73), channel_id=1, source_target_pairs={{0,2},{1,3},{2,4},{3,5},{4,6},{5,7},{6,0},{7,1},{8,10},{9,11},{10,... | collective-permute-start | bytes 184328 | tf_op jit(solution)/shard_map/ppermute | solution.py:56
  122.1 15.3 %collective-permute-start.35 = (f32[384,128]{1,0:T(8,128)S(1)}, f32[384,128]{1,0:T(8,128)S(1)}, u32[]{:S(2)}, u32[]{:S(2)}) collective-permute-start(f32[384,128]{1,0:T(8,128)S(1)} %broadcast_select_fusion), channel_id=1, source_target_pairs={{0,1},{1,0},{2,3},{3,2},{4,5},{5,4},{6,7},{7,6},{8,9},{9,8},{10,11... | collective-permute-start | bytes 589832 | tf_op jit(solution)/shard_map/ppermute | solution.py:56
  136.8 14.7 %collective-permute-start.46 = (f32[32]{0:T(128)S(1)}, f32[32]{0:T(128)S(1)}, u32[]{:S(2)}, u32[]{:S(2)}) collective-permute-start(f32[32]{0:T(128)S(1)} %max.26), channel_id=1, source_target_pairs={{0,64},{1,65},{2,66},{3,67},{4,68},{5,69},{6,70},{7,71},{8,72},{9,... | collective-permute-start | bytes 392 | tf_op jit(solution)/shard_map/ppermute | solution.py:56
  137.4 15.4 %collective-permute-start.38 = (f32[384,128]{1,0:T(8,128)S(1)}, f32[384,128]{1,0:T(8,128)S(1)}, u32[]{:S(2)}, u32[]{:S(2)}) collective-permute-start(f32[384,128]{1,0:T(8,128)S(1)} %select_add_fusion.g0), channel_id=1, source_target_pairs={{0,6},{1,7},{2,0},{3,1},{4,2},{5,3},{6,4},{7,5},{8,14},{9,15},{10,... | collective-permute-start | bytes 589832 | tf_op jit(solution)/shard_map/ppermute | solution.py:56
  176.8 24.4 %collective-permute-start.58 = (bf16[4,352,128]{2,1,0:T(8,128)(2,1)S(1)}, bf16[4,352,128]{2,1,0:T(8,128)(2,1)S(1)}, u32[]{:S(2)}, u32[]{:S(2)}) collective-permute-start(bf16[4,352,128]{2,1,0:T(8,128)(2,1)S(1)} %pad_maximum_fusion.1.refs_4_), channel_id=1, source_target_pairs={{0,96},{1,97},{2,98},{3,99},{4,100},{5,101},{6,102},{7,103},{8,104... | collective-permute-start | bytes 1081352 | tf_op jit(solution)/shard_map/ppermute | solution.py:56
  178.0 12.2 %collective-permute-start.49 = (bf16[352,128]{1,0:T(8,128)(2,1)S(1)}, bf16[352,128]{1,0:T(8,128)(2,1)S(1)}, u32[]{:S(2)}, u32[]{:S(2)}) collective-permute-start(bf16[352,128]{1,0:T(8,128)(2,1)S(1)} %get-tuple-element.56), channel_id=1, source_target_pairs={{0,96},{1,97},{2,98},{3,99},{4,100},{5,101},{6,102},{7,103},{8,104... | collective-permute-start | bytes 270344 | tf_op jit(solution)/shard_map/ppermute | solution.py:56
  180.1 20.9 %collective-permute-start.48 = (bf16[352,128]{1,0:T(8,128)(2,1)S(1)}, bf16[352,128]{1,0:T(8,128)(2,1)S(1)}, u32[]{:S(2)}, u32[]{:S(2)}) collective-permute-start(bf16[352,128]{1,0:T(8,128)(2,1)S(1)} %get-tuple-element.56), channel_id=1, source_target_pairs={{0,64},{1,65},{2,66},{3,67},{4,68},{5,69},{6,70},{7,71},{8,72},{9,... | collective-permute-start | bytes 270344 | tf_op jit(solution)/shard_map/ppermute | solution.py:56
  181.0 20.0 %collective-permute-start.47 = (bf16[352,128]{1,0:T(8,128)(2,1)S(1)}, bf16[352,128]{1,0:T(8,128)(2,1)S(1)}, u32[]{:S(2)}, u32[]{:S(2)}) collective-permute-start(bf16[352,128]{1,0:T(8,128)(2,1)S(1)} %get-tuple-element.56), channel_id=1, source_target_pairs={{0,32},{1,33},{2,34},{3,35},{4,36},{5,37},{6,38},{7,39},{8,40},{9,... | collective-permute-start | bytes 270344 | tf_op jit(solution)/shard_map/ppermute | solution.py:56
  183.3 19.9 %collective-permute-start.57 = (bf16[4,352,128]{2,1,0:T(8,128)(2,1)S(1)}, bf16[4,352,128]{2,1,0:T(8,128)(2,1)S(1)}, u32[]{:S(2)}, u32[]{:S(2)}) collective-permute-start(bf16[4,352,128]{2,1,0:T(8,128)(2,1)S(1)} %pad_maximum_fusion.1.refs_4_), channel_id=1, source_target_pairs={{0,64},{1,65},{2,66},{3,67},{4,68},{5,69},{6,70},{7,71},{8,72},{9,... | collective-permute-start | bytes 1081352 | tf_op jit(solution)/shard_map/ppermute | solution.py:56
  190.2 15.8 %collective-permute-start.56 = (bf16[4,352,128]{2,1,0:T(8,128)(2,1)S(1)}, bf16[4,352,128]{2,1,0:T(8,128)(2,1)S(1)}, u32[]{:S(2)}, u32[]{:S(2)}) collective-permute-start(bf16[4,352,128]{2,1,0:T(8,128)(2,1)S(1)} %pad_maximum_fusion.1.refs_4_), channel_id=1, source_target_pairs={{0,32},{1,33},{2,34},{3,35},{4,36},{5,37},{6,38},{7,39},{8,40},{9,... | collective-permute-start | bytes 1081352 | tf_op jit(solution)/shard_map/ppermute | solution.py:56
  201.1 12.2 %collective-permute-start.52 = (bf16[4,352,128]{2,1,0:T(8,128)(2,1)S(1)}, bf16[4,352,128]{2,1,0:T(8,128)(2,1)S(1)}, u32[]{:S(2)}, u32[]{:S(2)}) collective-permute-start(bf16[4,352,128]{2,1,0:T(8,128)(2,1)S(1)} %pad_maximum_fusion.refs_0_), channel_id=1, source_target_pairs={{0,24},{1,25},{2,26},{3,27},{4,28},{5,29},{6,30},{7,31},{8,0},{9,1... | collective-permute-start | bytes 1081352 | tf_op jit(solution)/shard_map/ppermute | solution.py:56
  201.1 12.1 %collective-permute-start.51 = (bf16[4,352,128]{2,1,0:T(8,128)(2,1)S(1)}, bf16[4,352,128]{2,1,0:T(8,128)(2,1)S(1)}, u32[]{:S(2)}, u32[]{:S(2)}) collective-permute-start(bf16[4,352,128]{2,1,0:T(8,128)(2,1)S(1)} %pad_maximum_fusion.refs_0_), channel_id=1, source_target_pairs={{0,16},{1,17},{2,18},{3,19},{4,20},{5,21},{6,22},{7,23},{8,24},{9,... | collective-permute-start | bytes 1081352 | tf_op jit(solution)/shard_map/ppermute | solution.py:56
  201.2 13.3 %collective-permute-start.50 = (bf16[4,352,128]{2,1,0:T(8,128)(2,1)S(1)}, bf16[4,352,128]{2,1,0:T(8,128)(2,1)S(1)}, u32[]{:S(2)}, u32[]{:S(2)}) collective-permute-start(bf16[4,352,128]{2,1,0:T(8,128)(2,1)S(1)} %pad_maximum_fusion.refs_0_), channel_id=1, source_target_pairs={{0,8},{1,9},{2,10},{3,11},{4,12},{5,13},{6,14},{7,15},{8,16},{9,17... | collective-permute-start | bytes 1081352 | tf_op jit(solution)/shard_map/ppermute | solution.py:56
  (43 other events, 491.9 us)

commit v2 on v0

v2 whole, which is shorter than its diff:
```python
import functools
import math

import jax
import jax.numpy as jnp
from jax import lax
from jax.experimental import pallas as pl
from jax.experimental.pallas import tpu as pltpu
from jax.sharding import PartitionSpec as P

QL = 1536
KVL = 512
QH = 192
QROPE = 64
KH = 128
ITERS = 5

momentum_decay = 0.9
learn_rate = 0.2
weight_decay = 0.1
clip_limit = 100.0
norm_epsilon = 1e-07
coef_first = 3.4445
coef_second = -4.775
coef_third = 2.0315

N = 4
QC, KC = 384, 256
QR, KR = 192, 64
RP, RC = 80, 32
MP = RP * 3
MC = RC * 3 + KR * 2
ML = 16
M_ALL = 2 * MP + MC
G_ROWS = 384

f32, bf16 = jnp.float32, jnp.bfloat16
AXES = ("dp", "ctx")
VMEM = pl.BlockSpec(memory_space=pltpu.VMEM)
SMEM = pl.BlockSpec(memory_space=pltpu.SMEM)
HBM = pl.BlockSpec(memory_space=pltpu.HBM)
HIGHEST = lax.Precision.HIGHEST


def params(mib):
    return pltpu.CompilerParams(vmem_limit_bytes=mib << 20)


def out(shape, dtype):
    return jax.ShapeDtypeStruct(shape, dtype)


def place(z, x, y, c):
    return ((z % N) * N + x % N) * 2 * N + (y % N) * 2 + c


def shift(array, axes, steps):
    def target(z, x, y, c):
        axis, by = axes[c], steps[c]
        return (z + by * (axis == "z"), x + by * (axis == "x"), y + by * (axis == "y"), c)

    pairs = [
        (place(z, x, y, c), place(*target(z, x, y, c)))
        for z in range(N)
        for x in range(N)
        for y in range(N)
        for c in range(2)
    ]
    return lax.ppermute(array, AXES, pairs)


def swap(array):
    pairs = [(i, i ^ 1) for i in range(2 * N**3)]
    return lax.ppermute(array, AXES, pairs)


def read(where):
    return where[0], where[1], where[2], where[3]


def columns(zz, xx, width, lane=None):
    start = (zz * N + xx) * width
    if lane is None:
        return pl.ds(pl.multiple_of(start, 128), width)
    return pl.ds(pl.multiple_of(start + lane * 128, 128), 128)


def slice_copies(where, other, step, query, key, logits, scratch):
    blocks, c_query, c_key, own_logits, sems = scratch
    z, x, y, core = read(where)
    if other:
        core = 1 - core
    ahead = N - step
    here = jnp.where(core == 0, x, z) + N
    block_c = (y + (1 - 2 * core) * ahead + N) % N
    main = []
    for i in range(N):
        for owner, block in ((0, (here + ahead) % N), (1, (here - ahead) % N)):
            start = jnp.where(core == 0, i * N + block, block * N + i) * QC
            main.append(
                pltpu.make_async_copy(
                    query.at[
                        :,
                        owner,
                        pl.ds(pl.multiple_of(core * RP, 16), RP),
                        pl.ds(pl.multiple_of(start, 128), QC),
                    ],
                    blocks.at[owner, i],
                    sems.at[owner * N + i],
                )
            )
    rest = [pltpu.make_async_copy(logits, own_logits, sems.at[2 * N])]
    for half in range(2):
        rows = pl.ds(half * RC // 2, RC // 2)
        rest.append(
            pltpu.make_async_copy(
                query.at[block_c, core, pl.ds(2 * RP + half * RC // 2, RC // 2), :],
                c_query.at[rows, :],
                sems.at[2 * N + 1 + 2 * half],
            )
        )
        rows = pl.ds(half * KR // 2, KR // 2)
        rest.append(
            pltpu.make_async_copy(
                key.at[block_c, core, rows, :],
                c_key.at[rows, :],
                sems.at[2 * N + 2 + 2 * half],
            )
        )
    return core, main, rest


def split_logits(value):
    high = value.astype(bf16)
    rest = value - high.astype(f32)
    middle = rest.astype(bf16)
    low = (rest - middle.astype(f32)).astype(bf16)
    return high, middle, low


def join_logits(rows):
    rows = rows.astype(f32)
    return rows[0:1] + rows[1:2] + rows[2:3]


def logit_rows(value):
    high, middle, low = (part.astype(f32) for part in split_logits(value))
    row = lax.broadcasted_iota(jnp.int32, (ML, 128), 0)
    return jnp.where(row == 0, high, jnp.where(row == 1, middle, jnp.where(row == 2, low, 0.0)))


def slice_kernel(step, where, query, key, logits, to, *scratch):
    scratch, lanes = scratch[:-1], scratch[-1]
    blocks, c_query, c_key, own_logits, _ = scratch
    core, main, rest = slice_copies(where, True, step, query, key, logits, scratch)
    for copy in rest + main:
        copy.start()
    lanes[...] = jnp.zeros_like(lanes)
    for copy in rest:
        copy.wait()
    lanes[pl.ds(0, 1), pl.ds(0, 32)] = own_logits[...]
    logit_block = logit_rows(lanes[pl.ds(0, 1), :]).astype(bf16)

    @pl.loop(0, N * N)
    def _(i):
        at = (i // N, i % N)
        to[at + (pl.ds(M_ALL, ML),)] = logit_block
        for source, height, width, start, size in (
            (c_query, RC, 3, 0, QC),
            (c_key, KR, 2, 3 * RC, KC),
        ):
            for lane in range(width):
                to[at + (pl.ds(2 * MP + start + lane * height, height),)] = source[
                    :, columns(at[0], at[1], size, lane)
                ]

    for i in range(N):
        main[2 * i].wait()
        main[2 * i + 1].wait()

        @pl.loop(0, N)
        def _(j):
            first, second = jnp.where(core == 0, j, i), jnp.where(core == 0, i, j)
            for owner in range(2):
                block = blocks[owner, i, j]
                for lane in range(3):
                    to[first, second, pl.ds(owner * MP + lane * RP, RP), :] = block[
                        :, lane * 128 : (lane + 1) * 128
                    ]


def slice_scratch():
    return [
        pltpu.VMEM((2, N, N, RP, QC), bf16),
        pltpu.VMEM((RC, N * N * QC), bf16),
        pltpu.VMEM((KR, N * N * KC), bf16),
        pltpu.VMEM((1, 32), f32),
        pltpu.SemaphoreType.DMA((2 * N + 5,)),
        pltpu.VMEM((8, 128), f32),
    ]


def in_hbm(*arrays):
    return tuple(pltpu.with_memory_space_constraint(a, pltpu.HBM) for a in arrays)


def in_hbm(*arrays):
    return tuple(pltpu.with_memory_space_constraint(a, pltpu.HBM) for a in arrays)


def slice_other(step, where, query, key, logits):
    return pl.pallas_call(
        functools.partial(slice_kernel, step),
        out_shape=out((N, N, M_ALL + ML, 128), bf16),
        in_specs=[SMEM, HBM, HBM, HBM],
        out_specs=VMEM,
        scratch_shapes=slice_scratch(),
        compiler_params=params(8),
        name=f"slice_other_{step}",
    )(where, *in_hbm(query, key, logits))


def total(*terms):
    value = terms[0].astype(f32)
    for term in terms[1:]:
        value = value + term.astype(f32)
    return value


def most(*terms):
    value = join_logits(terms[0])
    for term in terms[1:]:
        value = jnp.maximum(value, join_logits(term))
    return logit_rows(value)


def pre_kernel(step, where, query, key, logits, other, p, m, c, *scratch):
    scratch, lanes = scratch[:-1], scratch[-1]
    blocks, c_query, c_key, own_logits, _ = scratch
    core, main, rest = slice_copies(where, False, step, query, key, logits, scratch)
    for copy in rest + main:
        copy.start()
    lanes[...] = jnp.zeros_like(lanes)
    for copy in rest:
        copy.wait()
    lanes[pl.ds(0, 1), pl.ds(0, 32)] = own_logits[...]
    peak = jnp.maximum(
        lanes[pl.ds(0, 1), :], join_logits(other[0, 0, pl.ds(M_ALL, ML), :])
    )
    logit_block = logit_rows(peak).astype(bf16)

    @pl.loop(0, N * N)
    def _(i):
        at = (i // N, i % N)
        c[at + (pl.ds(MC, ML),)] = logit_block
        for source, height, width, start, size in (
            (c_query, RC, 3, 0, QC),
            (c_key, KR, 2, 3 * RC, KC),
        ):
            for lane in range(width):
                rows = start + lane * height
                c[at + (pl.ds(rows, height),)] = total(
                    source[:, columns(at[0], at[1], size, lane)],
                    other[at + (pl.ds(2 * MP + rows, height),)],
                ).astype(bf16)

    for i in range(N):
        main[2 * i].wait()
        main[2 * i + 1].wait()

        @pl.loop(0, N)
        def _(j):
            first, second = jnp.where(core == 0, j, i), jnp.where(core == 0, i, j)
            for owner, to in ((0, p), (1, m)):
                block = blocks[owner, i, j]
                for lane in range(3):
                    to[first, second, pl.ds(lane * RP, RP), :] = total(
                        block[:, lane * 128 : (lane + 1) * 128],
                        other[first, second, pl.ds(owner * MP + lane * RP, RP), :],
                    ).astype(bf16)


def pre_sum(step, where, query, key, logits, other):
    return pl.pallas_call(
        functools.partial(pre_kernel, step),
        out_shape=[out((N, N, height, 128), bf16) for height in (MP, MP, MC + ML)],
        in_specs=[SMEM, HBM, HBM, HBM, VMEM],
        out_specs=[VMEM] * 3,
        scratch_shapes=slice_scratch(),
        compiler_params=params(12),
        name=f"pre_sum_{step}",
    )(where, *in_hbm(query, key, logits), other)


def ring_add_kernel(p0, m0, c0, p1, m1, c1, p, m, c):
    peak = most(c0[0, 0, pl.ds(MC, ML), :], c1[0, 0, pl.ds(MC, ML), :]).astype(bf16)

    @pl.loop(0, N * N)
    def _(i):
        at = (i // N, i % N)
        p[at] = total(p0[at], p1[at]).astype(bf16)
        m[at] = total(m0[at], m1[at]).astype(bf16)
        rows = at + (pl.ds(0, MC),)
        c[rows] = total(c0[rows], c1[rows]).astype(bf16)
        c[at + (pl.ds(MC, ML),)] = peak


def ring_add(own, received):
    return pl.pallas_call(
        ring_add_kernel,
        out_shape=[out(a.shape, bf16) for a in own],
        in_specs=[VMEM] * 6,
        out_specs=[VMEM] * 3,
        compiler_params=params(14),
        name="ring_add",
    )(*own, *received)


def split_ab_kernel(where, p0, m0, p1, m1, *outs):
    _, x, y, core = read(where)
    here = jnp.where(core == 0, y, x)
    for by, to in enumerate(outs):
        block = (here + by) % N

        @pl.loop(0, N)
        def _(i):
            to[i, pl.ds(0, MP), :] = total(p0[block, i], p1[block, i]).astype(bf16)
            to[i, pl.ds(MP, MP), :] = total(m0[block, i], m1[block, i]).astype(bf16)


def split_ab(where, own, received):
    return pl.pallas_call(
        split_ab_kernel,
        out_shape=[out((N, 2 * MP, 128), bf16)] * N,
        in_specs=[SMEM] + [VMEM] * 4,
        out_specs=[VMEM] * N,
        compiler_params=params(10),
        name="split_ab",
    )(where, *own, *received)


def split_c_kernel(where, c0, c1, *outs):
    peak = most(c0[0, 0, pl.ds(MC, ML), :], c1[0, 0, pl.ds(MC, ML), :]).astype(bf16)
    for by, to in enumerate(outs):
        block = (where[0] + by) % N

        @pl.loop(0, N)
        def _(i):
            rows = (block, i, pl.ds(0, MC))
            to[i, pl.ds(0, MC), :] = total(c0[rows], c1[rows]).astype(bf16)
            to[i, pl.ds(MC, ML), :] = peak


def split_c(where, own, received):
    return pl.pallas_call(
        split_c_kernel,
        out_shape=[out((N, MC + ML, 128), bf16)] * N,
        in_specs=[SMEM] + [VMEM] * 2,
        out_specs=[VMEM] * N,
        compiler_params=params(6),
        name="split_c",
    )(where, own, received)


def next_ab_kernel(where, t0, t1, t2, t3, *outs):
    z, _, y, core = read(where)
    here = jnp.where(core == 0, z, y)
    for by, to in enumerate(outs):
        block = (here + by) % N
        to[...] = total(t0[block], t1[block], t2[block], t3[block]).astype(bf16)


def next_c_kernel(where, t0, t1, t2, t3, *outs):
    terms = (t0, t1, t2, t3)
    peak = most(*(t[0, pl.ds(MC, ML), :] for t in terms)).astype(bf16)
    for by, to in enumerate(outs):
        rows = ((where[1] + by) % N, pl.ds(0, MC))
        to[pl.ds(0, MC), :] = total(*(t[rows] for t in terms)).astype(bf16)
        to[pl.ds(MC, ML), :] = peak


def next_parts(kernel, name, where, terms):
    return pl.pallas_call(
        kernel,
        out_shape=[out((terms[0].shape[1], 128), bf16)] * N,
        in_specs=[SMEM] + [VMEM] * N,
        out_specs=[VMEM] * N,
        compiler_params=params(6),
        name=name,
    )(where, *terms)


def scatter(blocks, axes):
    return [blocks[0]] + [shift(blocks[by], axes, (by, by)) for by in (1, 2, 3)]


def moment_kernel(
    where, a0, a1, a2, a3, c0, c1, c2, c3, qm, theirs, km, qm_out, km_out, gram0, gram1, peak
):
    core = where[3]
    part = total(a0[...], a1[...], a2[...], a3[...])
    rows = pl.ds(0, MC)
    part_c = total(c0[rows, :], c1[rows, :], c2[rows, :], c3[rows, :])
    rows = pl.ds(MC, ML)
    value = join_logits(c0[rows, :])
    for ref in (c1, c2, c3):
        value = jnp.maximum(value, join_logits(ref[rows, :]))
    peak[...] = jnp.broadcast_to(value, (8, 128))
    for lane in range(3):
        lanes = pl.ds(lane * 128, 128)
        for owner in range(2):
            rows = pl.ds(owner * RP, RP)
            start = owner * MP + lane * RP
            moment = jnp.where(core == owner, qm[rows, lanes], theirs[:, lanes])
            qm_out[rows, lanes] = momentum_decay * moment + part[start : start + RP]
        rows = pl.ds(2 * RP, RC)
        qm_out[rows, lanes] = (
            momentum_decay * qm[rows, lanes] + part_c[lane * RC : (lane + 1) * RC]
        )
    for lane in range(2):
        lanes = pl.ds(lane * 128, 128)
        start = 3 * RC + lane * KR
        km_out[:, lanes] = momentum_decay * km[:, lanes] + part_c[start : start + KR]

    def gram_of(value):
        return lax.dot_general(
            value, value, (((0,), (0,)), ((), ())), precision=HIGHEST, preferred_element_type=f32
        )

    full = qm_out[...]
    for head, to in enumerate((gram0, gram1)):
        wide = (full if head == 0 else pltpu.roll(full, QH, 1))[:, :256]
        gram = gram_of(wide)
        to[pl.ds(0, 192), :] = gram[:192, :128]
        to[pl.ds(192, 64), :] = gram[128:192, 128:]
        to[pl.ds(256, 128), :] = gram_of(km_out[:, pl.ds(head * KH, KH)])


def moments(where, part, part_c, query_moment, theirs, key_moment):
    return pl.pallas_call(
        moment_kernel,
        out_shape=(
            out((QR, QC), f32),
            out((KR, KC), f32),
            out((G_ROWS, 128), f32),
            out((G_ROWS, 128), f32),
            out((8, 128), f32),
        ),
        in_specs=[SMEM] + [VMEM] * 11,
        out_specs=(VMEM,) * 5,
        compiler_params=params(12),
        name="moments",
    )(where, *part, *part_c, query_moment, theirs, key_moment)


def chain_kernel(g0, g1, g2, g3, to):
    packed = g0[...] + g1[...] + g2[...] + g3[...]
    top, side, corner = packed[:128], packed[128:192], packed[192:256]
    key_gram = packed[256:384]
    row = lax.broadcasted_iota(jnp.int32, (256, 256), 0)
    column = lax.broadcasted_iota(jnp.int32, (256, 256), 1)
    zeros = jnp.zeros((64, 128), f32)
    lower = jnp.concatenate([side, zeros], axis=0)
    query_gram = jnp.concatenate(
        [
            jnp.concatenate([top, lower.T], axis=1),
            jnp.concatenate([lower, jnp.concatenate([corner, zeros], axis=0)], axis=1),
        ],
        axis=0,
    )
    query_gram = jnp.where((row < QH) & (column < QH), query_gram, 0.0)
    query_eye = jnp.where((row == column) & (row < QH), 1.0, 0.0).astype(f32)
    key_eye = jnp.where(row == column, 1.0, 0.0).astype(f32)[:128, :128]

    def product(left, right):
        return jnp.dot(left, right, precision=HIGHEST, preferred_element_type=f32)

    def start(gram, eye):
        square = jnp.sum(jnp.sum(gram * eye, axis=1, keepdims=True), axis=0, keepdims=True)
        inverse = 1.0 / (jnp.sqrt(square) + norm_epsilon)
        return gram * inverse * inverse, inverse

    grams, inverses = zip(start(query_gram, query_eye), start(key_gram, key_eye))
    grams, eyes, totals = list(grams), (query_eye, key_eye), [None, None]
    for iteration in range(ITERS):
        mixers = []
        for i in range(2):
            square = product(grams[i], grams[i])
            mixers.append(coef_first * eyes[i] + coef_second * grams[i] + coef_third * square)
        if iteration < ITERS - 1:
            halves = [product(mixers[i], grams[i]) for i in range(2)]
        for i in range(2):
            totals[i] = mixers[i] if iteration == 0 else product(totals[i], mixers[i])
        if iteration < ITERS - 1:
            grams = [product(halves[i], mixers[i]) for i in range(2)]
    query_total, key_total = (totals[i] * inverses[i] for i in range(2))
    to[pl.ds(0, 192), :] = query_total[:192, :128]
    to[pl.ds(192, 192), :] = query_total[:192, 128:]
    to[pl.ds(384, 128), :] = key_total


def chain(grams):
    return pl.pallas_call(
        chain_kernel,
        out_shape=out((512, 128), f32),
        in_specs=[VMEM] * 4,
        out_specs=VMEM,
        compiler_params=params(12),
        name="newton_schulz_polynomial",
    )(*grams)

def update_kernel(where, own, other, peak, qm, km, qw, kw, to):
    z, x, _, core = read(where)
    mine, theirs = own[...], other[...]
    packs = (jnp.where(core == 0, mine, theirs), jnp.where(core == 0, theirs, mine))

    def product(left, right):
        return jnp.dot(left, right, precision=HIGHEST, preferred_element_type=f32)

    gamma = jnp.minimum(1.0, clip_limit / peak[pl.ds(0, 1), :])
    lane = lax.broadcasted_iota(jnp.int32, (1, 128), 1)
    first_head = 2 * (z * N + x)
    gammas = [
        jnp.sum(jnp.where(lane == first_head + h, gamma, 0.0), axis=1, keepdims=True)
        for h in range(2)
    ]
    roots = [jnp.sqrt(g) for g in gammas]
    column = lax.broadcasted_iota(jnp.int32, (1, QC), 1)
    second = column >= QH
    rope = jnp.where(second, column - QH, column) >= QH - QROPE
    query_factor = jnp.where(
        rope, jnp.where(second, gammas[1], gammas[0]), jnp.where(second, roots[1], roots[0])
    )
    key_factor = jnp.where(
        lax.broadcasted_iota(jnp.int32, (1, KC), 1) >= KH, roots[1], roots[0]
    )

    full = qm[...]
    zeros = jnp.zeros((64, 256), f32)
    pad = jnp.zeros((QR, 128), f32)
    pieces = []
    for head in range(2):
        wide = (full if head == 0 else pltpu.roll(full, QH, 1))[:, :256]
        matrix = jnp.concatenate([packs[head][:192], packs[head][192:384]], axis=1)
        matrix = jnp.concatenate([matrix, zeros], axis=0)
        piece = jnp.concatenate([product(wide, matrix), pad], axis=1)
        pieces.append(piece if head == 0 else pltpu.roll(piece, QH, 1))
    query_ortho = pieces[0] + pieces[1]
    key_ortho = jnp.concatenate(
        [product(km[:, pl.ds(h * KH, KH)], packs[h][384:]) for h in range(2)], axis=1
    )
    query_scale = 0.2 * math.sqrt(max(QL, QH))
    key_scale = 0.2 * math.sqrt(max(KVL, KH))
    query_weight, key_weight = qw[...], kw[...]
    query_next = query_weight - learn_rate * (
        query_scale * query_ortho + weight_decay * query_weight
    )
    key_next = key_weight - learn_rate * (key_scale * key_ortho + weight_decay * key_weight)
    query_block = (query_next * query_factor).astype(bf16)
    key_block = (key_next * key_factor).astype(bf16)
    for lane in range(3):
        to[pl.ds(lane * QR, QR), :] = query_block[:, lane * 128 : (lane + 1) * 128]
    for lane in range(2):
        to[pl.ds(3 * QR + lane * KR, KR), :] = key_block[:, lane * 128 : (lane + 1) * 128]


def update(where, own, other, peak, query_moment, key_moment, query_weight, key_weight):
    return pl.pallas_call(
        update_kernel,
        out_shape=out((M_ALL, 128), bf16),
        in_specs=[SMEM] + [VMEM] * 7,
        out_specs=VMEM,
        compiler_params=params(12),
        name="update",
    )(where, own, other, peak, query_moment, key_moment, query_weight, key_weight)


def assemble_kernel(where, s0, s1, s2, s3, query_out, key_out):
    z, x, _, core = read(where)
    for far, stack in enumerate((s0, s1, s2, s3)):

        @pl.loop(0, N)
        def _(near):
            back_z = jnp.where(core == 0, near, far)
            back_x = jnp.where(core == 0, far, near)
            zz, xx = (z + N - back_z) % N, (x + N - back_x) % N
            for lane in range(3):
                query_out[:, columns(zz, xx, QC, lane)] = stack[near, pl.ds(lane * QR, QR), :]
            for lane in range(2):
                key_out[:, columns(zz, xx, KC, lane)] = stack[
                    near, pl.ds(3 * QR + lane * KR, KR), :
                ]


def assemble(where, stacks):
    return pl.pallas_call(
        assemble_kernel,
        out_shape=(out((QR, N * N * QC), bf16), out((KR, N * N * KC), bf16)),
        in_specs=[SMEM] + [VMEM] * N,
        out_specs=(VMEM, VMEM),
        compiler_params=params(16),
        name="assemble",
    )(where, *stacks)


def on_device(grad_query, grad_key, query_weight, key_weight, query_moment, key_moment, max_logits):
    dp, ctx = lax.axis_index("dp"), lax.axis_index("ctx")
    z, x, y, core = dp // N, dp % N, ctx // 2, ctx % 2
    where = jnp.stack([z, x, y, core]).astype(jnp.int32)
    query = grad_query.reshape(N, 2, QR, N * N * QC)
    key = grad_key.reshape(N, 2, KR, N * N * KC)

    def after(value):
        return lax.optimization_barrier((where, value))[0]

    first = slice_other(1, where, query, key, max_logits)
    second = slice_other(2, after(first), query, key, max_logits)
    others, pre = [swap(first), swap(second)], []
    for step in range(1, N + 1):
        pre.append(pre_sum(step, where, query, key, max_logits, others[step - 1]))
        if step + 2 <= N:
            blocks = slice_other(step + 2, after(pre[-1][2]), query, key, max_logits)
            others.append(swap(blocks))

    parts = pre[0]
    for step in range(1, N):
        p, m, c = parts
        p = shift(p, ("x", "z"), (1, 1))
        m = shift(m, ("x", "z"), (-1, -1))
        c = shift(c, ("y", "y"), (1, -1))
        if step < N - 1:
            parts = ring_add(pre[step], (p, m, c))
        if step == 1:
            start = (1 - after(parts[0])[3]) * RP
            theirs = swap(lax.dynamic_slice_in_dim(query_moment, start, RP, 0))
        if step == 2:
            theirs, parts = lax.optimization_barrier((theirs, parts))
    pre = pre[-1]

    part = split_ab(where, pre[:2], (p, m))
    part_c = split_c(after(part[0]), pre[2], c)
    part, part_c = scatter(part, ("y", "x")), scatter(part_c, ("z", "z"))
    part = next_parts(next_ab_kernel, "next_ab", where, part)
    part_c = next_parts(next_c_kernel, "next_c", after(part[0]), part_c)
    part, part_c = scatter(part, ("z", "y")), scatter(part_c, ("x", "x"))
    moment, new_key_moment, gram0, gram1, peak = moments(
        where, part, part_c, query_moment, theirs, key_moment
    )

    keep, give = jnp.where(core == 0, gram0, gram1), jnp.where(core == 0, gram1, gram0)
    gram = keep + swap(give)
    own = chain([gram] + [shift(gram, ("y", "y"), (by, by)) for by in (1, 2, 3)])

    theirs = swap(lax.dynamic_slice_in_dim(moment, (1 - core) * RP, RP, 0))
    new_query_moment = jnp.concatenate(
        [
            jnp.where(core == 0, moment[:RP], theirs),
            jnp.where(core == 0, theirs, moment[RP : 2 * RP]),
            moment[2 * RP :],
        ]
    )
    block = update(
        where, own, swap(own), peak, new_query_moment, new_key_moment, query_weight, key_weight
    )
    stack = jnp.stack([block] + [shift(block, ("z", "x"), (by, by)) for by in (1, 2, 3)])
    stacks = [stack] + [shift(stack, ("x", "z"), (by, by)) for by in (1, 2, 3)]
    query_out, key_out = assemble(where, stacks)
    return (query_out, key_out, new_query_moment, new_key_moment)


def solution(mesh):
    in_specs = (
        P(("dp", "ctx"), None, None),
        P(("dp", "ctx"), None, None),
        P("ctx", "dp"),
        P("ctx", "dp"),
        P("ctx", "dp"),
        P("ctx", "dp"),
        P(("dp", "ctx"), None),
    )
    out_specs = (P("ctx", None), P("ctx", None), P("ctx", "dp"), P("ctx", "dp"))
    return jax.shard_map(
        on_device, mesh=mesh, in_specs=in_specs, out_specs=out_specs, check_vma=False
    )
```

time: 452 us -> 168 us (0.37)
  waiting for transfers between devices: 248 us -> 64 us
  blocking collectives: 104 us -> 0 us
  starting transfers between devices: 0.24 us -> 51.2 us
  Pallas kernels: 0 us -> 48.5 us
  matrix products: 37.7 us -> 0 us
  local copies, waits for them, and re-layouts: 33.9 us -> 0.64 us
  between operations: 14.7 us -> 1.64 us
  other arithmetic: 9.22 us -> 0.27 us
    unnamed x7 -> x0, waiting for transfers between devices: 124 us -> none
    reduce_scatter x3 -> x0, waiting for transfers between devices: 109 us -> none  [the longest x1 77.4 us: on_device(): lax.psum_scatter(key_terms, 'dp', scatter_dimension=1, tiled=True)]
    pmax x1 -> x0, blocking collectives: 66.6 us -> none  [on_device(): peak = lax.pmax(max_logits[0], ('dp', 'ctx'))]
    ppermute x0 -> x38, waiting for transfers between devices: none -> 64 us  [the longest x30 59.1 us: shift(): return lax.ppermute(array, AXES, pairs)]
    ppermute x0 -> x38, starting transfers between devices: none -> 51.2 us  [the longest x30 49.8 us: shift(): return lax.ppermute(array, AXES, pairs)]
    pallas_call x0 -> x18, Pallas kernels: none -> 48.5 us  [the longest x4 14 us: slice_other(): pl.pallas_call(functools.partial(slice_kernel, step), out_shape=out((N, N...]
    dot_general x30 -> x0, matrix products: 37.7 us -> none  [the longest x10 15.7 us: iterate_blocks(): jnp.einsum('rhi,hij->rhj', blocks, mixer, precision=lax.Precision.HIGHEST)]
    all_gather x2 -> x0, blocking collectives: 37.5 us -> none  [the longest x1 24.3 us: on_device(): lax.all_gather(key_block, 'dp', axis=1, tiled=True)]
  transfers between devices with their start and end apart: 6 -> 38, of which waited for: 4 -> 22; matrix products, arithmetic and copies ran while one was open for 4% -> 0% of each run, Pallas kernels for 0% -> 24%
where the time goes in v2:
time: 168 us; the launch traced here: 166 us
  waiting for transfers between devices  64 us (38%)
  starting transfers between devices  51.2 us (30%)
  Pallas kernels  48.5 us (29%)
    ppermute x30, waiting for transfers between devices, shift(): return lax.ppermute(array, AXES, pairs)  59.1 us
    ppermute x30, starting transfers between devices, shift(): return lax.ppermute(array, AXES, pairs)  49.8 us
    pallas_call x4, Pallas kernels, slice_other(): pl.pallas_call(functools.partial(slice_kernel, step), out_shape=out((N, N...  14 us
    pallas_call x4, Pallas kernels, pre_sum(): pl.pallas_call(functools.partial(pre_kernel, step), out_shape=[out((N, N,...  13.1 us
    pallas_call x1, Pallas kernels, chain(): pl.pallas_call(chain_kernel, out_shape=out((512, 128), f32), in_specs=[VM...  7.1 us
    pallas_call x2, Pallas kernels, ring_add(): pl.pallas_call(ring_add_kernel, out_shape=[out(a.shape, bf16) for a in ow...  5.2 us
    ppermute x8, waiting for transfers between devices, swap(): return lax.ppermute(array, AXES, pairs)  4.96 us
  transfers between devices with their start and end apart: 38, of which 22 were waited for; matrix products, arithmetic and copies ran while one was open for 0% of the time, Pallas kernels for 24%

profile of v2, /device:TPU:8, one launch (start us, length us, event | category | flops | bytes accessed | tf_op | source)
XLA Modules:
  0.0 166.3 jit_solution(16976230436410722125)
XLA Ops:
  0.7 2.7 %slice_other_1.1 = bf16[4,4,720,128]{3,2,1,0:T(8,128)(2,1)S(1)} custom-call(s32[4]{0:T(128)S(1)} %pad_add_fusion.where, bf16[4,2,192,6144]{3,2,1,0:T(8,128)(2,1)} %bitcast.12, bf16[4,2,64,4096]{3,2,1,0:T(8,128)(2,1)} %bitcast.20, f32[1,32]{1,0:T(1,128)} %logits.15), custom_call_target="tpu_custom_call" | custom-call | tf_op jit(solution)/shard_map/slice_other_1/pallas_call | solution.py:212
  3.5 2.7 %slice_other_2.1 = bf16[4,4,720,128]{3,2,1,0:T(8,128)(2,1)S(1)} custom-call(s32[4]{0:T(128)S(1)} %pad_add_fusion.where, bf16[4,2,192,6144]{3,2,1,0:T(8,128)(2,1)} %bitcast.13, bf16[4,2,64,4096]{3,2,1,0:T(8,128)(2,1)} %bitcast.21, f32[1,32]{1,0:T(1,128)} %logits.15), custom_call_target="tpu_custom_call" | custom-call | tf_op jit(solution)/shard_map/slice_other_2/pallas_call | solution.py:212
  6.8 2.1 %collective-permute-done.2.other = bf16[4,4,720,128]{3,2,1,0:T(8,128)(2,1)S(1)} collective-permute-done((bf16[4,4,720,128]{3,2,1,0:T(8,128)(2,1)S(1)}, bf16[4,4,720,128]{3,2,1,0:T(8,128)(2,1)S(1)}, u32[]{:S(2)}, u32[]{:S(2)}) %collective-permute-start.2) | collective-permute-done | bytes 2949152 | tf_op jit(solution)/shard_map/ppermute | solution.py:74
  8.9 2.9 %pre_sum_1.1 = (bf16[4,4,240,128]{3,2,1,0:T(8,128)(2,1)S(1)}, bf16[4,4,240,128]{3,2,1,0:T(8,128)(2,1)S(1)}, bf16[4,4,240,128]{3,2,1,0:T(8,128)(2,1)S(1)}) custom-call(s32[4]{0:T(128)S(1)} %pad_add_fusion.where, bf16[4,2,192,6144]{3,2,1,0:T(8,128)(2,1)} %bitcast.14, bf16[4,2,64,4096]{3,2,1,0:T(8,128)(2,1)} %bitcast.22, f32[1,32]{1,0:T(1,128)} %logits.15, ...), custom_call_target="tpu_custom_call" | custom-call | tf_op jit(solution)/shard_map/pre_sum_1/pallas_call | solution.py:284
  11.8 4.3 %slice_other_3.1 = bf16[4,4,720,128]{3,2,1,0:T(8,128)(2,1)} custom-call(s32[4]{0:T(128)S(1)} %pad_add_fusion.where, bf16[4,2,192,6144]{3,2,1,0:T(8,128)(2,1)} %bitcast.15, bf16[4,2,64,4096]{3,2,1,0:T(8,128)(2,1)} %bitcast.23, f32[1,32]{1,0:T(1,128)} %logits.15), custom_call_target="tpu_custom_call" | custom-call | tf_op jit(solution)/shard_map/slice_other_3/pallas_call | solution.py:212
  21.2 2.9 %pre_sum_2.1 = (bf16[4,4,240,128]{3,2,1,0:T(8,128)(2,1)S(1)}, bf16[4,4,240,128]{3,2,1,0:T(8,128)(2,1)S(1)}, bf16[4,4,240,128]{3,2,1,0:T(8,128)(2,1)S(1)}) custom-call(s32[4]{0:T(128)S(1)} %pad_add_fusion.where, bf16[4,2,192,6144]{3,2,1,0:T(8,128)(2,1)} %bitcast.16, bf16[4,2,64,4096]{3,2,1,0:T(8,128)(2,1)} %bitcast.24, f32[1,32]{1,0:T(1,128)} %logits.15, ...), custom_call_target="tpu_custom_call" | custom-call | tf_op jit(solution)/shard_map/pre_sum_2/pallas_call | solution.py:284
  24.1 4.3 %slice_other_4.1 = bf16[4,4,720,128]{3,2,1,0:T(8,128)(2,1)} custom-call(s32[4]{0:T(128)S(1)} %pad_add_fusion.where, bf16[4,2,192,6144]{3,2,1,0:T(8,128)(2,1)} %bitcast.17, bf16[4,2,64,4096]{3,2,1,0:T(8,128)(2,1)} %bitcast.25, f32[1,32]{1,0:T(1,128)} %logits.15), custom_call_target="tpu_custom_call" | custom-call | tf_op jit(solution)/shard_map/slice_other_4/pallas_call | solution.py:212
  28.5 3.2 %collective-permute-done.3.p1 = bf16[4,4,240,128]{3,2,1,0:T(8,128)(2,1)S(1)} collective-permute-done((bf16[4,4,240,128]{3,2,1,0:T(8,128)(2,1)S(1)}, bf16[4,4,240,128]{3,2,1,0:T(8,128)(2,1)S(1)}, u32[]{:S(2)}, u32[]{:S(2)}) %collective-permute-start.3) | collective-permute-done | bytes 983072 | tf_op jit(solution)/shard_map/ppermute | solution.py:69
  33.7 2.6 %ring_add.2 = (bf16[4,4,240,128]{3,2,1,0:T(8,128)(2,1)}, bf16[4,4,240,128]{3,2,1,0:T(8,128)(2,1)}, bf16[4,4,240,128]{3,2,1,0:T(8,128)(2,1)}) custom-call(bf16[4,4,240,128]{3,2,1,0:T(8,128)(2,1)S(1)} %get-tuple-element.60.p0, bf16[4,4,240,128]{3,2,1,0:T(8,128)(2,1)S(1)} %get-tuple-element.61.m0, bf16[4,4,240,128]{3,2,1,0:T(8,128)(2,1)S(1)} %get-tuple-element.56.c0, ...), custom_call_target="tpu_custom_call" | custom-call | tf_op jit(solution)/shard_map/ring_add/pallas_call | solution.py:309
  38.1 3.0 %collective-permute-start.9 = (bf16[4,4,240,128]{3,2,1,0:T(8,128)(2,1)}, bf16[4,4,240,128]{3,2,1,0:T(8,128)(2,1)}, u32[]{:S(2)}, u32[]{:S(2)}) collective-permute-start(bf16[4,4,240,128]{3,2,1,0:T(8,128)(2,1)} %get-tuple-element.71), channel_id=1, source_target_pairs={{0,24},{1,97},{2,26},{3,99},{4,28},{5,101},{6,30},{7,103},{8,0},{9... | collective-permute-start | bytes 2949128 | tf_op jit(solution)/shard_map/ppermute | solution.py:69
  42.5 4.3 %pre_sum_3.1 = (bf16[4,4,240,128]{3,2,1,0:T(8,128)(2,1)S(1)}, bf16[4,4,240,128]{3,2,1,0:T(8,128)(2,1)S(1)}, bf16[4,4,240,128]{3,2,1,0:T(8,128)(2,1)S(1)}) custom-call(s32[4]{0:T(128)S(1)} %pad_add_fusion.where, bf16[4,2,192,6144]{3,2,1,0:T(8,128)(2,1)} %bitcast.18, bf16[4,2,64,4096]{3,2,1,0:T(8,128)(2,1)} %bitcast.26, f32[1,32]{1,0:T(1,128)} %logits.15, ...), custom_call_target="tpu_custom_call" | custom-call | tf_op jit(solution)/shard_map/pre_sum_3/pallas_call | solution.py:284
  46.7 4.0 %collective-permute-done.10.c1 = bf16[4,4,240,128]{3,2,1,0:T(8,128)(2,1)} collective-permute-done((bf16[4,4,240,128]{3,2,1,0:T(8,128)(2,1)}, bf16[4,4,240,128]{3,2,1,0:T(8,128)(2,1)}, u32[]{:S(2)}, u32[]{:S(2)}) %collective-permute-start.10) | collective-permute-done | bytes 983072 | tf_op jit(solution)/shard_map/ppermute | solution.py:69
  50.7 2.8 %collective-permute-done.8.p1 = bf16[4,4,240,128]{3,2,1,0:T(8,128)(2,1)} collective-permute-done((bf16[4,4,240,128]{3,2,1,0:T(8,128)(2,1)}, bf16[4,4,240,128]{3,2,1,0:T(8,128)(2,1)}, u32[]{:S(2)}, u32[]{:S(2)}) %collective-permute-start.8) | collective-permute-done | bytes 983072 | tf_op jit(solution)/shard_map/ppermute | solution.py:69
  53.5 2.6 %ring_add.3 = (bf16[4,4,240,128]{3,2,1,0:T(8,128)(2,1)S(1)}, bf16[4,4,240,128]{3,2,1,0:T(8,128)(2,1)S(1)}, bf16[4,4,240,128]{3,2,1,0:T(8,128)(2,1)S(1)}) custom-call(bf16[4,4,240,128]{3,2,1,0:T(8,128)(2,1)S(1)} %get-tuple-element.68.p0, bf16[4,4,240,128]{3,2,1,0:T(8,128)(2,1)S(1)} %get-tuple-element.69.m0, ...), custom_call_target="tpu_custom_call" | custom-call | tf_op jit(solution)/shard_map/ring_add/pallas_call | solution.py:309
  56.8 2.8 %collective-permute-start.12 = (bf16[4,4,240,128]{3,2,1,0:T(8,128)(2,1)S(1)}, bf16[4,4,240,128]{3,2,1,0:T(8,128)(2,1)S(1)}, u32[]{:S(2)}, u32[]{:S(2)}) collective-permute-start(bf16[4,4,240,128]{3,2,1,0:T(8,128)(2,1)S(1)} %get-tuple-element.77), channel_id=1, source_target_pairs={{0,24},{1,97},{2,26},{3,99},{4,28},{5,101},{6,30},{7,103},{8,0},{9... | collective-permute-start | bytes 2949128 | tf_op jit(solution)/shard_map/ppermute | solution.py:69
  60.8 2.9 %pre_sum_4.1 = (bf16[4,4,240,128]{3,2,1,0:T(8,128)(2,1)S(1)}, bf16[4,4,240,128]{3,2,1,0:T(8,128)(2,1)S(1)}, bf16[4,4,240,128]{3,2,1,0:T(8,128)(2,1)S(1)}) custom-call(s32[4]{0:T(128)S(1)} %pad_add_fusion.where, bf16[4,2,192,6144]{3,2,1,0:T(8,128)(2,1)} %bitcast.19, bf16[4,2,64,4096]{3,2,1,0:T(8,128)(2,1)} %bitcast.27, f32[1,32]{1,0:T(1,128)} %logits.15, ...), custom_call_target="tpu_custom_call" | custom-call | tf_op jit(solution)/shard_map/pre_sum_4/pallas_call | solution.py:284
  63.8 7.8 %collective-permute-done.11.p1 = bf16[4,4,240,128]{3,2,1,0:T(8,128)(2,1)S(1)} collective-permute-done((bf16[4,4,240,128]{3,2,1,0:T(8,128)(2,1)S(1)}, bf16[4,4,240,128]{3,2,1,0:T(8,128)(2,1)S(1)}, u32[]{:S(2)}, u32[]{:S(2)}) %collective-permute-start.11) | collective-permute-done | bytes 983072 | tf_op jit(solution)/shard_map/ppermute | solution.py:69
  75.2 2.2 %collective-permute-start.15 = (bf16[4,480,128]{2,1,0:T(8,128)(2,1)S(1)}, bf16[4,480,128]{2,1,0:T(8,128)(2,1)S(1)}, u32[]{:S(2)}, u32[]{:S(2)}) collective-permute-start(bf16[4,480,128]{2,1,0:T(8,128)(2,1)S(1)} %get-tuple-element.81), channel_id=1, source_target_pairs={{0,6},{1,25},{2,0},{3,27},{4,2},{5,29},{6,4},{7,31},{8,14},{9,1},{... | collective-permute-start | bytes 1474568 | tf_op jit(solution)/shard_map/ppermute | solution.py:69
  80.4 3.6 %collective-permute-start.21 = (bf16[4,240,128]{2,1,0:T(8,128)(2,1)S(1)}, bf16[4,240,128]{2,1,0:T(8,128)(2,1)S(1)}, u32[]{:S(2)}, u32[]{:S(2)}) collective-permute-start(bf16[4,240,128]{2,1,0:T(8,128)(2,1)S(1)} %get-tuple-element.92), channel_id=1, source_target_pairs={{0,64},{1,65},{2,66},{3,67},{4,68},{5,69},{6,70},{7,71},{8,72},{9,... | collective-permute-start | bytes 737288 | tf_op jit(solution)/shard_map/ppermute | solution.py:69
  85.6 3.7 %collective-permute-done.15.t3 = bf16[4,480,128]{2,1,0:T(8,128)(2,1)S(1)} collective-permute-done((bf16[4,480,128]{2,1,0:T(8,128)(2,1)S(1)}, bf16[4,480,128]{2,1,0:T(8,128)(2,1)S(1)}, u32[]{:S(2)}, u32[]{:S(2)}) %collective-permute-start.15) | collective-permute-done | bytes 491552 | tf_op jit(solution)/shard_map/ppermute | solution.py:69
  94.4 3.4 %collective-permute-start.17 = (bf16[480,128]{1,0:T(8,128)(2,1)S(1)}, bf16[480,128]{1,0:T(8,128)(2,1)S(1)}, u32[]{:S(2)}, u32[]{:S(2)}) collective-permute-start(bf16[480,128]{1,0:T(8,128)(2,1)S(1)} %get-tuple-element.84), channel_id=1, source_target_pairs={{0,64},{1,5},{2,66},{3,7},{4,68},{5,1},{6,70},{7,3},{8,72},{9,13},... | collective-permute-start | bytes 368648 | tf_op jit(solution)/shard_map/ppermute | solution.py:69
  98.9 3.4 %collective-permute-start.24 = (bf16[240,128]{1,0:T(8,128)(2,1)S(1)}, bf16[240,128]{1,0:T(8,128)(2,1)S(1)}, u32[]{:S(2)}, u32[]{:S(2)}) collective-permute-start(bf16[240,128]{1,0:T(8,128)(2,1)S(1)} %get-tuple-element.96), channel_id=1, source_target_pairs={{0,16},{1,17},{2,18},{3,19},{4,20},{5,21},{6,22},{7,23},{8,24},{9,... | collective-permute-start | bytes 184328 | tf_op jit(solution)/shard_map/ppermute | solution.py:69
  114.0 3.5 %collective-permute-done.27.g1 = f32[384,128]{1,0:T(8,128)S(1)} collective-permute-done((f32[384,128]{1,0:T(8,128)S(1)}, f32[384,128]{1,0:T(8,128)S(1)}, u32[]{:S(2)}, u32[]{:S(2)}) %collective-permute-start.27) | collective-permute-done | bytes 196640 | tf_op jit(solution)/shard_map/ppermute | solution.py:69
  117.5 2.5 %collective-permute-done.28.g2 = f32[384,128]{1,0:T(8,128)S(1)} collective-permute-done((f32[384,128]{1,0:T(8,128)S(1)}, f32[384,128]{1,0:T(8,128)S(1)}, u32[]{:S(2)}, u32[]{:S(2)}) %collective-permute-start.28) | collective-permute-done | bytes 196640 | tf_op jit(solution)/shard_map/ppermute | solution.py:69
  120.0 3.0 %collective-permute-done.29.g3 = f32[384,128]{1,0:T(8,128)S(1)} collective-permute-done((f32[384,128]{1,0:T(8,128)S(1)}, f32[384,128]{1,0:T(8,128)S(1)}, u32[]{:S(2)}, u32[]{:S(2)}) %collective-permute-start.29) | collective-permute-done | bytes 196640 | tf_op jit(solution)/shard_map/ppermute | solution.py:69
  123.0 7.1 %newton_schulz_polynomial.1.own = f32[512,128]{1,0:T(8,128)S(1)} custom-call(f32[384,128]{1,0:T(8,128)S(1)} %select_add_fusion.g0, f32[384,128]{1,0:T(8,128)S(1)} %collective-permute-done.27.g1, f32[384,128]{1,0:T(8,128)S(1)} %collective-permute-done.28.g2, f32[384,128]{1,0:T(8,128)S(1)} %collective-permute-done.29.g3), custom_call_target="tpu_custom_call" | custom-call | tf_op jit(solution)/shard_map/newton_schulz_polynomial/pallas_call | solution.py:503
  136.1 2.4 %collective-permute-done.34 = bf16[704,128]{1,0:T(8,128)(2,1)S(1)} collective-permute-done((bf16[704,128]{1,0:T(8,128)(2,1)S(1)}, bf16[704,128]{1,0:T(8,128)(2,1)S(1)}, u32[]{:S(2)}, u32[]{:S(2)}) %collective-permute-start.34) | collective-permute-done | bytes 180256 | tf_op jit(solution)/shard_map/ppermute | solution.py:69
  139.9 2.2 %collective-permute-done.33 = bf16[704,128]{1,0:T(8,128)(2,1)S(1)} collective-permute-done((bf16[704,128]{1,0:T(8,128)(2,1)S(1)}, bf16[704,128]{1,0:T(8,128)(2,1)S(1)}, u32[]{:S(2)}, u32[]{:S(2)}) %collective-permute-start.33) | collective-permute-done | bytes 180256 | tf_op jit(solution)/shard_map/ppermute | solution.py:69
  142.8 3.5 %collective-permute-start.36 = (bf16[4,704,128]{2,1,0:T(8,128)(2,1)S(1)}, bf16[4,704,128]{2,1,0:T(8,128)(2,1)S(1)}, u32[]{:S(2)}, u32[]{:S(2)}) collective-permute-start(bf16[4,704,128]{2,1,0:T(8,128)(2,1)S(1)} %pad_maximum_fusion.s0), channel_id=1, source_target_pairs={{0,16},{1,65},{2,18},{3,67},{4,20},{5,69},{6,22},{7,71},{8,24},{9,... | collective-permute-start | bytes 2162696 | tf_op jit(solution)/shard_map/ppermute | solution.py:69
  146.4 8.4 %collective-permute-done.35.s1 = bf16[4,704,128]{2,1,0:T(8,128)(2,1)S(1)} collective-permute-done((bf16[4,704,128]{2,1,0:T(8,128)(2,1)S(1)}, bf16[4,704,128]{2,1,0:T(8,128)(2,1)S(1)}, u32[]{:S(2)}, u32[]{:S(2)}) %collective-permute-start.35) | collective-permute-done | bytes 720928 | tf_op jit(solution)/shard_map/ppermute | solution.py:69
  154.8 8.5 %collective-permute-done.36.s2 = bf16[4,704,128]{2,1,0:T(8,128)(2,1)S(1)} collective-permute-done((bf16[4,704,128]{2,1,0:T(8,128)(2,1)S(1)}, bf16[4,704,128]{2,1,0:T(8,128)(2,1)S(1)}, u32[]{:S(2)}, u32[]{:S(2)}) %collective-permute-start.36) | collective-permute-done | bytes 720928 | tf_op jit(solution)/shard_map/ppermute | solution.py:69
  163.4 2.9 %assemble.1 = (bf16[192,6144]{1,0:T(8,128)(2,1)}, bf16[64,4096]{1,0:T(8,128)(2,1)}) custom-call(s32[4]{0:T(128)S(1)} %pad_add_fusion.where, bf16[4,704,128]{2,1,0:T(8,128)(2,1)S(1)} %pad_maximum_fusion.s0, bf16[4,704,128]{2,1,0:T(8,128)(2,1)S(1)} %collective-permute-done.35.s1, bf16[4,704,128]{2,1,0:T(8,128)(2,1)S(1)} %collective-permute-done.36.s2, ...), custom_call_target="tpu_custom_call" | custom-call | tf_op jit(solution)/shard_map/assemble/pallas_call | solution.py:596
  (84 shorter events, 46.7 us)
Async XLA Ops:
  6.2 15.0 %collective-permute-start = (bf16[4,4,720,128]{3,2,1,0:T(8,128)(2,1)S(1)}, bf16[4,4,720,128]{3,2,1,0:T(8,128)(2,1)S(1)}, u32[]{:S(2)}, u32[]{:S(2)}) collective-permute-start(bf16[4,4,720,128]{3,2,1,0:T(8,128)(2,1)S(1)} %slice_other_2.1), channel_id=1, source_target_pairs={{0,1},{1,0},{2,3},{3,2},{4,5},{5,4},{6,7},{7,6},{8,9},{9,8},{10,11... | collective-permute-start | bytes 8847368 | tf_op jit(solution)/shard_map/ppermute | solution.py:74
  16.2 26.2 %collective-permute-start.7 = (bf16[4,4,720,128]{3,2,1,0:T(8,128)(2,1)}, bf16[4,4,720,128]{3,2,1,0:T(8,128)(2,1)}, u32[]{:S(2)}, u32[]{:S(2)}) collective-permute-start(bf16[4,4,720,128]{3,2,1,0:T(8,128)(2,1)} %slice_other_3.1), channel_id=1, source_target_pairs={{0,1},{1,0},{2,3},{3,2},{4,5},{5,4},{6,7},{7,6},{8,9},{9,8},{10,11... | collective-permute-start | bytes 8847368 | tf_op jit(solution)/shard_map/ppermute | solution.py:74
  16.4 15.3 %collective-permute-start.3 = (bf16[4,4,240,128]{3,2,1,0:T(8,128)(2,1)S(1)}, bf16[4,4,240,128]{3,2,1,0:T(8,128)(2,1)S(1)}, u32[]{:S(2)}, u32[]{:S(2)}) collective-permute-start(bf16[4,4,240,128]{3,2,1,0:T(8,128)(2,1)S(1)} %get-tuple-element.62), channel_id=1, source_target_pairs={{0,8},{1,33},{2,10},{3,35},{4,12},{5,37},{6,14},{7,39},{8,16},{9,4... | collective-permute-start | bytes 2949128 | tf_op jit(solution)/shard_map/ppermute | solution.py:69
  17.9 14.1 %collective-permute-start.4 = (bf16[4,4,240,128]{3,2,1,0:T(8,128)(2,1)S(1)}, bf16[4,4,240,128]{3,2,1,0:T(8,128)(2,1)S(1)}, u32[]{:S(2)}, u32[]{:S(2)}) collective-permute-start(bf16[4,4,240,128]{3,2,1,0:T(8,128)(2,1)S(1)} %get-tuple-element.63), channel_id=1, source_target_pairs={{0,24},{1,97},{2,26},{3,99},{4,28},{5,101},{6,30},{7,103},{8,0},{9... | collective-permute-start | bytes 2949128 | tf_op jit(solution)/shard_map/ppermute | solution.py:69
  19.6 14.1 %collective-permute-start.5 = (bf16[4,4,240,128]{3,2,1,0:T(8,128)(2,1)S(1)}, bf16[4,4,240,128]{3,2,1,0:T(8,128)(2,1)S(1)}, u32[]{:S(2)}, u32[]{:S(2)}) collective-permute-start(bf16[4,4,240,128]{3,2,1,0:T(8,128)(2,1)S(1)} %get-tuple-element.64), channel_id=1, source_target_pairs={{0,2},{1,7},{2,4},{3,1},{4,6},{5,3},{6,0},{7,5},{8,10},{9,15},{10,... | collective-permute-start | bytes 2949128 | tf_op jit(solution)/shard_map/ppermute | solution.py:69
  28.4 32.4 %collective-permute-start.1 = (bf16[4,4,720,128]{3,2,1,0:T(8,128)(2,1)}, bf16[4,4,720,128]{3,2,1,0:T(8,128)(2,1)S(1)}, u32[]{:S(2)}, u32[]{:S(2)}) collective-permute-start(bf16[4,4,720,128]{3,2,1,0:T(8,128)(2,1)} %slice_other_4.1), channel_id=1, source_target_pairs={{0,1},{1,0},{2,3},{3,2},{4,5},{5,4},{6,7},{7,6},{8,9},{9,8},{10,11... | collective-permute-start | bytes 8847368 | tf_op jit(solution)/shard_map/ppermute | solution.py:74
  36.3 14.4 %collective-permute-start.10 = (bf16[4,4,240,128]{3,2,1,0:T(8,128)(2,1)}, bf16[4,4,240,128]{3,2,1,0:T(8,128)(2,1)}, u32[]{:S(2)}, u32[]{:S(2)}) collective-permute-start(bf16[4,4,240,128]{3,2,1,0:T(8,128)(2,1)} %get-tuple-element.72), channel_id=1, source_target_pairs={{0,2},{1,7},{2,4},{3,1},{4,6},{5,3},{6,0},{7,5},{8,10},{9,15},{10,... | collective-permute-start | bytes 2949128 | tf_op jit(solution)/shard_map/ppermute | solution.py:69
  37.9 15.6 %collective-permute-start.8 = (bf16[4,4,240,128]{3,2,1,0:T(8,128)(2,1)}, bf16[4,4,240,128]{3,2,1,0:T(8,128)(2,1)}, u32[]{:S(2)}, u32[]{:S(2)}) collective-permute-start(bf16[4,4,240,128]{3,2,1,0:T(8,128)(2,1)} %get-tuple-element.65), channel_id=1, source_target_pairs={{0,8},{1,33},{2,10},{3,35},{4,12},{5,37},{6,14},{7,39},{8,16},{9,4... | collective-permute-start | bytes 2949128 | tf_op jit(solution)/shard_map/ppermute | solution.py:69
  38.1 15.3 %collective-permute-start.9 = (bf16[4,4,240,128]{3,2,1,0:T(8,128)(2,1)}, bf16[4,4,240,128]{3,2,1,0:T(8,128)(2,1)}, u32[]{:S(2)}, u32[]{:S(2)}) collective-permute-start(bf16[4,4,240,128]{3,2,1,0:T(8,128)(2,1)} %get-tuple-element.71), channel_id=1, source_target_pairs={{0,24},{1,97},{2,26},{3,99},{4,28},{5,101},{6,30},{7,103},{8,0},{9... | collective-permute-start | bytes 2949128 | tf_op jit(solution)/shard_map/ppermute | solution.py:69
  42.4 13.8 %collective-permute-start.6 = (f32[80,384]{1,0:T(8,128)S(1)}, f32[80,384]{1,0:T(8,128)S(1)}, u32[]{:S(2)}, u32[]{:S(2)}) collective-permute-start(f32[80,384]{1,0:T(8,128)S(1)} %constant_dynamic-slice_fusion.1), channel_id=1, source_target_pairs={{0,1},{1,0},{2,3},{3,2},{4,5},{5,4},{6,7},{7,6},{8,9},{9,8},{10,11... | collective-permute-start | bytes 368648 | tf_op jit(solution)/shard_map/ppermute | solution.py:74
  56.1 15.4 %collective-permute-start.11 = (bf16[4,4,240,128]{3,2,1,0:T(8,128)(2,1)S(1)}, bf16[4,4,240,128]{3,2,1,0:T(8,128)(2,1)S(1)}, u32[]{:S(2)}, u32[]{:S(2)}) collective-permute-start(bf16[4,4,240,128]{3,2,1,0:T(8,128)(2,1)S(1)} %get-tuple-element.76), channel_id=1, source_target_pairs={{0,8},{1,33},{2,10},{3,35},{4,12},{5,37},{6,14},{7,39},{8,16},{9,4... | collective-permute-start | bytes 2949128 | tf_op jit(solution)/shard_map/ppermute | solution.py:69
  56.8 14.8 %collective-permute-start.12 = (bf16[4,4,240,128]{3,2,1,0:T(8,128)(2,1)S(1)}, bf16[4,4,240,128]{3,2,1,0:T(8,128)(2,1)S(1)}, u32[]{:S(2)}, u32[]{:S(2)}) collective-permute-start(bf16[4,4,240,128]{3,2,1,0:T(8,128)(2,1)S(1)} %get-tuple-element.77), channel_id=1, source_target_pairs={{0,24},{1,97},{2,26},{3,99},{4,28},{5,101},{6,30},{7,103},{8,0},{9... | collective-permute-start | bytes 2949128 | tf_op jit(solution)/shard_map/ppermute | solution.py:69
  59.5 17.9 %collective-permute-start.19 = (bf16[4,4,240,128]{3,2,1,0:T(8,128)(2,1)S(1)}, bf16[4,4,240,128]{3,2,1,0:T(8,128)(2,1)S(1)}, u32[]{:S(2)}, u32[]{:S(2)}) collective-permute-start(bf16[4,4,240,128]{3,2,1,0:T(8,128)(2,1)S(1)} %get-tuple-element.89), channel_id=1, source_target_pairs={{0,2},{1,7},{2,4},{3,1},{4,6},{5,3},{6,0},{7,5},{8,10},{9,15},{10,... | collective-permute-start | bytes 2949128 | tf_op jit(solution)/shard_map/ppermute | solution.py:69
  72.6 11.3 %collective-permute-start.13 = (bf16[4,480,128]{2,1,0:T(8,128)(2,1)S(1)}, bf16[4,480,128]{2,1,0:T(8,128)(2,1)S(1)}, u32[]{:S(2)}, u32[]{:S(2)}) collective-permute-start(bf16[4,480,128]{2,1,0:T(8,128)(2,1)S(1)} %get-tuple-element.79), channel_id=1, source_target_pairs={{0,2},{1,9},{2,4},{3,11},{4,6},{5,13},{6,0},{7,15},{8,10},{9,17},{... | collective-permute-start | bytes 1474568 | tf_op jit(solution)/shard_map/ppermute | solution.py:69
  74.0 11.6 %collective-permute-start.14 = (bf16[4,480,128]{2,1,0:T(8,128)(2,1)S(1)}, bf16[4,480,128]{2,1,0:T(8,128)(2,1)S(1)}, u32[]{:S(2)}, u32[]{:S(2)}) collective-permute-start(bf16[4,480,128]{2,1,0:T(8,128)(2,1)S(1)} %get-tuple-element.80), channel_id=1, source_target_pairs={{0,4},{1,17},{2,6},{3,19},{4,0},{5,21},{6,2},{7,23},{8,12},{9,25},... | collective-permute-start | bytes 1474568 | tf_op jit(solution)/shard_map/ppermute | solution.py:69
  75.2 14.1 %collective-permute-start.15 = (bf16[4,480,128]{2,1,0:T(8,128)(2,1)S(1)}, bf16[4,480,128]{2,1,0:T(8,128)(2,1)S(1)}, u32[]{:S(2)}, u32[]{:S(2)}) collective-permute-start(bf16[4,480,128]{2,1,0:T(8,128)(2,1)S(1)} %get-tuple-element.81), channel_id=1, source_target_pairs={{0,6},{1,25},{2,0},{3,27},{4,2},{5,29},{6,4},{7,31},{8,14},{9,1},{... | collective-permute-start | bytes 1474568 | tf_op jit(solution)/shard_map/ppermute | solution.py:69
  78.3 11.8 %collective-permute-start.20 = (bf16[4,240,128]{2,1,0:T(8,128)(2,1)S(1)}, bf16[4,240,128]{2,1,0:T(8,128)(2,1)S(1)}, u32[]{:S(2)}, u32[]{:S(2)}) collective-permute-start(bf16[4,240,128]{2,1,0:T(8,128)(2,1)S(1)} %get-tuple-element.91), channel_id=1, source_target_pairs={{0,32},{1,33},{2,34},{3,35},{4,36},{5,37},{6,38},{7,39},{8,40},{9,... | collective-permute-start | bytes 737288 | tf_op jit(solution)/shard_map/ppermute | solution.py:69
  80.4 10.6 %collective-permute-start.21 = (bf16[4,240,128]{2,1,0:T(8,128)(2,1)S(1)}, bf16[4,240,128]{2,1,0:T(8,128)(2,1)S(1)}, u32[]{:S(2)}, u32[]{:S(2)}) collective-permute-start(bf16[4,240,128]{2,1,0:T(8,128)(2,1)S(1)} %get-tuple-element.92), channel_id=1, source_target_pairs={{0,64},{1,65},{2,66},{3,67},{4,68},{5,69},{6,70},{7,71},{8,72},{9,... | collective-permute-start | bytes 737288 | tf_op jit(solution)/shard_map/ppermute | solution.py:69
  83.9 7.0 %collective-permute-start.22 = (bf16[4,240,128]{2,1,0:T(8,128)(2,1)S(1)}, bf16[4,240,128]{2,1,0:T(8,128)(2,1)S(1)}, u32[]{:S(2)}, u32[]{:S(2)}) collective-permute-start(bf16[4,240,128]{2,1,0:T(8,128)(2,1)S(1)} %get-tuple-element.93), channel_id=1, source_target_pairs={{0,96},{1,97},{2,98},{3,99},{4,100},{5,101},{6,102},{7,103},{8,104... | collective-permute-start | bytes 737288 | tf_op jit(solution)/shard_map/ppermute | solution.py:69
  91.6 10.6 %collective-permute-start.23 = (bf16[240,128]{1,0:T(8,128)(2,1)S(1)}, bf16[240,128]{1,0:T(8,128)(2,1)S(1)}, u32[]{:S(2)}, u32[]{:S(2)}) collective-permute-start(bf16[240,128]{1,0:T(8,128)(2,1)S(1)} %get-tuple-element.95), channel_id=1, source_target_pairs={{0,8},{1,9},{2,10},{3,11},{4,12},{5,13},{6,14},{7,15},{8,16},{9,17... | collective-permute-start | bytes 184328 | tf_op jit(solution)/shard_map/ppermute | solution.py:69
  92.9 13.5 %collective-permute-start.16 = (bf16[480,128]{1,0:T(8,128)(2,1)S(1)}, bf16[480,128]{1,0:T(8,128)(2,1)S(1)}, u32[]{:S(2)}, u32[]{:S(2)}) collective-permute-start(bf16[480,128]{1,0:T(8,128)(2,1)S(1)} %get-tuple-element.83), channel_id=1, source_target_pairs={{0,32},{1,3},{2,34},{3,5},{4,36},{5,7},{6,38},{7,1},{8,40},{9,11},... | collective-permute-start | bytes 368648 | tf_op jit(solution)/shard_map/ppermute | solution.py:69
  94.4 12.0 %collective-permute-start.17 = (bf16[480,128]{1,0:T(8,128)(2,1)S(1)}, bf16[480,128]{1,0:T(8,128)(2,1)S(1)}, u32[]{:S(2)}, u32[]{:S(2)}) collective-permute-start(bf16[480,128]{1,0:T(8,128)(2,1)S(1)} %get-tuple-element.84), channel_id=1, source_target_pairs={{0,64},{1,5},{2,66},{3,7},{4,68},{5,1},{6,70},{7,3},{8,72},{9,13},... | collective-permute-start | bytes 368648 | tf_op jit(solution)/shard_map/ppermute | solution.py:69
  97.8 8.6 %collective-permute-start.18 = (bf16[480,128]{1,0:T(8,128)(2,1)S(1)}, bf16[480,128]{1,0:T(8,128)(2,1)S(1)}, u32[]{:S(2)}, u32[]{:S(2)}) collective-permute-start(bf16[480,128]{1,0:T(8,128)(2,1)S(1)} %get-tuple-element.85), channel_id=1, source_target_pairs={{0,96},{1,7},{2,98},{3,1},{4,100},{5,3},{6,102},{7,5},{8,104},{9,1... | collective-permute-start | bytes 368648 | tf_op jit(solution)/shard_map/ppermute | solution.py:69
  109.7 7.8 %collective-permute-start.27 = (f32[384,128]{1,0:T(8,128)S(1)}, f32[384,128]{1,0:T(8,128)S(1)}, u32[]{:S(2)}, u32[]{:S(2)}) collective-permute-start(f32[384,128]{1,0:T(8,128)S(1)} %select_add_fusion.g0), channel_id=1, source_target_pairs={{0,2},{1,3},{2,4},{3,5},{4,6},{5,7},{6,0},{7,1},{8,10},{9,11},{10,... | collective-permute-start | bytes 589832 | tf_op jit(solution)/shard_map/ppermute | solution.py:69
  110.6 9.3 %collective-permute-start.28 = (f32[384,128]{1,0:T(8,128)S(1)}, f32[384,128]{1,0:T(8,128)S(1)}, u32[]{:S(2)}, u32[]{:S(2)}) collective-permute-start(f32[384,128]{1,0:T(8,128)S(1)} %select_add_fusion.g0), channel_id=1, source_target_pairs={{0,4},{1,5},{2,6},{3,7},{4,0},{5,1},{6,2},{7,3},{8,12},{9,13},{10,... | collective-permute-start | bytes 589832 | tf_op jit(solution)/shard_map/ppermute | solution.py:69
  112.6 10.4 %collective-permute-start.29 = (f32[384,128]{1,0:T(8,128)S(1)}, f32[384,128]{1,0:T(8,128)S(1)}, u32[]{:S(2)}, u32[]{:S(2)}) collective-permute-start(f32[384,128]{1,0:T(8,128)S(1)} %select_add_fusion.g0), channel_id=1, source_target_pairs={{0,6},{1,7},{2,0},{3,1},{4,2},{5,3},{6,4},{7,5},{8,14},{9,15},{10,... | collective-permute-start | bytes 589832 | tf_op jit(solution)/shard_map/ppermute | solution.py:69
  113.9 16.3 %collective-permute-start.31 = (f32[80,384]{1,0:T(8,128)S(1)}, f32[80,384]{1,0:T(8,128)S(1)}, u32[]{:S(2)}, u32[]{:S(2)}) collective-permute-start(f32[80,384]{1,0:T(8,128)S(1)} %constant_dynamic-slice_fusion), channel_id=1, source_target_pairs={{0,1},{1,0},{2,3},{3,2},{4,5},{5,4},{6,7},{7,6},{8,9},{9,8},{10,11... | collective-permute-start | bytes 368648 | tf_op jit(solution)/shard_map/ppermute | solution.py:74
  133.1 6.8 %collective-permute-start.32 = (bf16[704,128]{1,0:T(8,128)(2,1)S(1)}, bf16[704,128]{1,0:T(8,128)(2,1)S(1)}, u32[]{:S(2)}, u32[]{:S(2)}) collective-permute-start(bf16[704,128]{1,0:T(8,128)(2,1)S(1)} %update.1), channel_id=1, source_target_pairs={{0,32},{1,9},{2,34},{3,11},{4,36},{5,13},{6,38},{7,15},{8,40},{9,1... | collective-permute-start | bytes 540680 | tf_op jit(solution)/shard_map/ppermute | solution.py:69
  135.1 7.0 %collective-permute-start.33 = (bf16[704,128]{1,0:T(8,128)(2,1)S(1)}, bf16[704,128]{1,0:T(8,128)(2,1)S(1)}, u32[]{:S(2)}, u32[]{:S(2)}) collective-permute-start(bf16[704,128]{1,0:T(8,128)(2,1)S(1)} %update.1), channel_id=1, source_target_pairs={{0,64},{1,17},{2,66},{3,19},{4,68},{5,21},{6,70},{7,23},{8,72},{9,... | collective-permute-start | bytes 540680 | tf_op jit(solution)/shard_map/ppermute | solution.py:69
  142.2 12.6 %collective-permute-start.35 = (bf16[4,704,128]{2,1,0:T(8,128)(2,1)S(1)}, bf16[4,704,128]{2,1,0:T(8,128)(2,1)S(1)}, u32[]{:S(2)}, u32[]{:S(2)}) collective-permute-start(bf16[4,704,128]{2,1,0:T(8,128)(2,1)S(1)} %pad_maximum_fusion.s0), channel_id=1, source_target_pairs={{0,8},{1,33},{2,10},{3,35},{4,12},{5,37},{6,14},{7,39},{8,16},{9,4... | collective-permute-start | bytes 2162696 | tf_op jit(solution)/shard_map/ppermute | solution.py:69
  142.8 20.5 %collective-permute-start.36 = (bf16[4,704,128]{2,1,0:T(8,128)(2,1)S(1)}, bf16[4,704,128]{2,1,0:T(8,128)(2,1)S(1)}, u32[]{:S(2)}, u32[]{:S(2)}) collective-permute-start(bf16[4,704,128]{2,1,0:T(8,128)(2,1)S(1)} %pad_maximum_fusion.s0), channel_id=1, source_target_pairs={{0,16},{1,65},{2,18},{3,67},{4,20},{5,69},{6,22},{7,71},{8,24},{9,... | collective-permute-start | bytes 2162696 | tf_op jit(solution)/shard_map/ppermute | solution.py:69
  146.3 17.1 %collective-permute-start.37 = (bf16[4,704,128]{2,1,0:T(8,128)(2,1)S(1)}, bf16[4,704,128]{2,1,0:T(8,128)(2,1)S(1)}, u32[]{:S(2)}, u32[]{:S(2)}) collective-permute-start(bf16[4,704,128]{2,1,0:T(8,128)(2,1)S(1)} %pad_maximum_fusion.s0), channel_id=1, source_target_pairs={{0,24},{1,97},{2,26},{3,99},{4,28},{5,101},{6,30},{7,103},{8,0},{9... | collective-permute-start | bytes 2162696 | tf_op jit(solution)/shard_map/ppermute | solution.py:69
  (12 other events, 207.8 us)

commit v3 on v2

--- a/solution.py
+++ b/solution.py
@@ -32,6 +32,7 @@
 MC = RC * 3 + KR * 2
 ML = 16
 M_ALL = 2 * MP + MC
+M_HALF = M_ALL // 2
 G_ROWS = 384
 
 f32, bf16 = jnp.float32, jnp.bfloat16
@@ -149,46 +150,6 @@
     return jnp.where(row == 0, high, jnp.where(row == 1, middle, jnp.where(row == 2, low, 0.0)))
 
 
-def slice_kernel(step, where, query, key, logits, to, *scratch):
-    scratch, lanes = scratch[:-1], scratch[-1]
-    blocks, c_query, c_key, own_logits, _ = scratch
-    core, main, rest = slice_copies(where, True, step, query, key, logits, scratch)
-    for copy in rest + main:
-        copy.start()
-    lanes[...] = jnp.zeros_like(lanes)
-    for copy in rest:
-        copy.wait()
-    lanes[pl.ds(0, 1), pl.ds(0, 32)] = own_logits[...]
-    logit_block = logit_rows(lanes[pl.ds(0, 1), :]).astype(bf16)
-
-    @pl.loop(0, N * N)
-    def _(i):
-        at = (i // N, i % N)
-        to[at + (pl.ds(M_ALL, ML),)] = logit_block
-        for source, height, width, start, size in (
-            (c_query, RC, 3, 0, QC),
-            (c_key, KR, 2, 3 * RC, KC),
-        ):
-            for lane in range(width):
-                to[at + (pl.ds(2 * MP + start + lane * height, height),)] = source[
-                    :, columns(at[0], at[1], size, lane)
-                ]
-
-    for i in range(N):
-        main[2 * i].wait()
-        main[2 * i + 1].wait()
-
-        @pl.loop(0, N)
-        def _(j):
-            first, second = jnp.where(core == 0, j, i), jnp.where(core == 0, i, j)
-            for owner in range(2):
-                block = blocks[owner, i, j]
-                for lane in range(3):
-                    to[first, second, pl.ds(owner * MP + lane * RP, RP), :] = block[
-                        :, lane * 128 : (lane + 1) * 128
-                    ]
-
-
 def slice_scratch():
     return [
         pltpu.VMEM((2, N, N, RP, QC), bf16),
@@ -196,8 +157,10 @@
         pltpu.VMEM((KR, N * N * KC), bf16),
         pltpu.VMEM((1, 32), f32),
         pltpu.SemaphoreType.DMA((2 * N + 5,)),
-        pltpu.VMEM((8, 128), f32),
     ]
+
+
+N_SCRATCH = 5
 
 
 def in_hbm(*arrays):
@@ -206,18 +169,6 @@
 
 def in_hbm(*arrays):
     return tuple(pltpu.with_memory_space_constraint(a, pltpu.HBM) for a in arrays)
-
-
-def slice_other(step, where, query, key, logits):
-    return pl.pallas_call(
-        functools.partial(slice_kernel, step),
-        out_shape=out((N, N, M_ALL + ML, 128), bf16),
-        in_specs=[SMEM, HBM, HBM, HBM],
-        out_specs=VMEM,
-        scratch_shapes=slice_scratch(),
-        compiler_params=params(8),
-        name=f"slice_other_{step}",
-    )(where, *in_hbm(query, key, logits))
 
 
 def total(*terms):
@@ -234,33 +185,26 @@
     return logit_rows(value)
 
 
-def pre_kernel(step, where, query, key, logits, other, p, m, c, *scratch):
-    scratch, lanes = scratch[:-1], scratch[-1]
-    blocks, c_query, c_key, own_logits, _ = scratch
-    core, main, rest = slice_copies(where, False, step, query, key, logits, scratch)
-    for copy in rest + main:
-        copy.start()
-    lanes[...] = jnp.zeros_like(lanes)
+C_PIECES = ((0, RC, 3, 0, QC), (1, KR, 2, 3 * RC, KC))
+
+
+def sum_blocks(work, other, lanes, p, m, c):
+    (core, main, rest), (blocks, c_query, c_key, own_logits, _) = work
     for copy in rest:
         copy.wait()
     lanes[pl.ds(0, 1), pl.ds(0, 32)] = own_logits[...]
-    peak = jnp.maximum(
-        lanes[pl.ds(0, 1), :], join_logits(other[0, 0, pl.ds(M_ALL, ML), :])
-    )
+    peak = jnp.maximum(lanes[pl.ds(0, 1), :], join_logits(other[0, 0, pl.ds(M_ALL, ML), :]))
     logit_block = logit_rows(peak).astype(bf16)
 
     @pl.loop(0, N * N)
     def _(i):
         at = (i // N, i % N)
         c[at + (pl.ds(MC, ML),)] = logit_block
-        for source, height, width, start, size in (
-            (c_query, RC, 3, 0, QC),
-            (c_key, KR, 2, 3 * RC, KC),
-        ):
+        for source, height, width, start, size in C_PIECES:
             for lane in range(width):
                 rows = start + lane * height
                 c[at + (pl.ds(rows, height),)] = total(
-                    source[:, columns(at[0], at[1], size, lane)],
+                    (c_query, c_key)[source][:, columns(at[0], at[1], size, lane)],
                     other[at + (pl.ds(2 * MP + rows, height),)],
                 ).astype(bf16)
 
@@ -280,40 +224,102 @@
                     ).astype(bf16)
 
 
-def pre_sum(step, where, query, key, logits, other):
-    return pl.pallas_call(
-        functools.partial(pre_kernel, step),
-        out_shape=[out((N, N, height, 128), bf16) for height in (MP, MP, MC + ML)],
-        in_specs=[SMEM, HBM, HBM, HBM, VMEM],
-        out_specs=[VMEM] * 3,
-        scratch_shapes=slice_scratch(),
-        compiler_params=params(12),
-        name=f"pre_sum_{step}",
-    )(where, *in_hbm(query, key, logits), other)
-
-
-def ring_add_kernel(p0, m0, c0, p1, m1, c1, p, m, c):
-    peak = most(c0[0, 0, pl.ds(MC, ML), :], c1[0, 0, pl.ds(MC, ML), :]).astype(bf16)
+def collect_blocks(work, lanes, to):
+    (core, main, rest), (blocks, c_query, c_key, own_logits, _) = work
+    for copy in rest:
+        copy.wait()
+    lanes[pl.ds(0, 1), pl.ds(0, 32)] = own_logits[...]
+    logit_block = logit_rows(lanes[pl.ds(0, 1), :]).astype(bf16)
 
     @pl.loop(0, N * N)
     def _(i):
         at = (i // N, i % N)
-        p[at] = total(p0[at], p1[at]).astype(bf16)
-        m[at] = total(m0[at], m1[at]).astype(bf16)
-        rows = at + (pl.ds(0, MC),)
-        c[rows] = total(c0[rows], c1[rows]).astype(bf16)
-        c[at + (pl.ds(MC, ML),)] = peak
-
-
-def ring_add(own, received):
-    return pl.pallas_call(
-        ring_add_kernel,
-        out_shape=[out(a.shape, bf16) for a in own],
-        in_specs=[VMEM] * 6,
-        out_specs=[VMEM] * 3,
-        compiler_params=params(14),
-        name="ring_add",
-    )(*own, *received)
+        to[at + (pl.ds(M_ALL, ML),)] = logit_block
+        for source, height, width, start, size in C_PIECES:
+            for lane in range(width):
+                to[at + (pl.ds(2 * MP + start + lane * height, height),)] = (c_query, c_key)[
+                    source
+                ][:, columns(at[0], at[1], size, lane)]
+
+    for i in range(N):
+        main[2 * i].wait()
+        main[2 * i + 1].wait()
+
+        @pl.loop(0, N)
+        def _(j):
+            first, second = jnp.where(core == 0, j, i), jnp.where(core == 0, i, j)
+            for owner in range(2):
+                block = blocks[owner, i, j]
+                for lane in range(3):
+                    to[first, second, pl.ds(owner * MP + lane * RP, RP), :] = block[
+                        :, lane * 128 : (lane + 1) * 128
+                    ]
+
+
+def local_kernel(sum_step, send_step, where, query, key, logits, *refs):
+    refs = list(refs)
+    other = [refs.pop(0)] if sum_step else []
+    sums = [refs.pop(0) for _ in range(3)] if sum_step else []
+    to = [refs.pop(0)] if send_step else []
+    lanes = refs.pop()
+    works = []
+    for step, is_other in ((sum_step, False), (send_step, True)):
+        if step:
+            scratch, refs = refs[:N_SCRATCH], refs[N_SCRATCH:]
+            copies = slice_copies(where, is_other, step, query, key, logits, scratch)
+            for copy in copies[2] + copies[1]:
+                copy.start()
+            works.append((copies, scratch))
+    lanes[...] = jnp.zeros_like(lanes)
+    if sum_step:
+        sum_blocks(works[0], *other, lanes, *sums)
+    if send_step:
+        collect_blocks(works[-1], lanes, *to)
+
+
+def local(sum_step, send_step, where, query, key, logits, other=None):
+    shapes, scratch, inputs = [], [], list(in_hbm(query, key, logits))
+    if sum_step:
+        shapes += [out((N, N, height, 128), bf16) for height in (MP, MP, MC + ML)]
+        scratch += slice_scratch()
+        inputs.append(other)
+    if send_step:
+        shapes += [out((N, N, M_ALL + ML, 128), bf16)]
+        scratch += slice_scratch()
+    return pl.pallas_call(
+        functools.partial(local_kernel, sum_step, send_step),
+        out_shape=shapes,
+        in_specs=[SMEM, HBM, HBM, HBM] + [VMEM] * (1 if sum_step else 0),
+        out_specs=[VMEM] * len(shapes),
+        scratch_shapes=scratch + [pltpu.VMEM((8, 128), f32)],
+        compiler_params=params(15 if sum_step and send_step else 10 if sum_step else 7),
+        name=f"local_sum_{sum_step}_send_{send_step}",
+    )(where, *inputs)
+
+
+def add(first, second):
+    return (first.astype(f32) + second.astype(f32)).astype(bf16)
+
+
+def add_c_kernel(first, second, to):
+    peak = most(first[0, 0, pl.ds(MC, ML), :], second[0, 0, pl.ds(MC, ML), :]).astype(bf16)
+
+    @pl.loop(0, N * N)
+    def _(i):
+        rows = (i // N, i % N, pl.ds(0, MC))
+        to[rows] = total(first[rows], second[rows]).astype(bf16)
+        to[i // N, i % N, pl.ds(MC, ML), :] = peak
+
+
+def add_c(first, second):
+    return pl.pallas_call(
+        add_c_kernel,
+        out_shape=out((N, N, MC + ML, 128), bf16),
+        in_specs=[VMEM, VMEM],
+        out_specs=VMEM,
+        compiler_params=params(6),
+        name="add_c",
+    )(first, second)
 
 
 def split_ab_kernel(where, p0, m0, p1, m1, *outs):
@@ -453,6 +459,20 @@
     )(where, *part, *part_c, query_moment, theirs, key_moment)
 
 
+def three_products(left, right):
+    def halves(value):
+        high = value.astype(bf16)
+        return high, (value - high.astype(f32)).astype(bf16)
+
+    def product(first, second):
+        return jnp.dot(first, second, preferred_element_type=f32)
+
+    (left_high, left_low), (right_high, right_low) = halves(left), halves(right)
+    return product(left_high, right_high) + (
+        product(left_high, right_low) + product(left_low, right_high)
+    )
+
+
 def chain_kernel(g0, g1, g2, g3, to):
     packed = g0[...] + g1[...] + g2[...] + g3[...]
     top, side, corner = packed[:128], packed[128:192], packed[192:256]
@@ -472,8 +492,10 @@
     query_eye = jnp.where((row == column) & (row < QH), 1.0, 0.0).astype(f32)
     key_eye = jnp.where(row == column, 1.0, 0.0).astype(f32)[:128, :128]
 
-    def product(left, right):
-        return jnp.dot(left, right, precision=HIGHEST, preferred_element_type=f32)
+    def product(left, right, exact):
+        if exact:
+            return jnp.dot(left, right, precision=HIGHEST, preferred_element_type=f32)
+        return three_products(left, right)
 
     def start(gram, eye):
         square = jnp.sum(jnp.sum(gram * eye, axis=1, keepdims=True), axis=0, keepdims=True)
@@ -483,16 +505,17 @@
     grams, inverses = zip(start(query_gram, query_eye), start(key_gram, key_eye))
     grams, eyes, totals = list(grams), (query_eye, key_eye), [None, None]
     for iteration in range(ITERS):
+        exact = iteration < 2
         mixers = []
         for i in range(2):
-            square = product(grams[i], grams[i])
+            square = product(grams[i], grams[i], exact)
             mixers.append(coef_first * eyes[i] + coef_second * grams[i] + coef_third * square)
         if iteration < ITERS - 1:
-            halves = [product(mixers[i], grams[i]) for i in range(2)]
+            halves = [product(mixers[i], grams[i], exact) for i in range(2)]
         for i in range(2):
-            totals[i] = mixers[i] if iteration == 0 else product(totals[i], mixers[i])
+            totals[i] = mixers[i] if iteration == 0 else product(totals[i], mixers[i], exact)
         if iteration < ITERS - 1:
-            grams = [product(halves[i], mixers[i]) for i in range(2)]
+            grams = [product(halves[i], mixers[i], exact) for i in range(2)]
     query_total, key_total = (totals[i] * inverses[i] for i in range(2))
     to[pl.ds(0, 192), :] = query_total[:192, :128]
     to[pl.ds(192, 192), :] = query_total[:192, 128:]
@@ -514,9 +537,7 @@
     mine, theirs = own[...], other[...]
     packs = (jnp.where(core == 0, mine, theirs), jnp.where(core == 0, theirs, mine))
 
-    def product(left, right):
-        return jnp.dot(left, right, precision=HIGHEST, preferred_element_type=f32)
-
+    product = three_products
     gamma = jnp.minimum(1.0, clip_limit / peak[pl.ds(0, 1), :])
     lane = lax.broadcasted_iota(jnp.int32, (1, 128), 1)
     first_head = 2 * (z * N + x)
@@ -558,10 +579,12 @@
     key_next = key_weight - learn_rate * (key_scale * key_ortho + weight_decay * key_weight)
     query_block = (query_next * query_factor).astype(bf16)
     key_block = (key_next * key_factor).astype(bf16)
-    for lane in range(3):
-        to[pl.ds(lane * QR, QR), :] = query_block[:, lane * 128 : (lane + 1) * 128]
-    for lane in range(2):
-        to[pl.ds(3 * QR + lane * KR, KR), :] = key_block[:, lane * 128 : (lane + 1) * 128]
+    half = QR // 2
+    for i in range(2):
+        start = i * M_HALF
+        to[pl.ds(start, QR), :] = query_block[:, i * 128 : (i + 1) * 128]
+        to[pl.ds(start + QR, half), :] = query_block[i * half : (i + 1) * half, 256:]
+        to[pl.ds(start + QR + half, KR), :] = key_block[:, i * 128 : (i + 1) * 128]
 
 
 def update(where, own, other, peak, query_moment, key_moment, query_weight, key_weight):
@@ -575,32 +598,35 @@
     )(where, own, other, peak, query_moment, key_moment, query_weight, key_weight)
 
 
-def assemble_kernel(where, s0, s1, s2, s3, query_out, key_out):
+def assemble_kernel(where, *refs):
     z, x, _, core = read(where)
-    for far, stack in enumerate((s0, s1, s2, s3)):
+    stacks, (query_out, key_out) = (refs[:N], refs[N : 2 * N]), refs[2 * N :]
+    half = QR // 2
+    for far in range(N):
 
         @pl.loop(0, N)
         def _(near):
             back_z = jnp.where(core == 0, near, far)
             back_x = jnp.where(core == 0, far, near)
             zz, xx = (z + N - back_z) % N, (x + N - back_x) % N
-            for lane in range(3):
-                query_out[:, columns(zz, xx, QC, lane)] = stack[near, pl.ds(lane * QR, QR), :]
-            for lane in range(2):
-                key_out[:, columns(zz, xx, KC, lane)] = stack[
-                    near, pl.ds(3 * QR + lane * KR, KR), :
+            for i in range(2):
+                stack = stacks[i][far]
+                query_out[:, columns(zz, xx, QC, i)] = stack[near, pl.ds(0, QR), :]
+                query_out[pl.ds(i * half, half), columns(zz, xx, QC, 2)] = stack[
+                    near, pl.ds(QR, half), :
                 ]
-
-
-def assemble(where, stacks):
+                key_out[:, columns(zz, xx, KC, i)] = stack[near, pl.ds(QR + half, KR), :]
+
+
+def assemble(where, first, second):
     return pl.pallas_call(
         assemble_kernel,
         out_shape=(out((QR, N * N * QC), bf16), out((KR, N * N * KC), bf16)),
-        in_specs=[SMEM] + [VMEM] * N,
+        in_specs=[SMEM] + [VMEM] * (2 * N),
         out_specs=(VMEM, VMEM),
         compiler_params=params(16),
         name="assemble",
-    )(where, *stacks)
+    )(where, *first, *second)
 
 
 def on_device(grad_query, grad_key, query_weight, key_weight, query_moment, key_moment, max_logits):
@@ -613,28 +639,27 @@
     def after(value):
         return lax.optimization_barrier((where, value))[0]
 
-    first = slice_other(1, where, query, key, max_logits)
-    second = slice_other(2, after(first), query, key, max_logits)
-    others, pre = [swap(first), swap(second)], []
-    for step in range(1, N + 1):
-        pre.append(pre_sum(step, where, query, key, max_logits, others[step - 1]))
-        if step + 2 <= N:
-            blocks = slice_other(step + 2, after(pre[-1][2]), query, key, max_logits)
-            others.append(swap(blocks))
-
-    parts = pre[0]
+    others, token = [], where
     for step in range(1, N):
-        p, m, c = parts
+        (blocks,) = local(None, step, token, query, key, max_logits)
+        token = after(blocks)
+        others.append(swap(blocks))
+    pre = [local(1, None, where, query, key, max_logits, others[0])]
+    *sums, blocks = local(2, N, after(pre[0][0]), query, key, max_logits, others[1])
+    pre.append(sums)
+    others.append(swap(blocks))
+    for step in range(3, N + 1):
+        pre.append(local(step, None, where, query, key, max_logits, others[step - 1]))
+
+    p, m, c = pre[0]
+    for step in range(1, N):
         p = shift(p, ("x", "z"), (1, 1))
         m = shift(m, ("x", "z"), (-1, -1))
         c = shift(c, ("y", "y"), (1, -1))
         if step < N - 1:
-            parts = ring_add(pre[step], (p, m, c))
+            p, m, c = add(pre[step][0], p), add(pre[step][1], m), add_c(pre[step][2], c)
         if step == 1:
-            start = (1 - after(parts[0])[3]) * RP
-            theirs = swap(lax.dynamic_slice_in_dim(query_moment, start, RP, 0))
-        if step == 2:
-            theirs, parts = lax.optimization_barrier((theirs, parts))
+            theirs = swap(lax.dynamic_slice_in_dim(query_moment, (1 - after(c)[3]) * RP, RP, 0))
     pre = pre[-1]
 
     part = split_ab(where, pre[:2], (p, m))
@@ -662,9 +687,20 @@
     block = update(
         where, own, swap(own), peak, new_query_moment, new_key_moment, query_weight, key_weight
     )
-    stack = jnp.stack([block] + [shift(block, ("z", "x"), (by, by)) for by in (1, 2, 3)])
-    stacks = [stack] + [shift(stack, ("x", "z"), (by, by)) for by in (1, 2, 3)]
-    query_out, key_out = assemble(where, stacks)
+    blocks = [block] + [shift(block, ("z", "x"), (by, by)) for by in (1, 2, 3)]
+
+    def along(stack, by):
+        return shift(stack, ("x", "z"), (by, by))
+
+    first, second = (jnp.stack([b[i * M_HALF : (i + 1) * M_HALF] for b in blocks]) for i in range(2))
+    first_back, second_ahead = along(first, 1), along(second, -1)
+    second_back, first_ahead = along(second, 1), along(first, -1)
+    first_far, second_far = along(first_back, 1), along(second_ahead, -1)
+    query_out, key_out = assemble(
+        where,
+        (first, first_back, first_far, first_ahead),
+        (second, second_back, second_far, second_ahead),
+    )
     return (query_out, key_out, new_query_moment, new_key_moment)
 
 

time: 168 us -> 160 us (0.952)
  Pallas kernels: 48.5 us -> 38.5 us
  waiting for transfers between devices: 64 us -> 54.8 us
  starting transfers between devices: 51.2 us -> 59.8 us
  local copies, waits for them, and re-layouts: 0.64 us -> 3.14 us
    pallas_call x10 -> x9, Pallas kernels: 32.2 us -> 21.5 us  [the longest x7 20.7 us: local(): pl.pallas_call(functools.partial(local_kernel, sum_step, send_step), out_...]
    ppermute x30 -> x33, starting transfers between devices: 49.8 us -> 57 us  [shift(): return lax.ppermute(array, AXES, pairs)]
    ppermute x30 -> x33, waiting for transfers between devices: 59.1 us -> 52 us  [shift(): return lax.ppermute(array, AXES, pairs)]
    unnamed x12 -> x20, local copies, waits for them, and re-layouts: 0.03 us -> 2.48 us
    ppermute x8, waiting for transfers between devices: 4.96 us -> 2.87 us  [swap(): return lax.ppermute(array, AXES, pairs)]
  transfers between devices with their start and end apart: 38 -> 41, of which waited for: 22 -> 24; matrix products, arithmetic and copies ran while one was open for 0% -> 1% of each run, Pallas kernels for 24% -> 19%
where the time goes in v3:
time: 160 us; the launch traced here: 159 us
  starting transfers between devices  59.8 us (37%)
  waiting for transfers between devices  54.8 us (34%)
  Pallas kernels  38.5 us (24%)
  local copies, waits for them, and re-layouts  3.14 us (2%)
  between operations  1.69 us (1%)
    ppermute x33, starting transfers between devices, shift(): return lax.ppermute(array, AXES, pairs)  57 us
    ppermute x33, waiting for transfers between devices, shift(): return lax.ppermute(array, AXES, pairs)  52 us
    pallas_call x7, Pallas kernels, local(): pl.pallas_call(functools.partial(local_kernel, sum_step, send_step), out_...  20.7 us
    pallas_call x1, Pallas kernels, chain(): pl.pallas_call(chain_kernel, out_shape=out((512, 128), f32), in_specs=[VM...  5.6 us
  transfers between devices with their start and end apart: 41, of which 24 were waited for; matrix products, arithmetic and copies ran while one was open for 1% of the time, Pallas kernels for 19%

profile of v3, /device:TPU:8, one launch (start us, length us, event | category | flops | bytes accessed | tf_op | source)
XLA Modules:
  0.0 159.3 jit_solution(788202318051947264)
XLA Ops:
  0.7 2.7 %local_sum_None_send_1.1 = bf16[4,4,720,128]{3,2,1,0:T(8,128)(2,1)S(1)} custom-call(s32[4]{0:T(128)S(1)} %pad_add_fusion.where, bf16[4,2,192,6144]{3,2,1,0:T(8,128)(2,1)} %bitcast.23, bf16[4,2,64,4096]{3,2,1,0:T(8,128)(2,1)} %bitcast.30, f32[1,32]{1,0:T(1,128)} %logits.13), custom_call_target="tpu_custom_call" | custom-call | tf_op jit(solution)/shard_map/local_sum_None_send_1/pallas_call | solution.py:289
  3.5 2.7 %local_sum_None_send_2.1 = bf16[4,4,720,128]{3,2,1,0:T(8,128)(2,1)S(1)} custom-call(s32[4]{0:T(128)S(1)} %pad_add_fusion.where, bf16[4,2,192,6144]{3,2,1,0:T(8,128)(2,1)} %bitcast.24, bf16[4,2,64,4096]{3,2,1,0:T(8,128)(2,1)} %bitcast.31, f32[1,32]{1,0:T(1,128)} %logits.13), custom_call_target="tpu_custom_call" | custom-call | tf_op jit(solution)/shard_map/local_sum_None_send_2/pallas_call | solution.py:289
  6.8 2.7 %local_sum_None_send_3.1 = bf16[4,4,720,128]{3,2,1,0:T(8,128)(2,1)S(1)} custom-call(s32[4]{0:T(128)S(1)} %pad_add_fusion.where, bf16[4,2,192,6144]{3,2,1,0:T(8,128)(2,1)} %bitcast.25, bf16[4,2,64,4096]{3,2,1,0:T(8,128)(2,1)} %bitcast.32, f32[1,32]{1,0:T(1,128)} %logits.13), custom_call_target="tpu_custom_call" | custom-call | tf_op jit(solution)/shard_map/local_sum_None_send_3/pallas_call | solution.py:289
  9.6 2.9 %local_sum_1_send_None.1 = (bf16[4,4,240,128]{3,2,1,0:T(8,128)(2,1)S(1)}, bf16[4,4,240,128]{3,2,1,0:T(8,128)(2,1)S(1)}, bf16[4,4,240,128]{3,2,1,0:T(8,128)(2,1)S(1)}) custom-call(s32[4]{0:T(128)S(1)} %pad_add_fusion.where, bf16[4,2,192,6144]{3,2,1,0:T(8,128)(2,1)} %bitcast.26, bf16[4,2,64,4096]{3,2,1,0:T(8,128)(2,1)} %bitcast.33, f32[1,32]{1,0:T(1,128)} %logits.13, ...), custom_call_target="tpu_custom_call" | custom-call | tf_op jit(solution)/shard_map/local_sum_1_send_None/pallas_call | solution.py:289
  12.5 2.8 %collective-permute-start.7 = (bf16[4,4,240,128]{3,2,1,0:T(8,128)(2,1)S(1)}, bf16[4,4,240,128]{3,2,1,0:T(8,128)(2,1)S(1)}, u32[]{:S(2)}, u32[]{:S(2)}) collective-permute-start(bf16[4,4,240,128]{3,2,1,0:T(8,128)(2,1)S(1)} %get-tuple-element.57), channel_id=1, source_target_pairs={{0,24},{1,97},{2,26},{3,99},{4,28},{5,101},{6,30},{7,103},{8,0},{9... | collective-permute-start | bytes 2949128 | tf_op jit(solution)/shard_map/ppermute | solution.py:70
  15.4 3.8 %local_sum_2_send_4.1 = (bf16[4,4,240,128]{3,2,1,0:T(8,128)(2,1)S(1)}, bf16[4,4,240,128]{3,2,1,0:T(8,128)(2,1)S(1)}, bf16[4,4,240,128]{3,2,1,0:T(8,128)(2,1)S(1)}, bf16[4,4,720,128]{3,2,1,0:T(8,128)(2,1)S(1)}) custom-call(s32[4]{0:T(128)S(1)} %pad_add_fusion.where, bf16[4,2,192,6144]{3,2,1,0:T(8,128)(2,1)} %bitcast.27, bf16[4,2,64,4096]{3,2,1,0:T(8,128)(2,1)} %bitcast.34, ...), custom_call_target="tpu_custom_call" | custom-call | tf_op jit(solution)/shard_map/local_sum_2_send_4/pallas_call | solution.py:289
  22.5 4.5 %collective-permute-done.7 = bf16[4,4,240,128]{3,2,1,0:T(8,128)(2,1)S(1)} collective-permute-done((bf16[4,4,240,128]{3,2,1,0:T(8,128)(2,1)S(1)}, bf16[4,4,240,128]{3,2,1,0:T(8,128)(2,1)S(1)}, u32[]{:S(2)}, u32[]{:S(2)}) %collective-permute-start.7) | collective-permute-done | bytes 983072 | tf_op jit(solution)/shard_map/ppermute | solution.py:70
  27.2 3.8 %collective-permute-start.8 = (bf16[4,4,240,128]{3,2,1,0:T(8,128)(2,1)S(1)}, bf16[4,4,240,128]{3,2,1,0:T(8,128)(2,1)S(1)}, u32[]{:S(2)}, u32[]{:S(2)}) collective-permute-start(bf16[4,4,240,128]{3,2,1,0:T(8,128)(2,1)S(1)} %add_convert_fusion.1), channel_id=1, source_target_pairs={{0,24},{1,97},{2,26},{3,99},{4,28},{5,101},{6,30},{7,103},{8,0},{9... | collective-permute-start | bytes 2949128 | tf_op jit(solution)/shard_map/ppermute | solution.py:70
  31.4 2.9 %local_sum_3_send_None.1 = (bf16[4,4,240,128]{3,2,1,0:T(8,128)(2,1)S(1)}, bf16[4,4,240,128]{3,2,1,0:T(8,128)(2,1)S(1)}, bf16[4,4,240,128]{3,2,1,0:T(8,128)(2,1)S(1)}) custom-call(s32[4]{0:T(128)S(1)} %pad_add_fusion.where, bf16[4,2,192,6144]{3,2,1,0:T(8,128)(2,1)} %bitcast.28, bf16[4,2,64,4096]{3,2,1,0:T(8,128)(2,1)} %bitcast.35, f32[1,32]{1,0:T(1,128)} %logits.13, ...), custom_call_target="tpu_custom_call" | custom-call | tf_op jit(solution)/shard_map/local_sum_3_send_None/pallas_call | solution.py:289
  37.1 5.6 %collective-permute-done.8 = bf16[4,4,240,128]{3,2,1,0:T(8,128)(2,1)S(1)} collective-permute-done((bf16[4,4,240,128]{3,2,1,0:T(8,128)(2,1)S(1)}, bf16[4,4,240,128]{3,2,1,0:T(8,128)(2,1)S(1)}, u32[]{:S(2)}, u32[]{:S(2)}) %collective-permute-start.8) | collective-permute-done | bytes 983072 | tf_op jit(solution)/shard_map/ppermute | solution.py:70
  42.9 3.8 %collective-permute-start.9 = (bf16[4,4,240,128]{3,2,1,0:T(8,128)(2,1)S(1)}, bf16[4,4,240,128]{3,2,1,0:T(8,128)(2,1)S(1)}, u32[]{:S(2)}, u32[]{:S(2)}) collective-permute-start(bf16[4,4,240,128]{3,2,1,0:T(8,128)(2,1)S(1)} %add_convert_fusion), channel_id=1, source_target_pairs={{0,24},{1,97},{2,26},{3,99},{4,28},{5,101},{6,30},{7,103},{8,0},{9... | collective-permute-start | bytes 2949128 | tf_op jit(solution)/shard_map/ppermute | solution.py:70
  47.0 2.6 %collective-permute-done.17.second = bf16[4,4,240,128]{3,2,1,0:T(8,128)(2,1)S(1)} collective-permute-done((bf16[4,4,240,128]{3,2,1,0:T(8,128)(2,1)S(1)}, bf16[4,4,240,128]{3,2,1,0:T(8,128)(2,1)S(1)}, u32[]{:S(2)}, u32[]{:S(2)}) %collective-permute-start.17) | collective-permute-done | bytes 983072 | tf_op jit(solution)/shard_map/ppermute | solution.py:70
  51.6 2.9 %local_sum_4_send_None.1 = (bf16[4,4,240,128]{3,2,1,0:T(8,128)(2,1)S(1)}, bf16[4,4,240,128]{3,2,1,0:T(8,128)(2,1)S(1)}, bf16[4,4,240,128]{3,2,1,0:T(8,128)(2,1)S(1)}) custom-call(s32[4]{0:T(128)S(1)} %pad_add_fusion.where, bf16[4,2,192,6144]{3,2,1,0:T(8,128)(2,1)} %bitcast.29, bf16[4,2,64,4096]{3,2,1,0:T(8,128)(2,1)} %bitcast.36, f32[1,32]{1,0:T(1,128)} %logits.13, ...), custom_call_target="tpu_custom_call" | custom-call | tf_op jit(solution)/shard_map/local_sum_4_send_None/pallas_call | solution.py:289
  54.6 3.7 %collective-permute-done.9.m1 = bf16[4,4,240,128]{3,2,1,0:T(8,128)(2,1)S(1)} collective-permute-done((bf16[4,4,240,128]{3,2,1,0:T(8,128)(2,1)S(1)}, bf16[4,4,240,128]{3,2,1,0:T(8,128)(2,1)S(1)}, u32[]{:S(2)}, u32[]{:S(2)}) %collective-permute-start.9) | collective-permute-done | bytes 983072 | tf_op jit(solution)/shard_map/ppermute | solution.py:70
  58.3 4.0 %collective-permute-done.6.p1 = bf16[4,4,240,128]{3,2,1,0:T(8,128)(2,1)S(1)} collective-permute-done((bf16[4,4,240,128]{3,2,1,0:T(8,128)(2,1)S(1)}, bf16[4,4,240,128]{3,2,1,0:T(8,128)(2,1)S(1)}, u32[]{:S(2)}, u32[]{:S(2)}) %collective-permute-start.6) | collective-permute-done | bytes 983072 | tf_op jit(solution)/shard_map/ppermute | solution.py:70
  66.8 2.4 %collective-permute-start.12 = (bf16[4,480,128]{2,1,0:T(8,128)(2,1)}, bf16[4,480,128]{2,1,0:T(8,128)(2,1)S(1)}, u32[]{:S(2)}, u32[]{:S(2)}) collective-permute-start(bf16[4,480,128]{2,1,0:T(8,128)(2,1)} %get-tuple-element.61), channel_id=1, source_target_pairs={{0,6},{1,25},{2,0},{3,27},{4,2},{5,29},{6,4},{7,31},{8,14},{9,1},{... | collective-permute-start | bytes 1474568 | tf_op jit(solution)/shard_map/ppermute | solution.py:70
  72.9 3.6 %collective-permute-start.20 = (bf16[4,240,128]{2,1,0:T(8,128)(2,1)}, bf16[4,240,128]{2,1,0:T(8,128)(2,1)S(1)}, u32[]{:S(2)}, u32[]{:S(2)}) collective-permute-start(bf16[4,240,128]{2,1,0:T(8,128)(2,1)} %get-tuple-element.74), channel_id=1, source_target_pairs={{0,64},{1,65},{2,66},{3,67},{4,68},{5,69},{6,70},{7,71},{8,72},{9,... | collective-permute-start | bytes 737288 | tf_op jit(solution)/shard_map/ppermute | solution.py:70
  86.2 3.6 %collective-permute-start.14 = (bf16[480,128]{1,0:T(8,128)(2,1)}, bf16[480,128]{1,0:T(8,128)(2,1)S(1)}, u32[]{:S(2)}, u32[]{:S(2)}) collective-permute-start(bf16[480,128]{1,0:T(8,128)(2,1)} %get-tuple-element.64), channel_id=1, source_target_pairs={{0,64},{1,5},{2,66},{3,7},{4,68},{5,1},{6,70},{7,3},{8,72},{9,13},... | collective-permute-start | bytes 368648 | tf_op jit(solution)/shard_map/ppermute | solution.py:70
  92.1 2.2 %collective-permute-start.24 = (bf16[240,128]{1,0:T(8,128)(2,1)S(1)}, bf16[240,128]{1,0:T(8,128)(2,1)S(1)}, u32[]{:S(2)}, u32[]{:S(2)}) collective-permute-start(bf16[240,128]{1,0:T(8,128)(2,1)S(1)} %get-tuple-element.79), channel_id=1, source_target_pairs={{0,24},{1,25},{2,26},{3,27},{4,28},{5,29},{6,30},{7,31},{8,0},{9,1... | collective-permute-start | bytes 184328 | tf_op jit(solution)/shard_map/ppermute | solution.py:70
  94.3 2.6 %collective-permute-done.23.c2 = bf16[240,128]{1,0:T(8,128)(2,1)S(1)} collective-permute-done((bf16[240,128]{1,0:T(8,128)(2,1)S(1)}, bf16[240,128]{1,0:T(8,128)(2,1)S(1)}, u32[]{:S(2)}, u32[]{:S(2)}) %collective-permute-start.23) | collective-permute-done | bytes 61472 | tf_op jit(solution)/shard_map/ppermute | solution.py:70
  103.1 3.9 %collective-permute-start.27 = (f32[384,128]{1,0:T(8,128)S(1)}, f32[384,128]{1,0:T(8,128)S(1)}, u32[]{:S(2)}, u32[]{:S(2)}) collective-permute-start(f32[384,128]{1,0:T(8,128)S(1)} %select_add_fusion.g0), channel_id=1, source_target_pairs={{0,2},{1,3},{2,4},{3,5},{4,6},{5,7},{6,0},{7,1},{8,10},{9,11},{10,... | collective-permute-start | bytes 589832 | tf_op jit(solution)/shard_map/ppermute | solution.py:70
  107.0 2.2 %collective-permute-start.29 = (f32[384,128]{1,0:T(8,128)S(1)}, f32[384,128]{1,0:T(8,128)S(1)}, u32[]{:S(2)}, u32[]{:S(2)}) collective-permute-start(f32[384,128]{1,0:T(8,128)S(1)} %select_add_fusion.g0), channel_id=1, source_target_pairs={{0,6},{1,7},{2,0},{3,1},{4,2},{5,3},{6,4},{7,5},{8,14},{9,15},{10,... | collective-permute-start | bytes 589832 | tf_op jit(solution)/shard_map/ppermute | solution.py:70
  109.2 6.4 %collective-permute-done.27.g1 = f32[384,128]{1,0:T(8,128)S(1)} collective-permute-done((f32[384,128]{1,0:T(8,128)S(1)}, f32[384,128]{1,0:T(8,128)S(1)}, u32[]{:S(2)}, u32[]{:S(2)}) %collective-permute-start.27) | collective-permute-done | bytes 196640 | tf_op jit(solution)/shard_map/ppermute | solution.py:70
  117.8 5.6 %newton_schulz_polynomial.1.own = f32[512,128]{1,0:T(8,128)S(1)} custom-call(f32[384,128]{1,0:T(8,128)S(1)} %select_add_fusion.g0, f32[384,128]{1,0:T(8,128)S(1)} %collective-permute-done.27.g1, f32[384,128]{1,0:T(8,128)S(1)} %collective-permute-done.28.g2, f32[384,128]{1,0:T(8,128)S(1)} %collective-permute-done.29.g3), custom_call_target="tpu_custom_call" | custom-call | tf_op jit(solution)/shard_map/newton_schulz_polynomial/pallas_call | solution.py:526
  127.9 2.7 %collective-permute-start.34 = (bf16[704,128]{1,0:T(8,128)(2,1)S(1)}, bf16[704,128]{1,0:T(8,128)(2,1)S(1)}, u32[]{:S(2)}, u32[]{:S(2)}) collective-permute-start(bf16[704,128]{1,0:T(8,128)(2,1)S(1)} %update.1), channel_id=1, source_target_pairs={{0,96},{1,25},{2,98},{3,27},{4,100},{5,29},{6,102},{7,31},{8,104},... | collective-permute-start | bytes 540680 | tf_op jit(solution)/shard_map/ppermute | solution.py:70
  130.6 2.3 %collective-permute-done.32 = bf16[704,128]{1,0:T(8,128)(2,1)S(1)} collective-permute-done((bf16[704,128]{1,0:T(8,128)(2,1)S(1)}, bf16[704,128]{1,0:T(8,128)(2,1)S(1)}, u32[]{:S(2)}, u32[]{:S(2)}) %collective-permute-start.32) | collective-permute-done | bytes 180256 | tf_op jit(solution)/shard_map/ppermute | solution.py:70
  135.8 3.2 %collective-permute-start.39 = (bf16[4,352,128]{2,1,0:T(8,128)(2,1)S(1)}, bf16[4,352,128]{2,1,0:T(8,128)(2,1)S(1)}, u32[]{:S(2)}, u32[]{:S(2)}) collective-permute-start(bf16[4,352,128]{2,1,0:T(8,128)(2,1)S(1)} %pad_maximum_fusion.1.refs_4_), channel_id=1, source_target_pairs={{0,24},{1,97},{2,26},{3,99},{4,28},{5,101},{6,30},{7,103},{8,0},{9... | collective-permute-start | bytes 1081352 | tf_op jit(solution)/shard_map/ppermute | solution.py:70
  139.4 3.1 %collective-permute-start.37 = (bf16[4,352,128]{2,1,0:T(8,128)(2,1)S(1)}, bf16[4,352,128]{2,1,0:T(8,128)(2,1)S(1)}, u32[]{:S(2)}, u32[]{:S(2)}) collective-permute-start(bf16[4,352,128]{2,1,0:T(8,128)(2,1)S(1)} %pad_maximum_fusion.refs_0_), channel_id=1, source_target_pairs={{0,24},{1,97},{2,26},{3,99},{4,28},{5,101},{6,30},{7,103},{8,0},{9... | collective-permute-start | bytes 1081352 | tf_op jit(solution)/shard_map/ppermute | solution.py:70
  144.0 3.7 %collective-permute-start.40 = (bf16[4,352,128]{2,1,0:T(8,128)(2,1)S(1)}, bf16[4,352,128]{2,1,0:T(8,128)(2,1)S(1)}, u32[]{:S(2)}, u32[]{:S(2)}) collective-permute-start(bf16[4,352,128]{2,1,0:T(8,128)(2,1)S(1)} %collective-permute-done.39.refs_7_), channel_id=1, source_target_pairs={{0,24},{1,97},{2,26},{3,99},{4,28},{5,101},{6,30},{7,103},{8,0},{9... | collective-permute-start | bytes 1081352 | tf_op jit(solution)/shard_map/ppermute | solution.py:70
  147.8 3.9 %collective-permute-done.38.refs_5_ = bf16[4,352,128]{2,1,0:T(8,128)(2,1)S(1)} collective-permute-done((bf16[4,352,128]{2,1,0:T(8,128)(2,1)S(1)}, bf16[4,352,128]{2,1,0:T(8,128)(2,1)S(1)}, u32[]{:S(2)}, u32[]{:S(2)}) %collective-permute-start.38) | collective-permute-done | bytes 360480 | tf_op jit(solution)/shard_map/ppermute | solution.py:70
  152.6 3.8 %collective-permute-done.36.refs_2_ = bf16[4,352,128]{2,1,0:T(8,128)(2,1)S(1)} collective-permute-done((bf16[4,352,128]{2,1,0:T(8,128)(2,1)S(1)}, bf16[4,352,128]{2,1,0:T(8,128)(2,1)S(1)}, u32[]{:S(2)}, u32[]{:S(2)}) %collective-permute-start.36) | collective-permute-done | bytes 360480 | tf_op jit(solution)/shard_map/ppermute | solution.py:70
  156.4 2.9 %assemble.1 = (bf16[192,6144]{1,0:T(8,128)(2,1)}, bf16[64,4096]{1,0:T(8,128)(2,1)}) custom-call(s32[4]{0:T(128)S(1)} %pad_add_fusion.where, bf16[4,352,128]{2,1,0:T(8,128)(2,1)S(1)} %pad_maximum_fusion.refs_0_, bf16[4,352,128]{2,1,0:T(8,128)(2,1)S(1)} %collective-permute-done.35.refs_1_, bf16[4,352,128]{2,1,0:T(8,128)(2,1)S(1)} %collective-permute-done.36.refs_2_, ...), custom_call_target="tpu_custom_call" | custom-call | tf_op jit(solution)/shard_map/assemble/pallas_call | solution.py:622
  (106 shorter events, 48.2 us)
Async XLA Ops:
  6.2 9.1 %collective-permute-start.1 = (bf16[4,4,720,128]{3,2,1,0:T(8,128)(2,1)S(1)}, bf16[4,4,720,128]{3,2,1,0:T(8,128)(2,1)S(1)}, u32[]{:S(2)}, u32[]{:S(2)}) collective-permute-start(bf16[4,4,720,128]{3,2,1,0:T(8,128)(2,1)S(1)} %local_sum_None_send_2.1), channel_id=1, source_target_pairs={{0,1},{1,0},{2,3},{3,2},{4,5},{5,4},{6,7},{7,6},{8,9},{9,8},{10,11... | collective-permute-start | bytes 8847368 | tf_op jit(solution)/shard_map/ppermute | solution.py:75
  9.5 21.9 %collective-permute-start.3 = (bf16[4,4,720,128]{3,2,1,0:T(8,128)(2,1)S(1)}, bf16[4,4,720,128]{3,2,1,0:T(8,128)(2,1)S(1)}, u32[]{:S(2)}, u32[]{:S(2)}) collective-permute-start(bf16[4,4,720,128]{3,2,1,0:T(8,128)(2,1)S(1)} %local_sum_None_send_3.1), channel_id=1, source_target_pairs={{0,1},{1,0},{2,3},{3,2},{4,5},{5,4},{6,7},{7,6},{8,9},{9,8},{10,11... | collective-permute-start | bytes 8847368 | tf_op jit(solution)/shard_map/ppermute | solution.py:75
  12.5 14.4 %collective-permute-start.7 = (bf16[4,4,240,128]{3,2,1,0:T(8,128)(2,1)S(1)}, bf16[4,4,240,128]{3,2,1,0:T(8,128)(2,1)S(1)}, u32[]{:S(2)}, u32[]{:S(2)}) collective-permute-start(bf16[4,4,240,128]{3,2,1,0:T(8,128)(2,1)S(1)} %get-tuple-element.57), channel_id=1, source_target_pairs={{0,24},{1,97},{2,26},{3,99},{4,28},{5,101},{6,30},{7,103},{8,0},{9... | collective-permute-start | bytes 2949128 | tf_op jit(solution)/shard_map/ppermute | solution.py:70
  15.4 15.6 %collective-permute-start.4 = (bf16[4,4,240,128]{3,2,1,0:T(8,128)(2,1)S(1)}, bf16[4,4,240,128]{3,2,1,0:T(8,128)(2,1)S(1)}, u32[]{:S(2)}, u32[]{:S(2)}) collective-permute-start(bf16[4,4,240,128]{3,2,1,0:T(8,128)(2,1)S(1)} %get-tuple-element.46), channel_id=1, source_target_pairs={{0,8},{1,33},{2,10},{3,35},{4,12},{5,37},{6,14},{7,39},{8,16},{9,4... | collective-permute-start | bytes 2949128 | tf_op jit(solution)/shard_map/ppermute | solution.py:70
  19.2 32.4 %collective-permute-start.2 = (bf16[4,4,720,128]{3,2,1,0:T(8,128)(2,1)S(1)}, bf16[4,4,720,128]{3,2,1,0:T(8,128)(2,1)S(1)}, u32[]{:S(2)}, u32[]{:S(2)}) collective-permute-start(bf16[4,4,720,128]{3,2,1,0:T(8,128)(2,1)S(1)} %get-tuple-element.49), channel_id=1, source_target_pairs={{0,1},{1,0},{2,3},{3,2},{4,5},{5,4},{6,7},{7,6},{8,9},{9,8},{10,11... | collective-permute-start | bytes 8847368 | tf_op jit(solution)/shard_map/ppermute | solution.py:75
  20.9 14.1 %collective-permute-start.16 = (bf16[4,4,240,128]{3,2,1,0:T(8,128)(2,1)S(1)}, bf16[4,4,240,128]{3,2,1,0:T(8,128)(2,1)S(1)}, u32[]{:S(2)}, u32[]{:S(2)}) collective-permute-start(bf16[4,4,240,128]{3,2,1,0:T(8,128)(2,1)S(1)} %get-tuple-element.71), channel_id=1, source_target_pairs={{0,2},{1,7},{2,4},{3,1},{4,6},{5,3},{6,0},{7,5},{8,10},{9,15},{10,... | collective-permute-start | bytes 2949128 | tf_op jit(solution)/shard_map/ppermute | solution.py:70
  27.2 15.4 %collective-permute-start.8 = (bf16[4,4,240,128]{3,2,1,0:T(8,128)(2,1)S(1)}, bf16[4,4,240,128]{3,2,1,0:T(8,128)(2,1)S(1)}, u32[]{:S(2)}, u32[]{:S(2)}) collective-permute-start(bf16[4,4,240,128]{3,2,1,0:T(8,128)(2,1)S(1)} %add_convert_fusion.1), channel_id=1, source_target_pairs={{0,24},{1,97},{2,26},{3,99},{4,28},{5,101},{6,30},{7,103},{8,0},{9... | collective-permute-start | bytes 2949128 | tf_op jit(solution)/shard_map/ppermute | solution.py:70
  31.3 15.4 %collective-permute-start.5 = (bf16[4,4,240,128]{3,2,1,0:T(8,128)(2,1)S(1)}, bf16[4,4,240,128]{3,2,1,0:T(8,128)(2,1)S(1)}, u32[]{:S(2)}, u32[]{:S(2)}) collective-permute-start(bf16[4,4,240,128]{3,2,1,0:T(8,128)(2,1)S(1)} %add_convert_fusion.3), channel_id=1, source_target_pairs={{0,8},{1,33},{2,10},{3,35},{4,12},{5,37},{6,14},{7,39},{8,16},{9,4... | collective-permute-start | bytes 2949128 | tf_op jit(solution)/shard_map/ppermute | solution.py:70
  35.5 14.2 %collective-permute-start.17 = (bf16[4,4,240,128]{3,2,1,0:T(8,128)(2,1)S(1)}, bf16[4,4,240,128]{3,2,1,0:T(8,128)(2,1)S(1)}, u32[]{:S(2)}, u32[]{:S(2)}) collective-permute-start(bf16[4,4,240,128]{3,2,1,0:T(8,128)(2,1)S(1)} %add_c.2), channel_id=1, source_target_pairs={{0,2},{1,7},{2,4},{3,1},{4,6},{5,3},{6,0},{7,5},{8,10},{9,15},{10,... | collective-permute-start | bytes 2949128 | tf_op jit(solution)/shard_map/ppermute | solution.py:70
  42.9 15.4 %collective-permute-start.9 = (bf16[4,4,240,128]{3,2,1,0:T(8,128)(2,1)S(1)}, bf16[4,4,240,128]{3,2,1,0:T(8,128)(2,1)S(1)}, u32[]{:S(2)}, u32[]{:S(2)}) collective-permute-start(bf16[4,4,240,128]{3,2,1,0:T(8,128)(2,1)S(1)} %add_convert_fusion), channel_id=1, source_target_pairs={{0,24},{1,97},{2,26},{3,99},{4,28},{5,101},{6,30},{7,103},{8,0},{9... | collective-permute-start | bytes 2949128 | tf_op jit(solution)/shard_map/ppermute | solution.py:70
  46.9 15.4 %collective-permute-start.6 = (bf16[4,4,240,128]{3,2,1,0:T(8,128)(2,1)S(1)}, bf16[4,4,240,128]{3,2,1,0:T(8,128)(2,1)S(1)}, u32[]{:S(2)}, u32[]{:S(2)}) collective-permute-start(bf16[4,4,240,128]{3,2,1,0:T(8,128)(2,1)S(1)} %add_convert_fusion.2), channel_id=1, source_target_pairs={{0,8},{1,33},{2,10},{3,35},{4,12},{5,37},{6,14},{7,39},{8,16},{9,4... | collective-permute-start | bytes 2949128 | tf_op jit(solution)/shard_map/ppermute | solution.py:70
  50.0 19.2 %collective-permute-start.18 = (bf16[4,4,240,128]{3,2,1,0:T(8,128)(2,1)S(1)}, bf16[4,4,240,128]{3,2,1,0:T(8,128)(2,1)S(1)}, u32[]{:S(2)}, u32[]{:S(2)}) collective-permute-start(bf16[4,4,240,128]{3,2,1,0:T(8,128)(2,1)S(1)} %add_c.3), channel_id=1, source_target_pairs={{0,2},{1,7},{2,4},{3,1},{4,6},{5,3},{6,0},{7,5},{8,10},{9,15},{10,... | collective-permute-start | bytes 2949128 | tf_op jit(solution)/shard_map/ppermute | solution.py:70
  64.3 12.2 %collective-permute-start.10 = (bf16[4,480,128]{2,1,0:T(8,128)(2,1)S(1)}, bf16[4,480,128]{2,1,0:T(8,128)(2,1)S(1)}, u32[]{:S(2)}, u32[]{:S(2)}) collective-permute-start(bf16[4,480,128]{2,1,0:T(8,128)(2,1)S(1)} %get-tuple-element.59), channel_id=1, source_target_pairs={{0,2},{1,9},{2,4},{3,11},{4,6},{5,13},{6,0},{7,15},{8,10},{9,17},{... | collective-permute-start | bytes 1474568 | tf_op jit(solution)/shard_map/ppermute | solution.py:70
  65.9 13.5 %collective-permute-start.11 = (bf16[4,480,128]{2,1,0:T(8,128)(2,1)}, bf16[4,480,128]{2,1,0:T(8,128)(2,1)S(1)}, u32[]{:S(2)}, u32[]{:S(2)}) collective-permute-start(bf16[4,480,128]{2,1,0:T(8,128)(2,1)} %get-tuple-element.60), channel_id=1, source_target_pairs={{0,4},{1,17},{2,6},{3,19},{4,0},{5,21},{6,2},{7,23},{8,12},{9,25},... | collective-permute-start | bytes 1474568 | tf_op jit(solution)/shard_map/ppermute | solution.py:70
  66.8 14.3 %collective-permute-start.12 = (bf16[4,480,128]{2,1,0:T(8,128)(2,1)}, bf16[4,480,128]{2,1,0:T(8,128)(2,1)S(1)}, u32[]{:S(2)}, u32[]{:S(2)}) collective-permute-start(bf16[4,480,128]{2,1,0:T(8,128)(2,1)} %get-tuple-element.61), channel_id=1, source_target_pairs={{0,6},{1,25},{2,0},{3,27},{4,2},{5,29},{6,4},{7,31},{8,14},{9,1},{... | collective-permute-start | bytes 1474568 | tf_op jit(solution)/shard_map/ppermute | solution.py:70
  71.0 11.6 %collective-permute-start.19 = (bf16[4,240,128]{2,1,0:T(8,128)(2,1)}, bf16[4,240,128]{2,1,0:T(8,128)(2,1)S(1)}, u32[]{:S(2)}, u32[]{:S(2)}) collective-permute-start(bf16[4,240,128]{2,1,0:T(8,128)(2,1)} %get-tuple-element.73), channel_id=1, source_target_pairs={{0,32},{1,33},{2,34},{3,35},{4,36},{5,37},{6,38},{7,39},{8,40},{9,... | collective-permute-start | bytes 737288 | tf_op jit(solution)/shard_map/ppermute | solution.py:70
  72.9 10.6 %collective-permute-start.20 = (bf16[4,240,128]{2,1,0:T(8,128)(2,1)}, bf16[4,240,128]{2,1,0:T(8,128)(2,1)S(1)}, u32[]{:S(2)}, u32[]{:S(2)}) collective-permute-start(bf16[4,240,128]{2,1,0:T(8,128)(2,1)} %get-tuple-element.74), channel_id=1, source_target_pairs={{0,64},{1,65},{2,66},{3,67},{4,68},{5,69},{6,70},{7,71},{8,72},{9,... | collective-permute-start | bytes 737288 | tf_op jit(solution)/shard_map/ppermute | solution.py:70
  79.4 11.1 %collective-permute-start.25 = (f32[80,384]{1,0:T(8,128)S(1)}, f32[80,384]{1,0:T(8,128)S(1)}, u32[]{:S(2)}, u32[]{:S(2)}) collective-permute-start(f32[80,384]{1,0:T(8,128)S(1)} %constant_dynamic-slice_fusion.1), channel_id=1, source_target_pairs={{0,1},{1,0},{2,3},{3,2},{4,5},{5,4},{6,7},{7,6},{8,9},{9,8},{10,11... | collective-permute-start | bytes 368648 | tf_op jit(solution)/shard_map/ppermute | solution.py:75
  86.0 12.0 %collective-permute-start.13 = (bf16[480,128]{1,0:T(8,128)(2,1)}, bf16[480,128]{1,0:T(8,128)(2,1)S(1)}, u32[]{:S(2)}, u32[]{:S(2)}) collective-permute-start(bf16[480,128]{1,0:T(8,128)(2,1)} %get-tuple-element.63), channel_id=1, source_target_pairs={{0,32},{1,3},{2,34},{3,5},{4,36},{5,7},{6,38},{7,1},{8,40},{9,11},... | collective-permute-start | bytes 368648 | tf_op jit(solution)/shard_map/ppermute | solution.py:70
  86.2 11.8 %collective-permute-start.14 = (bf16[480,128]{1,0:T(8,128)(2,1)}, bf16[480,128]{1,0:T(8,128)(2,1)S(1)}, u32[]{:S(2)}, u32[]{:S(2)}) collective-permute-start(bf16[480,128]{1,0:T(8,128)(2,1)} %get-tuple-element.64), channel_id=1, source_target_pairs={{0,64},{1,5},{2,66},{3,7},{4,68},{5,1},{6,70},{7,3},{8,72},{9,13},... | collective-permute-start | bytes 368648 | tf_op jit(solution)/shard_map/ppermute | solution.py:70
  89.8 8.2 %collective-permute-start.15 = (bf16[480,128]{1,0:T(8,128)(2,1)}, bf16[480,128]{1,0:T(8,128)(2,1)S(1)}, u32[]{:S(2)}, u32[]{:S(2)}) collective-permute-start(bf16[480,128]{1,0:T(8,128)(2,1)} %get-tuple-element.65), channel_id=1, source_target_pairs={{0,96},{1,7},{2,98},{3,1},{4,100},{5,3},{6,102},{7,5},{8,104},{9,1... | collective-permute-start | bytes 368648 | tf_op jit(solution)/shard_map/ppermute | solution.py:70
  103.1 12.6 %collective-permute-start.27 = (f32[384,128]{1,0:T(8,128)S(1)}, f32[384,128]{1,0:T(8,128)S(1)}, u32[]{:S(2)}, u32[]{:S(2)}) collective-permute-start(f32[384,128]{1,0:T(8,128)S(1)} %select_add_fusion.g0), channel_id=1, source_target_pairs={{0,2},{1,3},{2,4},{3,5},{4,6},{5,7},{6,0},{7,1},{8,10},{9,11},{10,... | collective-permute-start | bytes 589832 | tf_op jit(solution)/shard_map/ppermute | solution.py:70
  107.0 9.3 %collective-permute-start.28 = (f32[384,128]{1,0:T(8,128)S(1)}, f32[384,128]{1,0:T(8,128)S(1)}, u32[]{:S(2)}, u32[]{:S(2)}) collective-permute-start(f32[384,128]{1,0:T(8,128)S(1)} %select_add_fusion.g0), channel_id=1, source_target_pairs={{0,4},{1,5},{2,6},{3,7},{4,0},{5,1},{6,2},{7,3},{8,12},{9,13},{10,... | collective-permute-start | bytes 589832 | tf_op jit(solution)/shard_map/ppermute | solution.py:70
  107.0 10.9 %collective-permute-start.29 = (f32[384,128]{1,0:T(8,128)S(1)}, f32[384,128]{1,0:T(8,128)S(1)}, u32[]{:S(2)}, u32[]{:S(2)}) collective-permute-start(f32[384,128]{1,0:T(8,128)S(1)} %select_add_fusion.g0), channel_id=1, source_target_pairs={{0,6},{1,7},{2,0},{3,1},{4,2},{5,3},{6,4},{7,5},{8,14},{9,15},{10,... | collective-permute-start | bytes 589832 | tf_op jit(solution)/shard_map/ppermute | solution.py:70
  109.1 14.4 %collective-permute-start.31 = (f32[80,384]{1,0:T(8,128)S(1)}, f32[80,384]{1,0:T(8,128)S(1)}, u32[]{:S(2)}, u32[]{:S(2)}) collective-permute-start(f32[80,384]{1,0:T(8,128)S(1)} %constant_dynamic-slice_fusion), channel_id=1, source_target_pairs={{0,1},{1,0},{2,3},{3,2},{4,5},{5,4},{6,7},{7,6},{8,9},{9,8},{10,11... | collective-permute-start | bytes 368648 | tf_op jit(solution)/shard_map/ppermute | solution.py:75
  127.9 7.8 %collective-permute-start.34 = (bf16[704,128]{1,0:T(8,128)(2,1)S(1)}, bf16[704,128]{1,0:T(8,128)(2,1)S(1)}, u32[]{:S(2)}, u32[]{:S(2)}) collective-permute-start(bf16[704,128]{1,0:T(8,128)(2,1)S(1)} %update.1), channel_id=1, source_target_pairs={{0,96},{1,25},{2,98},{3,27},{4,100},{5,29},{6,102},{7,31},{8,104},... | collective-permute-start | bytes 540680 | tf_op jit(solution)/shard_map/ppermute | solution.py:70
  135.8 8.2 %collective-permute-start.39 = (bf16[4,352,128]{2,1,0:T(8,128)(2,1)S(1)}, bf16[4,352,128]{2,1,0:T(8,128)(2,1)S(1)}, u32[]{:S(2)}, u32[]{:S(2)}) collective-permute-start(bf16[4,352,128]{2,1,0:T(8,128)(2,1)S(1)} %pad_maximum_fusion.1.refs_4_), channel_id=1, source_target_pairs={{0,24},{1,97},{2,26},{3,99},{4,28},{5,101},{6,30},{7,103},{8,0},{9... | collective-permute-start | bytes 1081352 | tf_op jit(solution)/shard_map/ppermute | solution.py:70
  139.1 8.7 %collective-permute-start.35 = (bf16[4,352,128]{2,1,0:T(8,128)(2,1)S(1)}, bf16[4,352,128]{2,1,0:T(8,128)(2,1)S(1)}, u32[]{:S(2)}, u32[]{:S(2)}) collective-permute-start(bf16[4,352,128]{2,1,0:T(8,128)(2,1)S(1)} %pad_maximum_fusion.refs_0_), channel_id=1, source_target_pairs={{0,8},{1,33},{2,10},{3,35},{4,12},{5,37},{6,14},{7,39},{8,16},{9,4... | collective-permute-start | bytes 1081352 | tf_op jit(solution)/shard_map/ppermute | solution.py:70
  139.2 12.5 %collective-permute-start.38 = (bf16[4,352,128]{2,1,0:T(8,128)(2,1)S(1)}, bf16[4,352,128]{2,1,0:T(8,128)(2,1)S(1)}, u32[]{:S(2)}, u32[]{:S(2)}) collective-permute-start(bf16[4,352,128]{2,1,0:T(8,128)(2,1)S(1)} %pad_maximum_fusion.1.refs_4_), channel_id=1, source_target_pairs={{0,8},{1,33},{2,10},{3,35},{4,12},{5,37},{6,14},{7,39},{8,16},{9,4... | collective-permute-start | bytes 1081352 | tf_op jit(solution)/shard_map/ppermute | solution.py:70
  139.4 12.3 %collective-permute-start.37 = (bf16[4,352,128]{2,1,0:T(8,128)(2,1)S(1)}, bf16[4,352,128]{2,1,0:T(8,128)(2,1)S(1)}, u32[]{:S(2)}, u32[]{:S(2)}) collective-permute-start(bf16[4,352,128]{2,1,0:T(8,128)(2,1)S(1)} %pad_maximum_fusion.refs_0_), channel_id=1, source_target_pairs={{0,24},{1,97},{2,26},{3,99},{4,28},{5,101},{6,30},{7,103},{8,0},{9... | collective-permute-start | bytes 1081352 | tf_op jit(solution)/shard_map/ppermute | solution.py:70
  144.0 8.6 %collective-permute-start.40 = (bf16[4,352,128]{2,1,0:T(8,128)(2,1)S(1)}, bf16[4,352,128]{2,1,0:T(8,128)(2,1)S(1)}, u32[]{:S(2)}, u32[]{:S(2)}) collective-permute-start(bf16[4,352,128]{2,1,0:T(8,128)(2,1)S(1)} %collective-permute-done.39.refs_7_), channel_id=1, source_target_pairs={{0,24},{1,97},{2,26},{3,99},{4,28},{5,101},{6,30},{7,103},{8,0},{9... | collective-permute-start | bytes 1081352 | tf_op jit(solution)/shard_map/ppermute | solution.py:70
  147.8 8.6 %collective-permute-start.36 = (bf16[4,352,128]{2,1,0:T(8,128)(2,1)S(1)}, bf16[4,352,128]{2,1,0:T(8,128)(2,1)S(1)}, u32[]{:S(2)}, u32[]{:S(2)}) collective-permute-start(bf16[4,352,128]{2,1,0:T(8,128)(2,1)S(1)} %collective-permute-done.35.refs_1_), channel_id=1, source_target_pairs={{0,8},{1,33},{2,10},{3,35},{4,12},{5,37},{6,14},{7,39},{8,16},{9,4... | collective-permute-start | bytes 1081352 | tf_op jit(solution)/shard_map/ppermute | solution.py:70
  (19 other events, 188.3 us)

commit v4 on v3

--- a/solution.py
+++ b/solution.py
@@ -33,7 +33,7 @@
 ML = 16
 M_ALL = 2 * MP + MC
 M_HALF = M_ALL // 2
-G_ROWS = 384
+G_ROWS = 288
 
 f32, bf16 = jnp.float32, jnp.bfloat16
 AXES = ("dp", "ctx")
@@ -437,9 +437,14 @@
     for head, to in enumerate((gram0, gram1)):
         wide = (full if head == 0 else pltpu.roll(full, QH, 1))[:, :256]
         gram = gram_of(wide)
-        to[pl.ds(0, 192), :] = gram[:192, :128]
-        to[pl.ds(192, 64), :] = gram[128:192, 128:]
-        to[pl.ds(256, 128), :] = gram_of(km_out[:, pl.ds(head * KH, KH)])
+        left = lax.broadcasted_iota(jnp.int32, (64, 128), 1) < 64
+        to[pl.ds(0, 64), :] = jnp.where(
+            left, gram[:64, :128], pltpu.roll(gram[128:192, 128:], 64, 1)
+        )
+        to[pl.ds(64, 128), :] = gram[64:192, :128]
+        gram = gram_of(km_out[:, pl.ds(head * KH, KH)])
+        to[pl.ds(192, 64), :] = gram[64:]
+        to[pl.ds(256, 32), :] = jnp.where(left[:32], gram[:32], pltpu.roll(gram[32:64], 64, 1))
 
 
 def moments(where, part, part_c, query_moment, theirs, key_moment):
@@ -475,20 +480,28 @@
 
 def chain_kernel(g0, g1, g2, g3, to):
     packed = g0[...] + g1[...] + g2[...] + g3[...]
-    top, side, corner = packed[:128], packed[128:192], packed[192:256]
-    key_gram = packed[256:384]
     row = lax.broadcasted_iota(jnp.int32, (256, 256), 0)
     column = lax.broadcasted_iota(jnp.int32, (256, 256), 1)
+    left = lax.broadcasted_iota(jnp.int32, (64, 128), 1) < 64
     zeros = jnp.zeros((64, 128), f32)
-    lower = jnp.concatenate([side, zeros], axis=0)
+
+    def stacked(*blocks):
+        return jnp.concatenate(blocks, axis=0)
+
+    def part(block, keep_left):
+        return jnp.where(left if keep_left else ~left, block, 0.0)
+
+    diagonal, middle, last = packed[:64], packed[64:128], packed[128:192]
+    lower = stacked(zeros, part(middle, True), last, zeros)
+    first = lower + stacked(part(diagonal, True), part(middle, False), zeros, zeros)
+    corner = part(pltpu.roll(diagonal, 64, 1), True)
     query_gram = jnp.concatenate(
-        [
-            jnp.concatenate([top, lower.T], axis=1),
-            jnp.concatenate([lower, jnp.concatenate([corner, zeros], axis=0)], axis=1),
-        ],
-        axis=0,
-    )
-    query_gram = jnp.where((row < QH) & (column < QH), query_gram, 0.0)
+        [first, stacked(zeros, zeros, corner, zeros)], axis=1
+    ) + stacked(lower.T, jnp.zeros((128, 256), f32))
+    middle, diagonal = packed[192:256], packed[256:288]
+    lower = stacked(zeros, part(middle, True))
+    diagonal = part(stacked(diagonal, pltpu.roll(diagonal, 64, 1)), True)
+    key_gram = lower + lower.T + stacked(diagonal, part(middle, False))
     query_eye = jnp.where((row == column) & (row < QH), 1.0, 0.0).astype(f32)
     key_eye = jnp.where(row == column, 1.0, 0.0).astype(f32)[:128, :128]
 

time: 160 us -> 156 us (0.975)
  waiting for transfers between devices: 54.8 us -> 52.6 us
  local copies, waits for them, and re-layouts: 3.14 us -> 1.52 us
    ppermute x33, waiting for transfers between devices: 52 us -> 49.8 us  [shift(): return lax.ppermute(array, AXES, pairs)]
    unnamed x20 -> x12, local copies, waits for them, and re-layouts: 2.48 us -> 0.86 us
where the time goes in v4:
time: 156 us; the launch traced here: 155 us
  starting transfers between devices  59.9 us (38%)
  waiting for transfers between devices  52.6 us (34%)
  Pallas kernels  38.5 us (25%)
  between operations  1.67 us (1%)
    ppermute x33, starting transfers between devices, shift(): return lax.ppermute(array, AXES, pairs)  57.1 us
    ppermute x33, waiting for transfers between devices, shift(): return lax.ppermute(array, AXES, pairs)  49.8 us
    pallas_call x7, Pallas kernels, local(): pl.pallas_call(functools.partial(local_kernel, sum_step, send_step), out_...  20.7 us
    pallas_call x1, Pallas kernels, chain(): pl.pallas_call(chain_kernel, out_shape=out((512, 128), f32), in_specs=[VM...  5.56 us
  transfers between devices with their start and end apart: 41, of which 24 were waited for; matrix products, arithmetic and copies ran while one was open for 1% of the time, Pallas kernels for 19%

profile of v4, /device:TPU:8, one launch (start us, length us, event | category | flops | bytes accessed | tf_op | source)
XLA Modules:
  0.0 155.4 jit_solution(8227868336542993175)
XLA Ops:
  0.7 2.7 %local_sum_None_send_1.1 = bf16[4,4,720,128]{3,2,1,0:T(8,128)(2,1)S(1)} custom-call(s32[4]{0:T(128)S(1)} %pad_add_fusion.where, bf16[4,2,192,6144]{3,2,1,0:T(8,128)(2,1)} %bitcast.23, bf16[4,2,64,4096]{3,2,1,0:T(8,128)(2,1)} %bitcast.30, f32[1,32]{1,0:T(1,128)} %logits.13), custom_call_target="tpu_custom_call" | custom-call | tf_op jit(solution)/shard_map/local_sum_None_send_1/pallas_call | solution.py:289
  3.5 2.7 %local_sum_None_send_2.1 = bf16[4,4,720,128]{3,2,1,0:T(8,128)(2,1)S(1)} custom-call(s32[4]{0:T(128)S(1)} %pad_add_fusion.where, bf16[4,2,192,6144]{3,2,1,0:T(8,128)(2,1)} %bitcast.24, bf16[4,2,64,4096]{3,2,1,0:T(8,128)(2,1)} %bitcast.31, f32[1,32]{1,0:T(1,128)} %logits.13), custom_call_target="tpu_custom_call" | custom-call | tf_op jit(solution)/shard_map/local_sum_None_send_2/pallas_call | solution.py:289
  6.8 2.7 %local_sum_None_send_3.1 = bf16[4,4,720,128]{3,2,1,0:T(8,128)(2,1)S(1)} custom-call(s32[4]{0:T(128)S(1)} %pad_add_fusion.where, bf16[4,2,192,6144]{3,2,1,0:T(8,128)(2,1)} %bitcast.25, bf16[4,2,64,4096]{3,2,1,0:T(8,128)(2,1)} %bitcast.32, f32[1,32]{1,0:T(1,128)} %logits.13), custom_call_target="tpu_custom_call" | custom-call | tf_op jit(solution)/shard_map/local_sum_None_send_3/pallas_call | solution.py:289
  9.6 2.9 %local_sum_1_send_None.1 = (bf16[4,4,240,128]{3,2,1,0:T(8,128)(2,1)S(1)}, bf16[4,4,240,128]{3,2,1,0:T(8,128)(2,1)S(1)}, bf16[4,4,240,128]{3,2,1,0:T(8,128)(2,1)S(1)}) custom-call(s32[4]{0:T(128)S(1)} %pad_add_fusion.where, bf16[4,2,192,6144]{3,2,1,0:T(8,128)(2,1)} %bitcast.26, bf16[4,2,64,4096]{3,2,1,0:T(8,128)(2,1)} %bitcast.33, f32[1,32]{1,0:T(1,128)} %logits.13, ...), custom_call_target="tpu_custom_call" | custom-call | tf_op jit(solution)/shard_map/local_sum_1_send_None/pallas_call | solution.py:289
  12.5 2.8 %collective-permute-start.7 = (bf16[4,4,240,128]{3,2,1,0:T(8,128)(2,1)S(1)}, bf16[4,4,240,128]{3,2,1,0:T(8,128)(2,1)S(1)}, u32[]{:S(2)}, u32[]{:S(2)}) collective-permute-start(bf16[4,4,240,128]{3,2,1,0:T(8,128)(2,1)S(1)} %get-tuple-element.57), channel_id=1, source_target_pairs={{0,24},{1,97},{2,26},{3,99},{4,28},{5,101},{6,30},{7,103},{8,0},{9... | collective-permute-start | bytes 2949128 | tf_op jit(solution)/shard_map/ppermute | solution.py:70
  15.4 3.8 %local_sum_2_send_4.1 = (bf16[4,4,240,128]{3,2,1,0:T(8,128)(2,1)S(1)}, bf16[4,4,240,128]{3,2,1,0:T(8,128)(2,1)S(1)}, bf16[4,4,240,128]{3,2,1,0:T(8,128)(2,1)S(1)}, bf16[4,4,720,128]{3,2,1,0:T(8,128)(2,1)S(1)}) custom-call(s32[4]{0:T(128)S(1)} %pad_add_fusion.where, bf16[4,2,192,6144]{3,2,1,0:T(8,128)(2,1)} %bitcast.27, bf16[4,2,64,4096]{3,2,1,0:T(8,128)(2,1)} %bitcast.34, ...), custom_call_target="tpu_custom_call" | custom-call | tf_op jit(solution)/shard_map/local_sum_2_send_4/pallas_call | solution.py:289
  22.5 4.5 %collective-permute-done.7 = bf16[4,4,240,128]{3,2,1,0:T(8,128)(2,1)S(1)} collective-permute-done((bf16[4,4,240,128]{3,2,1,0:T(8,128)(2,1)S(1)}, bf16[4,4,240,128]{3,2,1,0:T(8,128)(2,1)S(1)}, u32[]{:S(2)}, u32[]{:S(2)}) %collective-permute-start.7) | collective-permute-done | bytes 983072 | tf_op jit(solution)/shard_map/ppermute | solution.py:70
  27.2 3.8 %collective-permute-start.8 = (bf16[4,4,240,128]{3,2,1,0:T(8,128)(2,1)S(1)}, bf16[4,4,240,128]{3,2,1,0:T(8,128)(2,1)S(1)}, u32[]{:S(2)}, u32[]{:S(2)}) collective-permute-start(bf16[4,4,240,128]{3,2,1,0:T(8,128)(2,1)S(1)} %add_convert_fusion.1), channel_id=1, source_target_pairs={{0,24},{1,97},{2,26},{3,99},{4,28},{5,101},{6,30},{7,103},{8,0},{9... | collective-permute-start | bytes 2949128 | tf_op jit(solution)/shard_map/ppermute | solution.py:70
  31.4 2.9 %local_sum_3_send_None.1 = (bf16[4,4,240,128]{3,2,1,0:T(8,128)(2,1)S(1)}, bf16[4,4,240,128]{3,2,1,0:T(8,128)(2,1)S(1)}, bf16[4,4,240,128]{3,2,1,0:T(8,128)(2,1)S(1)}) custom-call(s32[4]{0:T(128)S(1)} %pad_add_fusion.where, bf16[4,2,192,6144]{3,2,1,0:T(8,128)(2,1)} %bitcast.28, bf16[4,2,64,4096]{3,2,1,0:T(8,128)(2,1)} %bitcast.35, f32[1,32]{1,0:T(1,128)} %logits.13, ...), custom_call_target="tpu_custom_call" | custom-call | tf_op jit(solution)/shard_map/local_sum_3_send_None/pallas_call | solution.py:289
  37.1 5.6 %collective-permute-done.8 = bf16[4,4,240,128]{3,2,1,0:T(8,128)(2,1)S(1)} collective-permute-done((bf16[4,4,240,128]{3,2,1,0:T(8,128)(2,1)S(1)}, bf16[4,4,240,128]{3,2,1,0:T(8,128)(2,1)S(1)}, u32[]{:S(2)}, u32[]{:S(2)}) %collective-permute-start.8) | collective-permute-done | bytes 983072 | tf_op jit(solution)/shard_map/ppermute | solution.py:70
  42.9 3.8 %collective-permute-start.9 = (bf16[4,4,240,128]{3,2,1,0:T(8,128)(2,1)S(1)}, bf16[4,4,240,128]{3,2,1,0:T(8,128)(2,1)S(1)}, u32[]{:S(2)}, u32[]{:S(2)}) collective-permute-start(bf16[4,4,240,128]{3,2,1,0:T(8,128)(2,1)S(1)} %add_convert_fusion), channel_id=1, source_target_pairs={{0,24},{1,97},{2,26},{3,99},{4,28},{5,101},{6,30},{7,103},{8,0},{9... | collective-permute-start | bytes 2949128 | tf_op jit(solution)/shard_map/ppermute | solution.py:70
  47.0 2.6 %collective-permute-done.17.second = bf16[4,4,240,128]{3,2,1,0:T(8,128)(2,1)S(1)} collective-permute-done((bf16[4,4,240,128]{3,2,1,0:T(8,128)(2,1)S(1)}, bf16[4,4,240,128]{3,2,1,0:T(8,128)(2,1)S(1)}, u32[]{:S(2)}, u32[]{:S(2)}) %collective-permute-start.17) | collective-permute-done | bytes 983072 | tf_op jit(solution)/shard_map/ppermute | solution.py:70
  51.6 2.9 %local_sum_4_send_None.1 = (bf16[4,4,240,128]{3,2,1,0:T(8,128)(2,1)S(1)}, bf16[4,4,240,128]{3,2,1,0:T(8,128)(2,1)S(1)}, bf16[4,4,240,128]{3,2,1,0:T(8,128)(2,1)S(1)}) custom-call(s32[4]{0:T(128)S(1)} %pad_add_fusion.where, bf16[4,2,192,6144]{3,2,1,0:T(8,128)(2,1)} %bitcast.29, bf16[4,2,64,4096]{3,2,1,0:T(8,128)(2,1)} %bitcast.36, f32[1,32]{1,0:T(1,128)} %logits.13, ...), custom_call_target="tpu_custom_call" | custom-call | tf_op jit(solution)/shard_map/local_sum_4_send_None/pallas_call | solution.py:289
  54.6 3.7 %collective-permute-done.9.m1 = bf16[4,4,240,128]{3,2,1,0:T(8,128)(2,1)S(1)} collective-permute-done((bf16[4,4,240,128]{3,2,1,0:T(8,128)(2,1)S(1)}, bf16[4,4,240,128]{3,2,1,0:T(8,128)(2,1)S(1)}, u32[]{:S(2)}, u32[]{:S(2)}) %collective-permute-start.9) | collective-permute-done | bytes 983072 | tf_op jit(solution)/shard_map/ppermute | solution.py:70
  58.3 4.0 %collective-permute-done.6.p1 = bf16[4,4,240,128]{3,2,1,0:T(8,128)(2,1)S(1)} collective-permute-done((bf16[4,4,240,128]{3,2,1,0:T(8,128)(2,1)S(1)}, bf16[4,4,240,128]{3,2,1,0:T(8,128)(2,1)S(1)}, u32[]{:S(2)}, u32[]{:S(2)}) %collective-permute-start.6) | collective-permute-done | bytes 983072 | tf_op jit(solution)/shard_map/ppermute | solution.py:70
  66.8 2.4 %collective-permute-start.12 = (bf16[4,480,128]{2,1,0:T(8,128)(2,1)}, bf16[4,480,128]{2,1,0:T(8,128)(2,1)S(1)}, u32[]{:S(2)}, u32[]{:S(2)}) collective-permute-start(bf16[4,480,128]{2,1,0:T(8,128)(2,1)} %get-tuple-element.61), channel_id=1, source_target_pairs={{0,6},{1,25},{2,0},{3,27},{4,2},{5,29},{6,4},{7,31},{8,14},{9,1},{... | collective-permute-start | bytes 1474568 | tf_op jit(solution)/shard_map/ppermute | solution.py:70
  72.9 3.6 %collective-permute-start.20 = (bf16[4,240,128]{2,1,0:T(8,128)(2,1)}, bf16[4,240,128]{2,1,0:T(8,128)(2,1)S(1)}, u32[]{:S(2)}, u32[]{:S(2)}) collective-permute-start(bf16[4,240,128]{2,1,0:T(8,128)(2,1)} %get-tuple-element.74), channel_id=1, source_target_pairs={{0,64},{1,65},{2,66},{3,67},{4,68},{5,69},{6,70},{7,71},{8,72},{9,... | collective-permute-start | bytes 737288 | tf_op jit(solution)/shard_map/ppermute | solution.py:70
  86.2 3.6 %collective-permute-start.14 = (bf16[480,128]{1,0:T(8,128)(2,1)}, bf16[480,128]{1,0:T(8,128)(2,1)S(1)}, u32[]{:S(2)}, u32[]{:S(2)}) collective-permute-start(bf16[480,128]{1,0:T(8,128)(2,1)} %get-tuple-element.64), channel_id=1, source_target_pairs={{0,64},{1,5},{2,66},{3,7},{4,68},{5,1},{6,70},{7,3},{8,72},{9,13},... | collective-permute-start | bytes 368648 | tf_op jit(solution)/shard_map/ppermute | solution.py:70
  91.4 2.3 %collective-permute-start.24 = (bf16[240,128]{1,0:T(8,128)(2,1)S(1)}, bf16[240,128]{1,0:T(8,128)(2,1)S(1)}, u32[]{:S(2)}, u32[]{:S(2)}) collective-permute-start(bf16[240,128]{1,0:T(8,128)(2,1)S(1)} %get-tuple-element.79), channel_id=1, source_target_pairs={{0,24},{1,25},{2,26},{3,27},{4,28},{5,29},{6,30},{7,31},{8,0},{9,1... | collective-permute-start | bytes 184328 | tf_op jit(solution)/shard_map/ppermute | solution.py:70
  93.7 2.5 %collective-permute-done.23.c2 = bf16[240,128]{1,0:T(8,128)(2,1)S(1)} collective-permute-done((bf16[240,128]{1,0:T(8,128)(2,1)S(1)}, bf16[240,128]{1,0:T(8,128)(2,1)S(1)}, u32[]{:S(2)}, u32[]{:S(2)}) %collective-permute-start.23) | collective-permute-done | bytes 61472 | tf_op jit(solution)/shard_map/ppermute | solution.py:70
  101.3 3.9 %collective-permute-start.27 = (f32[288,128]{1,0:T(8,128)S(1)}, f32[288,128]{1,0:T(8,128)S(1)}, u32[]{:S(2)}, u32[]{:S(2)}) collective-permute-start(f32[288,128]{1,0:T(8,128)S(1)} %select_add_fusion.g0), channel_id=1, source_target_pairs={{0,2},{1,3},{2,4},{3,5},{4,6},{5,7},{6,0},{7,1},{8,10},{9,11},{10,... | collective-permute-start | bytes 442376 | tf_op jit(solution)/shard_map/ppermute | solution.py:70
  105.2 2.2 %collective-permute-start.29 = (f32[288,128]{1,0:T(8,128)S(1)}, f32[288,128]{1,0:T(8,128)S(1)}, u32[]{:S(2)}, u32[]{:S(2)}) collective-permute-start(f32[288,128]{1,0:T(8,128)S(1)} %select_add_fusion.g0), channel_id=1, source_target_pairs={{0,6},{1,7},{2,0},{3,1},{4,2},{5,3},{6,4},{7,5},{8,14},{9,15},{10,... | collective-permute-start | bytes 442376 | tf_op jit(solution)/shard_map/ppermute | solution.py:70
  107.5 4.3 %collective-permute-done.27.g1 = f32[288,128]{1,0:T(8,128)S(1)} collective-permute-done((f32[288,128]{1,0:T(8,128)S(1)}, f32[288,128]{1,0:T(8,128)S(1)}, u32[]{:S(2)}, u32[]{:S(2)}) %collective-permute-start.27) | collective-permute-done | bytes 147488 | tf_op jit(solution)/shard_map/ppermute | solution.py:70
  114.0 5.6 %newton_schulz_polynomial.1.own = f32[512,128]{1,0:T(8,128)S(1)} custom-call(f32[288,128]{1,0:T(8,128)S(1)} %select_add_fusion.g0, f32[288,128]{1,0:T(8,128)S(1)} %collective-permute-done.27.g1, f32[288,128]{1,0:T(8,128)S(1)} %collective-permute-done.28.g2, f32[288,128]{1,0:T(8,128)S(1)} %collective-permute-done.29.g3), custom_call_target="tpu_custom_call" | custom-call | tf_op jit(solution)/shard_map/newton_schulz_polynomial/pallas_call | solution.py:539
  124.7 2.1 %collective-permute-start.34 = (bf16[704,128]{1,0:T(8,128)(2,1)S(1)}, bf16[704,128]{1,0:T(8,128)(2,1)S(1)}, u32[]{:S(2)}, u32[]{:S(2)}) collective-permute-start(bf16[704,128]{1,0:T(8,128)(2,1)S(1)} %update.1), channel_id=1, source_target_pairs={{0,96},{1,25},{2,98},{3,27},{4,100},{5,29},{6,102},{7,31},{8,104},... | collective-permute-start | bytes 540680 | tf_op jit(solution)/shard_map/ppermute | solution.py:70
  126.8 2.3 %collective-permute-done.32 = bf16[704,128]{1,0:T(8,128)(2,1)S(1)} collective-permute-done((bf16[704,128]{1,0:T(8,128)(2,1)S(1)}, bf16[704,128]{1,0:T(8,128)(2,1)S(1)}, u32[]{:S(2)}, u32[]{:S(2)}) %collective-permute-start.32) | collective-permute-done | bytes 180256 | tf_op jit(solution)/shard_map/ppermute | solution.py:70
  131.9 3.2 %collective-permute-start.39 = (bf16[4,352,128]{2,1,0:T(8,128)(2,1)S(1)}, bf16[4,352,128]{2,1,0:T(8,128)(2,1)S(1)}, u32[]{:S(2)}, u32[]{:S(2)}) collective-permute-start(bf16[4,352,128]{2,1,0:T(8,128)(2,1)S(1)} %pad_maximum_fusion.1.refs_4_), channel_id=1, source_target_pairs={{0,24},{1,97},{2,26},{3,99},{4,28},{5,101},{6,30},{7,103},{8,0},{9... | collective-permute-start | bytes 1081352 | tf_op jit(solution)/shard_map/ppermute | solution.py:70
  135.5 3.1 %collective-permute-start.37 = (bf16[4,352,128]{2,1,0:T(8,128)(2,1)S(1)}, bf16[4,352,128]{2,1,0:T(8,128)(2,1)S(1)}, u32[]{:S(2)}, u32[]{:S(2)}) collective-permute-start(bf16[4,352,128]{2,1,0:T(8,128)(2,1)S(1)} %pad_maximum_fusion.refs_0_), channel_id=1, source_target_pairs={{0,24},{1,97},{2,26},{3,99},{4,28},{5,101},{6,30},{7,103},{8,0},{9... | collective-permute-start | bytes 1081352 | tf_op jit(solution)/shard_map/ppermute | solution.py:70
  140.1 3.7 %collective-permute-start.40 = (bf16[4,352,128]{2,1,0:T(8,128)(2,1)S(1)}, bf16[4,352,128]{2,1,0:T(8,128)(2,1)S(1)}, u32[]{:S(2)}, u32[]{:S(2)}) collective-permute-start(bf16[4,352,128]{2,1,0:T(8,128)(2,1)S(1)} %collective-permute-done.39.refs_7_), channel_id=1, source_target_pairs={{0,24},{1,97},{2,26},{3,99},{4,28},{5,101},{6,30},{7,103},{8,0},{9... | collective-permute-start | bytes 1081352 | tf_op jit(solution)/shard_map/ppermute | solution.py:70
  143.9 3.9 %collective-permute-done.38.refs_5_ = bf16[4,352,128]{2,1,0:T(8,128)(2,1)S(1)} collective-permute-done((bf16[4,352,128]{2,1,0:T(8,128)(2,1)S(1)}, bf16[4,352,128]{2,1,0:T(8,128)(2,1)S(1)}, u32[]{:S(2)}, u32[]{:S(2)}) %collective-permute-start.38) | collective-permute-done | bytes 360480 | tf_op jit(solution)/shard_map/ppermute | solution.py:70
  148.7 3.8 %collective-permute-done.36.refs_2_ = bf16[4,352,128]{2,1,0:T(8,128)(2,1)S(1)} collective-permute-done((bf16[4,352,128]{2,1,0:T(8,128)(2,1)S(1)}, bf16[4,352,128]{2,1,0:T(8,128)(2,1)S(1)}, u32[]{:S(2)}, u32[]{:S(2)}) %collective-permute-start.36) | collective-permute-done | bytes 360480 | tf_op jit(solution)/shard_map/ppermute | solution.py:70
  152.6 2.9 %assemble.1 = (bf16[192,6144]{1,0:T(8,128)(2,1)}, bf16[64,4096]{1,0:T(8,128)(2,1)}) custom-call(s32[4]{0:T(128)S(1)} %pad_add_fusion.where, bf16[4,352,128]{2,1,0:T(8,128)(2,1)S(1)} %pad_maximum_fusion.refs_0_, bf16[4,352,128]{2,1,0:T(8,128)(2,1)S(1)} %collective-permute-done.35.refs_1_, bf16[4,352,128]{2,1,0:T(8,128)(2,1)S(1)} %collective-permute-done.36.refs_2_, ...), custom_call_target="tpu_custom_call" | custom-call | tf_op jit(solution)/shard_map/assemble/pallas_call | solution.py:635
  (98 shorter events, 47.1 us)
Async XLA Ops:
  6.2 9.1 %collective-permute-start.1 = (bf16[4,4,720,128]{3,2,1,0:T(8,128)(2,1)S(1)}, bf16[4,4,720,128]{3,2,1,0:T(8,128)(2,1)S(1)}, u32[]{:S(2)}, u32[]{:S(2)}) collective-permute-start(bf16[4,4,720,128]{3,2,1,0:T(8,128)(2,1)S(1)} %local_sum_None_send_2.1), channel_id=1, source_target_pairs={{0,1},{1,0},{2,3},{3,2},{4,5},{5,4},{6,7},{7,6},{8,9},{9,8},{10,11... | collective-permute-start | bytes 8847368 | tf_op jit(solution)/shard_map/ppermute | solution.py:75
  9.5 21.9 %collective-permute-start.3 = (bf16[4,4,720,128]{3,2,1,0:T(8,128)(2,1)S(1)}, bf16[4,4,720,128]{3,2,1,0:T(8,128)(2,1)S(1)}, u32[]{:S(2)}, u32[]{:S(2)}) collective-permute-start(bf16[4,4,720,128]{3,2,1,0:T(8,128)(2,1)S(1)} %local_sum_None_send_3.1), channel_id=1, source_target_pairs={{0,1},{1,0},{2,3},{3,2},{4,5},{5,4},{6,7},{7,6},{8,9},{9,8},{10,11... | collective-permute-start | bytes 8847368 | tf_op jit(solution)/shard_map/ppermute | solution.py:75
  12.5 14.4 %collective-permute-start.7 = (bf16[4,4,240,128]{3,2,1,0:T(8,128)(2,1)S(1)}, bf16[4,4,240,128]{3,2,1,0:T(8,128)(2,1)S(1)}, u32[]{:S(2)}, u32[]{:S(2)}) collective-permute-start(bf16[4,4,240,128]{3,2,1,0:T(8,128)(2,1)S(1)} %get-tuple-element.57), channel_id=1, source_target_pairs={{0,24},{1,97},{2,26},{3,99},{4,28},{5,101},{6,30},{7,103},{8,0},{9... | collective-permute-start | bytes 2949128 | tf_op jit(solution)/shard_map/ppermute | solution.py:70
  15.4 15.6 %collective-permute-start.4 = (bf16[4,4,240,128]{3,2,1,0:T(8,128)(2,1)S(1)}, bf16[4,4,240,128]{3,2,1,0:T(8,128)(2,1)S(1)}, u32[]{:S(2)}, u32[]{:S(2)}) collective-permute-start(bf16[4,4,240,128]{3,2,1,0:T(8,128)(2,1)S(1)} %get-tuple-element.46), channel_id=1, source_target_pairs={{0,8},{1,33},{2,10},{3,35},{4,12},{5,37},{6,14},{7,39},{8,16},{9,4... | collective-permute-start | bytes 2949128 | tf_op jit(solution)/shard_map/ppermute | solution.py:70
  19.2 32.4 %collective-permute-start.2 = (bf16[4,4,720,128]{3,2,1,0:T(8,128)(2,1)S(1)}, bf16[4,4,720,128]{3,2,1,0:T(8,128)(2,1)S(1)}, u32[]{:S(2)}, u32[]{:S(2)}) collective-permute-start(bf16[4,4,720,128]{3,2,1,0:T(8,128)(2,1)S(1)} %get-tuple-element.49), channel_id=1, source_target_pairs={{0,1},{1,0},{2,3},{3,2},{4,5},{5,4},{6,7},{7,6},{8,9},{9,8},{10,11... | collective-permute-start | bytes 8847368 | tf_op jit(solution)/shard_map/ppermute | solution.py:75
  20.9 14.1 %collective-permute-start.16 = (bf16[4,4,240,128]{3,2,1,0:T(8,128)(2,1)S(1)}, bf16[4,4,240,128]{3,2,1,0:T(8,128)(2,1)S(1)}, u32[]{:S(2)}, u32[]{:S(2)}) collective-permute-start(bf16[4,4,240,128]{3,2,1,0:T(8,128)(2,1)S(1)} %get-tuple-element.71), channel_id=1, source_target_pairs={{0,2},{1,7},{2,4},{3,1},{4,6},{5,3},{6,0},{7,5},{8,10},{9,15},{10,... | collective-permute-start | bytes 2949128 | tf_op jit(solution)/shard_map/ppermute | solution.py:70
  27.2 15.4 %collective-permute-start.8 = (bf16[4,4,240,128]{3,2,1,0:T(8,128)(2,1)S(1)}, bf16[4,4,240,128]{3,2,1,0:T(8,128)(2,1)S(1)}, u32[]{:S(2)}, u32[]{:S(2)}) collective-permute-start(bf16[4,4,240,128]{3,2,1,0:T(8,128)(2,1)S(1)} %add_convert_fusion.1), channel_id=1, source_target_pairs={{0,24},{1,97},{2,26},{3,99},{4,28},{5,101},{6,30},{7,103},{8,0},{9... | collective-permute-start | bytes 2949128 | tf_op jit(solution)/shard_map/ppermute | solution.py:70
  31.3 15.4 %collective-permute-start.5 = (bf16[4,4,240,128]{3,2,1,0:T(8,128)(2,1)S(1)}, bf16[4,4,240,128]{3,2,1,0:T(8,128)(2,1)S(1)}, u32[]{:S(2)}, u32[]{:S(2)}) collective-permute-start(bf16[4,4,240,128]{3,2,1,0:T(8,128)(2,1)S(1)} %add_convert_fusion.3), channel_id=1, source_target_pairs={{0,8},{1,33},{2,10},{3,35},{4,12},{5,37},{6,14},{7,39},{8,16},{9,4... | collective-permute-start | bytes 2949128 | tf_op jit(solution)/shard_map/ppermute | solution.py:70
  35.5 14.2 %collective-permute-start.17 = (bf16[4,4,240,128]{3,2,1,0:T(8,128)(2,1)S(1)}, bf16[4,4,240,128]{3,2,1,0:T(8,128)(2,1)S(1)}, u32[]{:S(2)}, u32[]{:S(2)}) collective-permute-start(bf16[4,4,240,128]{3,2,1,0:T(8,128)(2,1)S(1)} %add_c.2), channel_id=1, source_target_pairs={{0,2},{1,7},{2,4},{3,1},{4,6},{5,3},{6,0},{7,5},{8,10},{9,15},{10,... | collective-permute-start | bytes 2949128 | tf_op jit(solution)/shard_map/ppermute | solution.py:70
  42.9 15.4 %collective-permute-start.9 = (bf16[4,4,240,128]{3,2,1,0:T(8,128)(2,1)S(1)}, bf16[4,4,240,128]{3,2,1,0:T(8,128)(2,1)S(1)}, u32[]{:S(2)}, u32[]{:S(2)}) collective-permute-start(bf16[4,4,240,128]{3,2,1,0:T(8,128)(2,1)S(1)} %add_convert_fusion), channel_id=1, source_target_pairs={{0,24},{1,97},{2,26},{3,99},{4,28},{5,101},{6,30},{7,103},{8,0},{9... | collective-permute-start | bytes 2949128 | tf_op jit(solution)/shard_map/ppermute | solution.py:70
  46.9 15.4 %collective-permute-start.6 = (bf16[4,4,240,128]{3,2,1,0:T(8,128)(2,1)S(1)}, bf16[4,4,240,128]{3,2,1,0:T(8,128)(2,1)S(1)}, u32[]{:S(2)}, u32[]{:S(2)}) collective-permute-start(bf16[4,4,240,128]{3,2,1,0:T(8,128)(2,1)S(1)} %add_convert_fusion.2), channel_id=1, source_target_pairs={{0,8},{1,33},{2,10},{3,35},{4,12},{5,37},{6,14},{7,39},{8,16},{9,4... | collective-permute-start | bytes 2949128 | tf_op jit(solution)/shard_map/ppermute | solution.py:70
  50.0 19.2 %collective-permute-start.18 = (bf16[4,4,240,128]{3,2,1,0:T(8,128)(2,1)S(1)}, bf16[4,4,240,128]{3,2,1,0:T(8,128)(2,1)S(1)}, u32[]{:S(2)}, u32[]{:S(2)}) collective-permute-start(bf16[4,4,240,128]{3,2,1,0:T(8,128)(2,1)S(1)} %add_c.3), channel_id=1, source_target_pairs={{0,2},{1,7},{2,4},{3,1},{4,6},{5,3},{6,0},{7,5},{8,10},{9,15},{10,... | collective-permute-start | bytes 2949128 | tf_op jit(solution)/shard_map/ppermute | solution.py:70
  64.3 12.1 %collective-permute-start.10 = (bf16[4,480,128]{2,1,0:T(8,128)(2,1)S(1)}, bf16[4,480,128]{2,1,0:T(8,128)(2,1)S(1)}, u32[]{:S(2)}, u32[]{:S(2)}) collective-permute-start(bf16[4,480,128]{2,1,0:T(8,128)(2,1)S(1)} %get-tuple-element.59), channel_id=1, source_target_pairs={{0,2},{1,9},{2,4},{3,11},{4,6},{5,13},{6,0},{7,15},{8,10},{9,17},{... | collective-permute-start | bytes 1474568 | tf_op jit(solution)/shard_map/ppermute | solution.py:70
  65.9 13.4 %collective-permute-start.11 = (bf16[4,480,128]{2,1,0:T(8,128)(2,1)}, bf16[4,480,128]{2,1,0:T(8,128)(2,1)S(1)}, u32[]{:S(2)}, u32[]{:S(2)}) collective-permute-start(bf16[4,480,128]{2,1,0:T(8,128)(2,1)} %get-tuple-element.60), channel_id=1, source_target_pairs={{0,4},{1,17},{2,6},{3,19},{4,0},{5,21},{6,2},{7,23},{8,12},{9,25},... | collective-permute-start | bytes 1474568 | tf_op jit(solution)/shard_map/ppermute | solution.py:70
  66.8 14.3 %collective-permute-start.12 = (bf16[4,480,128]{2,1,0:T(8,128)(2,1)}, bf16[4,480,128]{2,1,0:T(8,128)(2,1)S(1)}, u32[]{:S(2)}, u32[]{:S(2)}) collective-permute-start(bf16[4,480,128]{2,1,0:T(8,128)(2,1)} %get-tuple-element.61), channel_id=1, source_target_pairs={{0,6},{1,25},{2,0},{3,27},{4,2},{5,29},{6,4},{7,31},{8,14},{9,1},{... | collective-permute-start | bytes 1474568 | tf_op jit(solution)/shard_map/ppermute | solution.py:70
  71.0 11.6 %collective-permute-start.19 = (bf16[4,240,128]{2,1,0:T(8,128)(2,1)}, bf16[4,240,128]{2,1,0:T(8,128)(2,1)S(1)}, u32[]{:S(2)}, u32[]{:S(2)}) collective-permute-start(bf16[4,240,128]{2,1,0:T(8,128)(2,1)} %get-tuple-element.73), channel_id=1, source_target_pairs={{0,32},{1,33},{2,34},{3,35},{4,36},{5,37},{6,38},{7,39},{8,40},{9,... | collective-permute-start | bytes 737288 | tf_op jit(solution)/shard_map/ppermute | solution.py:70
  72.9 10.6 %collective-permute-start.20 = (bf16[4,240,128]{2,1,0:T(8,128)(2,1)}, bf16[4,240,128]{2,1,0:T(8,128)(2,1)S(1)}, u32[]{:S(2)}, u32[]{:S(2)}) collective-permute-start(bf16[4,240,128]{2,1,0:T(8,128)(2,1)} %get-tuple-element.74), channel_id=1, source_target_pairs={{0,64},{1,65},{2,66},{3,67},{4,68},{5,69},{6,70},{7,71},{8,72},{9,... | collective-permute-start | bytes 737288 | tf_op jit(solution)/shard_map/ppermute | solution.py:70
  76.5 7.6 %collective-permute-start.21 = (bf16[4,240,128]{2,1,0:T(8,128)(2,1)}, bf16[4,240,128]{2,1,0:T(8,128)(2,1)S(1)}, u32[]{:S(2)}, u32[]{:S(2)}) collective-permute-start(bf16[4,240,128]{2,1,0:T(8,128)(2,1)} %get-tuple-element.75), channel_id=1, source_target_pairs={{0,96},{1,97},{2,98},{3,99},{4,100},{5,101},{6,102},{7,103},{8,104... | collective-permute-start | bytes 737288 | tf_op jit(solution)/shard_map/ppermute | solution.py:70
  79.3 11.1 %collective-permute-start.25 = (f32[80,384]{1,0:T(8,128)S(1)}, f32[80,384]{1,0:T(8,128)S(1)}, u32[]{:S(2)}, u32[]{:S(2)}) collective-permute-start(f32[80,384]{1,0:T(8,128)S(1)} %constant_dynamic-slice_fusion.1), channel_id=1, source_target_pairs={{0,1},{1,0},{2,3},{3,2},{4,5},{5,4},{6,7},{7,6},{8,9},{9,8},{10,11... | collective-permute-start | bytes 368648 | tf_op jit(solution)/shard_map/ppermute | solution.py:75
  86.0 11.4 %collective-permute-start.13 = (bf16[480,128]{1,0:T(8,128)(2,1)}, bf16[480,128]{1,0:T(8,128)(2,1)S(1)}, u32[]{:S(2)}, u32[]{:S(2)}) collective-permute-start(bf16[480,128]{1,0:T(8,128)(2,1)} %get-tuple-element.63), channel_id=1, source_target_pairs={{0,32},{1,3},{2,34},{3,5},{4,36},{5,7},{6,38},{7,1},{8,40},{9,11},... | collective-permute-start | bytes 368648 | tf_op jit(solution)/shard_map/ppermute | solution.py:70
  86.2 11.1 %collective-permute-start.14 = (bf16[480,128]{1,0:T(8,128)(2,1)}, bf16[480,128]{1,0:T(8,128)(2,1)S(1)}, u32[]{:S(2)}, u32[]{:S(2)}) collective-permute-start(bf16[480,128]{1,0:T(8,128)(2,1)} %get-tuple-element.64), channel_id=1, source_target_pairs={{0,64},{1,5},{2,66},{3,7},{4,68},{5,1},{6,70},{7,3},{8,72},{9,13},... | collective-permute-start | bytes 368648 | tf_op jit(solution)/shard_map/ppermute | solution.py:70
  89.8 7.6 %collective-permute-start.15 = (bf16[480,128]{1,0:T(8,128)(2,1)}, bf16[480,128]{1,0:T(8,128)(2,1)S(1)}, u32[]{:S(2)}, u32[]{:S(2)}) collective-permute-start(bf16[480,128]{1,0:T(8,128)(2,1)} %get-tuple-element.65), channel_id=1, source_target_pairs={{0,96},{1,7},{2,98},{3,1},{4,100},{5,3},{6,102},{7,5},{8,104},{9,1... | collective-permute-start | bytes 368648 | tf_op jit(solution)/shard_map/ppermute | solution.py:70
  101.3 10.5 %collective-permute-start.27 = (f32[288,128]{1,0:T(8,128)S(1)}, f32[288,128]{1,0:T(8,128)S(1)}, u32[]{:S(2)}, u32[]{:S(2)}) collective-permute-start(f32[288,128]{1,0:T(8,128)S(1)} %select_add_fusion.g0), channel_id=1, source_target_pairs={{0,2},{1,3},{2,4},{3,5},{4,6},{5,7},{6,0},{7,1},{8,10},{9,11},{10,... | collective-permute-start | bytes 442376 | tf_op jit(solution)/shard_map/ppermute | solution.py:70
  105.2 8.2 %collective-permute-start.28 = (f32[288,128]{1,0:T(8,128)S(1)}, f32[288,128]{1,0:T(8,128)S(1)}, u32[]{:S(2)}, u32[]{:S(2)}) collective-permute-start(f32[288,128]{1,0:T(8,128)S(1)} %select_add_fusion.g0), channel_id=1, source_target_pairs={{0,4},{1,5},{2,6},{3,7},{4,0},{5,1},{6,2},{7,3},{8,12},{9,13},{10,... | collective-permute-start | bytes 442376 | tf_op jit(solution)/shard_map/ppermute | solution.py:70
  105.2 8.8 %collective-permute-start.29 = (f32[288,128]{1,0:T(8,128)S(1)}, f32[288,128]{1,0:T(8,128)S(1)}, u32[]{:S(2)}, u32[]{:S(2)}) collective-permute-start(f32[288,128]{1,0:T(8,128)S(1)} %select_add_fusion.g0), channel_id=1, source_target_pairs={{0,6},{1,7},{2,0},{3,1},{4,2},{5,3},{6,4},{7,5},{8,14},{9,15},{10,... | collective-permute-start | bytes 442376 | tf_op jit(solution)/shard_map/ppermute | solution.py:70
  107.4 12.3 %collective-permute-start.31 = (f32[80,384]{1,0:T(8,128)S(1)}, f32[80,384]{1,0:T(8,128)S(1)}, u32[]{:S(2)}, u32[]{:S(2)}) collective-permute-start(f32[80,384]{1,0:T(8,128)S(1)} %constant_dynamic-slice_fusion), channel_id=1, source_target_pairs={{0,1},{1,0},{2,3},{3,2},{4,5},{5,4},{6,7},{7,6},{8,9},{9,8},{10,11... | collective-permute-start | bytes 368648 | tf_op jit(solution)/shard_map/ppermute | solution.py:75
  131.9 8.2 %collective-permute-start.39 = (bf16[4,352,128]{2,1,0:T(8,128)(2,1)S(1)}, bf16[4,352,128]{2,1,0:T(8,128)(2,1)S(1)}, u32[]{:S(2)}, u32[]{:S(2)}) collective-permute-start(bf16[4,352,128]{2,1,0:T(8,128)(2,1)S(1)} %pad_maximum_fusion.1.refs_4_), channel_id=1, source_target_pairs={{0,24},{1,97},{2,26},{3,99},{4,28},{5,101},{6,30},{7,103},{8,0},{9... | collective-permute-start | bytes 1081352 | tf_op jit(solution)/shard_map/ppermute | solution.py:70
  135.2 8.7 %collective-permute-start.35 = (bf16[4,352,128]{2,1,0:T(8,128)(2,1)S(1)}, bf16[4,352,128]{2,1,0:T(8,128)(2,1)S(1)}, u32[]{:S(2)}, u32[]{:S(2)}) collective-permute-start(bf16[4,352,128]{2,1,0:T(8,128)(2,1)S(1)} %pad_maximum_fusion.refs_0_), channel_id=1, source_target_pairs={{0,8},{1,33},{2,10},{3,35},{4,12},{5,37},{6,14},{7,39},{8,16},{9,4... | collective-permute-start | bytes 1081352 | tf_op jit(solution)/shard_map/ppermute | solution.py:70
  135.3 12.5 %collective-permute-start.38 = (bf16[4,352,128]{2,1,0:T(8,128)(2,1)S(1)}, bf16[4,352,128]{2,1,0:T(8,128)(2,1)S(1)}, u32[]{:S(2)}, u32[]{:S(2)}) collective-permute-start(bf16[4,352,128]{2,1,0:T(8,128)(2,1)S(1)} %pad_maximum_fusion.1.refs_4_), channel_id=1, source_target_pairs={{0,8},{1,33},{2,10},{3,35},{4,12},{5,37},{6,14},{7,39},{8,16},{9,4... | collective-permute-start | bytes 1081352 | tf_op jit(solution)/shard_map/ppermute | solution.py:70
  135.5 12.2 %collective-permute-start.37 = (bf16[4,352,128]{2,1,0:T(8,128)(2,1)S(1)}, bf16[4,352,128]{2,1,0:T(8,128)(2,1)S(1)}, u32[]{:S(2)}, u32[]{:S(2)}) collective-permute-start(bf16[4,352,128]{2,1,0:T(8,128)(2,1)S(1)} %pad_maximum_fusion.refs_0_), channel_id=1, source_target_pairs={{0,24},{1,97},{2,26},{3,99},{4,28},{5,101},{6,30},{7,103},{8,0},{9... | collective-permute-start | bytes 1081352 | tf_op jit(solution)/shard_map/ppermute | solution.py:70
  140.1 8.6 %collective-permute-start.40 = (bf16[4,352,128]{2,1,0:T(8,128)(2,1)S(1)}, bf16[4,352,128]{2,1,0:T(8,128)(2,1)S(1)}, u32[]{:S(2)}, u32[]{:S(2)}) collective-permute-start(bf16[4,352,128]{2,1,0:T(8,128)(2,1)S(1)} %collective-permute-done.39.refs_7_), channel_id=1, source_target_pairs={{0,24},{1,97},{2,26},{3,99},{4,28},{5,101},{6,30},{7,103},{8,0},{9... | collective-permute-start | bytes 1081352 | tf_op jit(solution)/shard_map/ppermute | solution.py:70
  143.9 8.6 %collective-permute-start.36 = (bf16[4,352,128]{2,1,0:T(8,128)(2,1)S(1)}, bf16[4,352,128]{2,1,0:T(8,128)(2,1)S(1)}, u32[]{:S(2)}, u32[]{:S(2)}) collective-permute-start(bf16[4,352,128]{2,1,0:T(8,128)(2,1)S(1)} %collective-permute-done.35.refs_1_), channel_id=1, source_target_pairs={{0,8},{1,33},{2,10},{3,35},{4,12},{5,37},{6,14},{7,39},{8,16},{9,4... | collective-permute-start | bytes 1081352 | tf_op jit(solution)/shard_map/ppermute | solution.py:70
  (15 other events, 143.9 us)

commit v5 on v4

--- a/solution.py
+++ b/solution.py
@@ -32,7 +32,6 @@
 MC = RC * 3 + KR * 2
 ML = 16
 M_ALL = 2 * MP + MC
-M_HALF = M_ALL // 2
 G_ROWS = 288
 
 f32, bf16 = jnp.float32, jnp.bfloat16
@@ -592,12 +591,10 @@
     key_next = key_weight - learn_rate * (key_scale * key_ortho + weight_decay * key_weight)
     query_block = (query_next * query_factor).astype(bf16)
     key_block = (key_next * key_factor).astype(bf16)
-    half = QR // 2
-    for i in range(2):
-        start = i * M_HALF
-        to[pl.ds(start, QR), :] = query_block[:, i * 128 : (i + 1) * 128]
-        to[pl.ds(start + QR, half), :] = query_block[i * half : (i + 1) * half, 256:]
-        to[pl.ds(start + QR + half, KR), :] = key_block[:, i * 128 : (i + 1) * 128]
+    for lane in range(3):
+        to[pl.ds(lane * QR, QR), :] = query_block[:, lane * 128 : (lane + 1) * 128]
+    for lane in range(2):
+        to[pl.ds(3 * QR + lane * KR, KR), :] = key_block[:, lane * 128 : (lane + 1) * 128]
 
 
 def update(where, own, other, peak, query_moment, key_moment, query_weight, key_weight):
@@ -611,35 +608,63 @@
     )(where, own, other, peak, query_moment, key_moment, query_weight, key_weight)
 
 
-def assemble_kernel(where, *refs):
+def gathered_pieces(where, far, i, stack, query_out, key_out):
     z, x, _, core = read(where)
-    stacks, (query_out, key_out) = (refs[:N], refs[N : 2 * N]), refs[2 * N :]
-    half = QR // 2
-    for far in range(N):
-
-        @pl.loop(0, N)
-        def _(near):
-            back_z = jnp.where(core == 0, near, far)
-            back_x = jnp.where(core == 0, far, near)
-            zz, xx = (z + N - back_z) % N, (x + N - back_x) % N
-            for i in range(2):
-                stack = stacks[i][far]
-                query_out[:, columns(zz, xx, QC, i)] = stack[near, pl.ds(0, QR), :]
-                query_out[pl.ds(i * half, half), columns(zz, xx, QC, 2)] = stack[
-                    near, pl.ds(QR, half), :
-                ]
-                key_out[:, columns(zz, xx, KC, i)] = stack[near, pl.ds(QR + half, KR), :]
+    for j in range(2):
+        near = 2 * i + j
+        back_z, back_x = jnp.where(core == 0, near, far), jnp.where(core == 0, far, near)
+        zz, xx = (z + N - back_z) % N, (x + N - back_x) % N
+        for lane in range(3):
+            rows = pl.ds(lane * QR, QR)
+            yield stack.at[j, rows, :], query_out.at[:, columns(zz, xx, QC, lane)]
+        for lane in range(2):
+            rows = pl.ds(3 * QR + lane * KR, KR)
+            yield stack.at[j, rows, :], key_out.at[:, columns(zz, xx, KC, lane)]
+
+
+def assemble_kernel(where, f0, f1, f3, s0, s1, s3, query_out, key_out):
+    for i, stacks in enumerate(((f0, f1, f3), (s0, s1, s3))):
+        for far, stack in zip((0, 1, 3), stacks):
+            for source, to in gathered_pieces(where, far, i, stack, query_out, key_out):
+                to[...] = source[...]
+
+
+RESULT = (pltpu.HBM((QR, N * N * QC), bf16), pltpu.HBM((KR, N * N * KC), bf16))
 
 
 def assemble(where, first, second):
     return pl.pallas_call(
         assemble_kernel,
-        out_shape=(out((QR, N * N * QC), bf16), out((KR, N * N * KC), bf16)),
-        in_specs=[SMEM] + [VMEM] * (2 * N),
+        out_shape=RESULT,
+        in_specs=[SMEM] + [VMEM] * 6,
         out_specs=(VMEM, VMEM),
         compiler_params=params(16),
         name="assemble",
     )(where, *first, *second)
+
+
+def finish_kernel(where, query_in, key_in, first, second, query_out, key_out, sems):
+    copies = []
+    for i, stack in enumerate((first, second)):
+        for source, to in gathered_pieces(where, 2, i, stack, query_out, key_out):
+            copies.append(pltpu.make_async_copy(source, to, sems.at[len(copies)]))
+    for copy in copies:
+        copy.start()
+    for copy in copies:
+        copy.wait()
+
+
+def finish(where, query_out, key_out, first, second):
+    return pl.pallas_call(
+        finish_kernel,
+        out_shape=RESULT,
+        in_specs=[SMEM, HBM, HBM, VMEM, VMEM],
+        out_specs=(HBM, HBM),
+        scratch_shapes=[pltpu.SemaphoreType.DMA((20,))],
+        input_output_aliases={1: 0, 2: 1},
+        compiler_params=params(4),
+        name="finish",
+    )(where, *in_hbm(query_out, key_out), first, second)
 
 
 def on_device(grad_query, grad_key, query_weight, key_weight, query_moment, key_moment, max_logits):
@@ -705,15 +730,14 @@
     def along(stack, by):
         return shift(stack, ("x", "z"), (by, by))
 
-    first, second = (jnp.stack([b[i * M_HALF : (i + 1) * M_HALF] for b in blocks]) for i in range(2))
+    first, second = jnp.stack(blocks[:2]), jnp.stack(blocks[2:])
     first_back, second_ahead = along(first, 1), along(second, -1)
     second_back, first_ahead = along(second, 1), along(first, -1)
     first_far, second_far = along(first_back, 1), along(second_ahead, -1)
     query_out, key_out = assemble(
-        where,
-        (first, first_back, first_far, first_ahead),
-        (second, second_back, second_far, second_ahead),
-    )
+        where, (first, first_back, first_ahead), (second, second_back, second_ahead)
+    )
+    query_out, key_out = finish(where, query_out, key_out, first_far, second_far)
     return (query_out, key_out, new_query_moment, new_key_moment)
 
 

time: 156 us -> 153 us (0.981)
  waiting for transfers between devices: 52.6 us -> 48.1 us
    ppermute x33, waiting for transfers between devices: 49.8 us -> 45.3 us  [shift(): return lax.ppermute(array, AXES, pairs)]
    pallas_call x1 -> x2, Pallas kernels: 2.87 us -> 4.25 us  [the longest x1 2.69 us: assemble(): pl.pallas_call(assemble_kernel, out_shape=RESULT, in_specs=[SMEM] + [VMEM...]
  transfers between devices with their start and end apart: 41 -> 41, of which waited for: 24 -> 22; matrix products, arithmetic and copies ran while one was open for 1% -> 1% of each run, Pallas kernels for 19% -> 22%
where the time goes in v5:
time: 153 us; the launch traced here: 152 us
  starting transfers between devices  59.8 us (39%)
  waiting for transfers between devices  48.1 us (31%)
  Pallas kernels  39.9 us (26%)
  between operations  1.81 us (1%)
    ppermute x33, starting transfers between devices, shift(): return lax.ppermute(array, AXES, pairs)  57 us
    ppermute x33, waiting for transfers between devices, shift(): return lax.ppermute(array, AXES, pairs)  45.3 us
    pallas_call x7, Pallas kernels, local(): pl.pallas_call(functools.partial(local_kernel, sum_step, send_step), out_...  20.7 us
    pallas_call x1, Pallas kernels, chain(): pl.pallas_call(chain_kernel, out_shape=out((512, 128), f32), in_specs=[VM...  5.56 us
  transfers between devices with their start and end apart: 41, of which 22 were waited for; matrix products, arithmetic and copies ran while one was open for 1% of the time, Pallas kernels for 22%

profile of v5, /device:TPU:8, one launch (start us, length us, event | category | flops | bytes accessed | tf_op | source)
XLA Modules:
  0.0 152.3 jit_solution(1141362647819361789)
XLA Ops:
  0.7 2.7 %local_sum_None_send_1.1 = bf16[4,4,720,128]{3,2,1,0:T(8,128)(2,1)S(1)} custom-call(s32[4]{0:T(128)S(1)} %pad_add_fusion.where, bf16[4,2,192,6144]{3,2,1,0:T(8,128)(2,1)} %bitcast.12, bf16[4,2,64,4096]{3,2,1,0:T(8,128)(2,1)} %bitcast.19, f32[1,32]{1,0:T(1,128)} %logits.13), custom_call_target="tpu_custom_call" | custom-call | tf_op jit(solution)/shard_map/local_sum_None_send_1/pallas_call | solution.py:288
  3.5 2.7 %local_sum_None_send_2.1 = bf16[4,4,720,128]{3,2,1,0:T(8,128)(2,1)S(1)} custom-call(s32[4]{0:T(128)S(1)} %pad_add_fusion.where, bf16[4,2,192,6144]{3,2,1,0:T(8,128)(2,1)} %bitcast.13, bf16[4,2,64,4096]{3,2,1,0:T(8,128)(2,1)} %bitcast.20, f32[1,32]{1,0:T(1,128)} %logits.13), custom_call_target="tpu_custom_call" | custom-call | tf_op jit(solution)/shard_map/local_sum_None_send_2/pallas_call | solution.py:288
  6.8 2.7 %local_sum_None_send_3.1 = bf16[4,4,720,128]{3,2,1,0:T(8,128)(2,1)S(1)} custom-call(s32[4]{0:T(128)S(1)} %pad_add_fusion.where, bf16[4,2,192,6144]{3,2,1,0:T(8,128)(2,1)} %bitcast.14, bf16[4,2,64,4096]{3,2,1,0:T(8,128)(2,1)} %bitcast.21, f32[1,32]{1,0:T(1,128)} %logits.13), custom_call_target="tpu_custom_call" | custom-call | tf_op jit(solution)/shard_map/local_sum_None_send_3/pallas_call | solution.py:288
  9.6 2.9 %local_sum_1_send_None.1 = (bf16[4,4,240,128]{3,2,1,0:T(8,128)(2,1)S(1)}, bf16[4,4,240,128]{3,2,1,0:T(8,128)(2,1)S(1)}, bf16[4,4,240,128]{3,2,1,0:T(8,128)(2,1)S(1)}) custom-call(s32[4]{0:T(128)S(1)} %pad_add_fusion.where, bf16[4,2,192,6144]{3,2,1,0:T(8,128)(2,1)} %bitcast.15, bf16[4,2,64,4096]{3,2,1,0:T(8,128)(2,1)} %bitcast.22, f32[1,32]{1,0:T(1,128)} %logits.13, ...), custom_call_target="tpu_custom_call" | custom-call | tf_op jit(solution)/shard_map/local_sum_1_send_None/pallas_call | solution.py:288
  12.5 2.8 %collective-permute-start.7 = (bf16[4,4,240,128]{3,2,1,0:T(8,128)(2,1)S(1)}, bf16[4,4,240,128]{3,2,1,0:T(8,128)(2,1)S(1)}, u32[]{:S(2)}, u32[]{:S(2)}) collective-permute-start(bf16[4,4,240,128]{3,2,1,0:T(8,128)(2,1)S(1)} %get-tuple-element.59), channel_id=1, source_target_pairs={{0,24},{1,97},{2,26},{3,99},{4,28},{5,101},{6,30},{7,103},{8,0},{9... | collective-permute-start | bytes 2949128 | tf_op jit(solution)/shard_map/ppermute | solution.py:69
  15.4 3.8 %local_sum_2_send_4.1 = (bf16[4,4,240,128]{3,2,1,0:T(8,128)(2,1)S(1)}, bf16[4,4,240,128]{3,2,1,0:T(8,128)(2,1)S(1)}, bf16[4,4,240,128]{3,2,1,0:T(8,128)(2,1)S(1)}, bf16[4,4,720,128]{3,2,1,0:T(8,128)(2,1)S(1)}) custom-call(s32[4]{0:T(128)S(1)} %pad_add_fusion.where, bf16[4,2,192,6144]{3,2,1,0:T(8,128)(2,1)} %bitcast.16, bf16[4,2,64,4096]{3,2,1,0:T(8,128)(2,1)} %bitcast.23, ...), custom_call_target="tpu_custom_call" | custom-call | tf_op jit(solution)/shard_map/local_sum_2_send_4/pallas_call | solution.py:288
  22.5 4.5 %collective-permute-done.7 = bf16[4,4,240,128]{3,2,1,0:T(8,128)(2,1)S(1)} collective-permute-done((bf16[4,4,240,128]{3,2,1,0:T(8,128)(2,1)S(1)}, bf16[4,4,240,128]{3,2,1,0:T(8,128)(2,1)S(1)}, u32[]{:S(2)}, u32[]{:S(2)}) %collective-permute-start.7) | collective-permute-done | bytes 983072 | tf_op jit(solution)/shard_map/ppermute | solution.py:69
  27.2 3.8 %collective-permute-start.8 = (bf16[4,4,240,128]{3,2,1,0:T(8,128)(2,1)S(1)}, bf16[4,4,240,128]{3,2,1,0:T(8,128)(2,1)S(1)}, u32[]{:S(2)}, u32[]{:S(2)}) collective-permute-start(bf16[4,4,240,128]{3,2,1,0:T(8,128)(2,1)S(1)} %add_convert_fusion.1), channel_id=1, source_target_pairs={{0,24},{1,97},{2,26},{3,99},{4,28},{5,101},{6,30},{7,103},{8,0},{9... | collective-permute-start | bytes 2949128 | tf_op jit(solution)/shard_map/ppermute | solution.py:69
  31.4 2.9 %local_sum_3_send_None.1 = (bf16[4,4,240,128]{3,2,1,0:T(8,128)(2,1)S(1)}, bf16[4,4,240,128]{3,2,1,0:T(8,128)(2,1)S(1)}, bf16[4,4,240,128]{3,2,1,0:T(8,128)(2,1)S(1)}) custom-call(s32[4]{0:T(128)S(1)} %pad_add_fusion.where, bf16[4,2,192,6144]{3,2,1,0:T(8,128)(2,1)} %bitcast.17, bf16[4,2,64,4096]{3,2,1,0:T(8,128)(2,1)} %bitcast.24, f32[1,32]{1,0:T(1,128)} %logits.13, ...), custom_call_target="tpu_custom_call" | custom-call | tf_op jit(solution)/shard_map/local_sum_3_send_None/pallas_call | solution.py:288
  37.1 5.6 %collective-permute-done.8 = bf16[4,4,240,128]{3,2,1,0:T(8,128)(2,1)S(1)} collective-permute-done((bf16[4,4,240,128]{3,2,1,0:T(8,128)(2,1)S(1)}, bf16[4,4,240,128]{3,2,1,0:T(8,128)(2,1)S(1)}, u32[]{:S(2)}, u32[]{:S(2)}) %collective-permute-start.8) | collective-permute-done | bytes 983072 | tf_op jit(solution)/shard_map/ppermute | solution.py:69
  42.9 3.8 %collective-permute-start.9 = (bf16[4,4,240,128]{3,2,1,0:T(8,128)(2,1)S(1)}, bf16[4,4,240,128]{3,2,1,0:T(8,128)(2,1)S(1)}, u32[]{:S(2)}, u32[]{:S(2)}) collective-permute-start(bf16[4,4,240,128]{3,2,1,0:T(8,128)(2,1)S(1)} %add_convert_fusion), channel_id=1, source_target_pairs={{0,24},{1,97},{2,26},{3,99},{4,28},{5,101},{6,30},{7,103},{8,0},{9... | collective-permute-start | bytes 2949128 | tf_op jit(solution)/shard_map/ppermute | solution.py:69
  47.0 2.6 %collective-permute-done.17.second = bf16[4,4,240,128]{3,2,1,0:T(8,128)(2,1)S(1)} collective-permute-done((bf16[4,4,240,128]{3,2,1,0:T(8,128)(2,1)S(1)}, bf16[4,4,240,128]{3,2,1,0:T(8,128)(2,1)S(1)}, u32[]{:S(2)}, u32[]{:S(2)}) %collective-permute-start.17) | collective-permute-done | bytes 983072 | tf_op jit(solution)/shard_map/ppermute | solution.py:69
  51.6 2.9 %local_sum_4_send_None.1 = (bf16[4,4,240,128]{3,2,1,0:T(8,128)(2,1)S(1)}, bf16[4,4,240,128]{3,2,1,0:T(8,128)(2,1)S(1)}, bf16[4,4,240,128]{3,2,1,0:T(8,128)(2,1)S(1)}) custom-call(s32[4]{0:T(128)S(1)} %pad_add_fusion.where, bf16[4,2,192,6144]{3,2,1,0:T(8,128)(2,1)} %bitcast.18, bf16[4,2,64,4096]{3,2,1,0:T(8,128)(2,1)} %bitcast.25, f32[1,32]{1,0:T(1,128)} %logits.13, ...), custom_call_target="tpu_custom_call" | custom-call | tf_op jit(solution)/shard_map/local_sum_4_send_None/pallas_call | solution.py:288
  54.6 3.7 %collective-permute-done.9.m1 = bf16[4,4,240,128]{3,2,1,0:T(8,128)(2,1)S(1)} collective-permute-done((bf16[4,4,240,128]{3,2,1,0:T(8,128)(2,1)S(1)}, bf16[4,4,240,128]{3,2,1,0:T(8,128)(2,1)S(1)}, u32[]{:S(2)}, u32[]{:S(2)}) %collective-permute-start.9) | collective-permute-done | bytes 983072 | tf_op jit(solution)/shard_map/ppermute | solution.py:69
  58.3 4.0 %collective-permute-done.6.p1 = bf16[4,4,240,128]{3,2,1,0:T(8,128)(2,1)S(1)} collective-permute-done((bf16[4,4,240,128]{3,2,1,0:T(8,128)(2,1)S(1)}, bf16[4,4,240,128]{3,2,1,0:T(8,128)(2,1)S(1)}, u32[]{:S(2)}, u32[]{:S(2)}) %collective-permute-start.6) | collective-permute-done | bytes 983072 | tf_op jit(solution)/shard_map/ppermute | solution.py:69
  66.8 2.4 %collective-permute-start.12 = (bf16[4,480,128]{2,1,0:T(8,128)(2,1)}, bf16[4,480,128]{2,1,0:T(8,128)(2,1)S(1)}, u32[]{:S(2)}, u32[]{:S(2)}) collective-permute-start(bf16[4,480,128]{2,1,0:T(8,128)(2,1)} %get-tuple-element.63), channel_id=1, source_target_pairs={{0,6},{1,25},{2,0},{3,27},{4,2},{5,29},{6,4},{7,31},{8,14},{9,1},{... | collective-permute-start | bytes 1474568 | tf_op jit(solution)/shard_map/ppermute | solution.py:69
  72.9 3.6 %collective-permute-start.20 = (bf16[4,240,128]{2,1,0:T(8,128)(2,1)}, bf16[4,240,128]{2,1,0:T(8,128)(2,1)S(1)}, u32[]{:S(2)}, u32[]{:S(2)}) collective-permute-start(bf16[4,240,128]{2,1,0:T(8,128)(2,1)} %get-tuple-element.76), channel_id=1, source_target_pairs={{0,64},{1,65},{2,66},{3,67},{4,68},{5,69},{6,70},{7,71},{8,72},{9,... | collective-permute-start | bytes 737288 | tf_op jit(solution)/shard_map/ppermute | solution.py:69
  86.2 3.6 %collective-permute-start.14 = (bf16[480,128]{1,0:T(8,128)(2,1)}, bf16[480,128]{1,0:T(8,128)(2,1)S(1)}, u32[]{:S(2)}, u32[]{:S(2)}) collective-permute-start(bf16[480,128]{1,0:T(8,128)(2,1)} %get-tuple-element.66), channel_id=1, source_target_pairs={{0,64},{1,5},{2,66},{3,7},{4,68},{5,1},{6,70},{7,3},{8,72},{9,13},... | collective-permute-start | bytes 368648 | tf_op jit(solution)/shard_map/ppermute | solution.py:69
  91.4 2.3 %collective-permute-start.24 = (bf16[240,128]{1,0:T(8,128)(2,1)S(1)}, bf16[240,128]{1,0:T(8,128)(2,1)S(1)}, u32[]{:S(2)}, u32[]{:S(2)}) collective-permute-start(bf16[240,128]{1,0:T(8,128)(2,1)S(1)} %get-tuple-element.81), channel_id=1, source_target_pairs={{0,24},{1,25},{2,26},{3,27},{4,28},{5,29},{6,30},{7,31},{8,0},{9,1... | collective-permute-start | bytes 184328 | tf_op jit(solution)/shard_map/ppermute | solution.py:69
  93.7 2.5 %collective-permute-done.23.c2 = bf16[240,128]{1,0:T(8,128)(2,1)S(1)} collective-permute-done((bf16[240,128]{1,0:T(8,128)(2,1)S(1)}, bf16[240,128]{1,0:T(8,128)(2,1)S(1)}, u32[]{:S(2)}, u32[]{:S(2)}) %collective-permute-start.23) | collective-permute-done | bytes 61472 | tf_op jit(solution)/shard_map/ppermute | solution.py:69
  101.4 3.9 %collective-permute-start.27 = (f32[288,128]{1,0:T(8,128)S(1)}, f32[288,128]{1,0:T(8,128)S(1)}, u32[]{:S(2)}, u32[]{:S(2)}) collective-permute-start(f32[288,128]{1,0:T(8,128)S(1)} %select_add_fusion.g0), channel_id=1, source_target_pairs={{0,2},{1,3},{2,4},{3,5},{4,6},{5,7},{6,0},{7,1},{8,10},{9,11},{10,... | collective-permute-start | bytes 442376 | tf_op jit(solution)/shard_map/ppermute | solution.py:69
  105.3 2.2 %collective-permute-start.29 = (f32[288,128]{1,0:T(8,128)S(1)}, f32[288,128]{1,0:T(8,128)S(1)}, u32[]{:S(2)}, u32[]{:S(2)}) collective-permute-start(f32[288,128]{1,0:T(8,128)S(1)} %select_add_fusion.g0), channel_id=1, source_target_pairs={{0,6},{1,7},{2,0},{3,1},{4,2},{5,3},{6,4},{7,5},{8,14},{9,15},{10,... | collective-permute-start | bytes 442376 | tf_op jit(solution)/shard_map/ppermute | solution.py:69
  107.5 4.3 %collective-permute-done.27.g1 = f32[288,128]{1,0:T(8,128)S(1)} collective-permute-done((f32[288,128]{1,0:T(8,128)S(1)}, f32[288,128]{1,0:T(8,128)S(1)}, u32[]{:S(2)}, u32[]{:S(2)}) %collective-permute-start.27) | collective-permute-done | bytes 147488 | tf_op jit(solution)/shard_map/ppermute | solution.py:69
  114.0 5.6 %newton_schulz_polynomial.1.own = f32[512,128]{1,0:T(8,128)S(1)} custom-call(f32[288,128]{1,0:T(8,128)S(1)} %select_add_fusion.g0, f32[288,128]{1,0:T(8,128)S(1)} %collective-permute-done.27.g1, f32[288,128]{1,0:T(8,128)S(1)} %collective-permute-done.28.g2, f32[288,128]{1,0:T(8,128)S(1)} %collective-permute-done.29.g3), custom_call_target="tpu_custom_call" | custom-call | tf_op jit(solution)/shard_map/newton_schulz_polynomial/pallas_call | solution.py:538
  123.2 2.9 %collective-permute-start.35 = (bf16[704,128]{1,0:T(8,128)(2,1)S(1)}, bf16[704,128]{1,0:T(8,128)(2,1)S(1)}, u32[]{:S(2)}, u32[]{:S(2)}) collective-permute-start(bf16[704,128]{1,0:T(8,128)(2,1)S(1)} %update.1), channel_id=1, source_target_pairs={{0,64},{1,17},{2,66},{3,19},{4,68},{5,21},{6,70},{7,23},{8,72},{9,... | collective-permute-start | bytes 540680 | tf_op jit(solution)/shard_map/ppermute | solution.py:69
  127.9 2.4 %collective-permute-done.35 = bf16[704,128]{1,0:T(8,128)(2,1)S(1)} collective-permute-done((bf16[704,128]{1,0:T(8,128)(2,1)S(1)}, bf16[704,128]{1,0:T(8,128)(2,1)S(1)}, u32[]{:S(2)}, u32[]{:S(2)}) %collective-permute-start.35) | collective-permute-done | bytes 180256 | tf_op jit(solution)/shard_map/ppermute | solution.py:69
  130.3 2.9 %collective-permute-start.38 = (bf16[2,704,128]{2,1,0:T(8,128)(2,1)S(1)}, bf16[2,704,128]{2,1,0:T(8,128)(2,1)S(1)}, u32[]{:S(2)}, u32[]{:S(2)}) collective-permute-start(bf16[2,704,128]{2,1,0:T(8,128)(2,1)S(1)} %pad_maximum_fusion.1.s0), channel_id=1, source_target_pairs={{0,24},{1,97},{2,26},{3,99},{4,28},{5,101},{6,30},{7,103},{8,0},{9... | collective-permute-start | bytes 1081352 | tf_op jit(solution)/shard_map/ppermute | solution.py:69
  135.3 2.2 %collective-permute-start.34 = (bf16[2,704,128]{2,1,0:T(8,128)(2,1)S(1)}, bf16[2,704,128]{2,1,0:T(8,128)(2,1)S(1)}, u32[]{:S(2)}, u32[]{:S(2)}) collective-permute-start(bf16[2,704,128]{2,1,0:T(8,128)(2,1)S(1)} %pad_maximum_fusion.f0), channel_id=1, source_target_pairs={{0,24},{1,97},{2,26},{3,99},{4,28},{5,101},{6,30},{7,103},{8,0},{9... | collective-permute-start | bytes 1081352 | tf_op jit(solution)/shard_map/ppermute | solution.py:69
  138.1 3.7 %collective-permute-start.40 = (bf16[2,704,128]{2,1,0:T(8,128)(2,1)S(1)}, bf16[2,704,128]{2,1,0:T(8,128)(2,1)S(1)}, u32[]{:S(2)}, u32[]{:S(2)}) collective-permute-start(bf16[2,704,128]{2,1,0:T(8,128)(2,1)S(1)} %collective-permute-done.38.s3), channel_id=1, source_target_pairs={{0,24},{1,97},{2,26},{3,99},{4,28},{5,101},{6,30},{7,103},{8,0},{9... | collective-permute-start | bytes 1081352 | tf_op jit(solution)/shard_map/ppermute | solution.py:69
  142.0 3.9 %collective-permute-done.37.s1 = bf16[2,704,128]{2,1,0:T(8,128)(2,1)S(1)} collective-permute-done((bf16[2,704,128]{2,1,0:T(8,128)(2,1)S(1)}, bf16[2,704,128]{2,1,0:T(8,128)(2,1)S(1)}, u32[]{:S(2)}, u32[]{:S(2)}) %collective-permute-start.37) | collective-permute-done | bytes 360480 | tf_op jit(solution)/shard_map/ppermute | solution.py:69
  145.8 2.7 %assemble.1 = (bf16[192,6144]{1,0:T(8,128)(2,1)}, bf16[64,4096]{1,0:T(8,128)(2,1)}) custom-call(s32[4]{0:T(128)S(1)} %pad_add_fusion.where, bf16[2,704,128]{2,1,0:T(8,128)(2,1)S(1)} %pad_maximum_fusion.f0, bf16[2,704,128]{2,1,0:T(8,128)(2,1)S(1)} %collective-permute-done.33.f1, bf16[2,704,128]{2,1,0:T(8,128)(2,1)S(1)} %collective-permute-done.34.f3, ...), custom_call_target="tpu_custom_call" | custom-call | tf_op jit(solution)/shard_map/assemble/pallas_call | solution.py:636
  148.5 2.1 %collective-permute-done.39.first = bf16[2,704,128]{2,1,0:T(8,128)(2,1)S(1)} collective-permute-done((bf16[2,704,128]{2,1,0:T(8,128)(2,1)S(1)}, bf16[2,704,128]{2,1,0:T(8,128)(2,1)S(1)}, u32[]{:S(2)}, u32[]{:S(2)}) %collective-permute-start.39) | collective-permute-done | bytes 360480 | tf_op jit(solution)/shard_map/ppermute | solution.py:69
  (95 shorter events, 46.1 us)
Async XLA Ops:
  6.2 9.1 %collective-permute-start.1 = (bf16[4,4,720,128]{3,2,1,0:T(8,128)(2,1)S(1)}, bf16[4,4,720,128]{3,2,1,0:T(8,128)(2,1)S(1)}, u32[]{:S(2)}, u32[]{:S(2)}) collective-permute-start(bf16[4,4,720,128]{3,2,1,0:T(8,128)(2,1)S(1)} %local_sum_None_send_2.1), channel_id=1, source_target_pairs={{0,1},{1,0},{2,3},{3,2},{4,5},{5,4},{6,7},{7,6},{8,9},{9,8},{10,11... | collective-permute-start | bytes 8847368 | tf_op jit(solution)/shard_map/ppermute | solution.py:74
  9.5 21.9 %collective-permute-start.3 = (bf16[4,4,720,128]{3,2,1,0:T(8,128)(2,1)S(1)}, bf16[4,4,720,128]{3,2,1,0:T(8,128)(2,1)S(1)}, u32[]{:S(2)}, u32[]{:S(2)}) collective-permute-start(bf16[4,4,720,128]{3,2,1,0:T(8,128)(2,1)S(1)} %local_sum_None_send_3.1), channel_id=1, source_target_pairs={{0,1},{1,0},{2,3},{3,2},{4,5},{5,4},{6,7},{7,6},{8,9},{9,8},{10,11... | collective-permute-start | bytes 8847368 | tf_op jit(solution)/shard_map/ppermute | solution.py:74
  12.5 14.4 %collective-permute-start.7 = (bf16[4,4,240,128]{3,2,1,0:T(8,128)(2,1)S(1)}, bf16[4,4,240,128]{3,2,1,0:T(8,128)(2,1)S(1)}, u32[]{:S(2)}, u32[]{:S(2)}) collective-permute-start(bf16[4,4,240,128]{3,2,1,0:T(8,128)(2,1)S(1)} %get-tuple-element.59), channel_id=1, source_target_pairs={{0,24},{1,97},{2,26},{3,99},{4,28},{5,101},{6,30},{7,103},{8,0},{9... | collective-permute-start | bytes 2949128 | tf_op jit(solution)/shard_map/ppermute | solution.py:69
  15.4 15.6 %collective-permute-start.4 = (bf16[4,4,240,128]{3,2,1,0:T(8,128)(2,1)S(1)}, bf16[4,4,240,128]{3,2,1,0:T(8,128)(2,1)S(1)}, u32[]{:S(2)}, u32[]{:S(2)}) collective-permute-start(bf16[4,4,240,128]{3,2,1,0:T(8,128)(2,1)S(1)} %get-tuple-element.48), channel_id=1, source_target_pairs={{0,8},{1,33},{2,10},{3,35},{4,12},{5,37},{6,14},{7,39},{8,16},{9,4... | collective-permute-start | bytes 2949128 | tf_op jit(solution)/shard_map/ppermute | solution.py:69
  19.2 32.4 %collective-permute-start.2 = (bf16[4,4,720,128]{3,2,1,0:T(8,128)(2,1)S(1)}, bf16[4,4,720,128]{3,2,1,0:T(8,128)(2,1)S(1)}, u32[]{:S(2)}, u32[]{:S(2)}) collective-permute-start(bf16[4,4,720,128]{3,2,1,0:T(8,128)(2,1)S(1)} %get-tuple-element.51), channel_id=1, source_target_pairs={{0,1},{1,0},{2,3},{3,2},{4,5},{5,4},{6,7},{7,6},{8,9},{9,8},{10,11... | collective-permute-start | bytes 8847368 | tf_op jit(solution)/shard_map/ppermute | solution.py:74
  20.9 14.1 %collective-permute-start.16 = (bf16[4,4,240,128]{3,2,1,0:T(8,128)(2,1)S(1)}, bf16[4,4,240,128]{3,2,1,0:T(8,128)(2,1)S(1)}, u32[]{:S(2)}, u32[]{:S(2)}) collective-permute-start(bf16[4,4,240,128]{3,2,1,0:T(8,128)(2,1)S(1)} %get-tuple-element.73), channel_id=1, source_target_pairs={{0,2},{1,7},{2,4},{3,1},{4,6},{5,3},{6,0},{7,5},{8,10},{9,15},{10,... | collective-permute-start | bytes 2949128 | tf_op jit(solution)/shard_map/ppermute | solution.py:69
  27.2 15.4 %collective-permute-start.8 = (bf16[4,4,240,128]{3,2,1,0:T(8,128)(2,1)S(1)}, bf16[4,4,240,128]{3,2,1,0:T(8,128)(2,1)S(1)}, u32[]{:S(2)}, u32[]{:S(2)}) collective-permute-start(bf16[4,4,240,128]{3,2,1,0:T(8,128)(2,1)S(1)} %add_convert_fusion.1), channel_id=1, source_target_pairs={{0,24},{1,97},{2,26},{3,99},{4,28},{5,101},{6,30},{7,103},{8,0},{9... | collective-permute-start | bytes 2949128 | tf_op jit(solution)/shard_map/ppermute | solution.py:69
  31.3 15.4 %collective-permute-start.5 = (bf16[4,4,240,128]{3,2,1,0:T(8,128)(2,1)S(1)}, bf16[4,4,240,128]{3,2,1,0:T(8,128)(2,1)S(1)}, u32[]{:S(2)}, u32[]{:S(2)}) collective-permute-start(bf16[4,4,240,128]{3,2,1,0:T(8,128)(2,1)S(1)} %add_convert_fusion.3), channel_id=1, source_target_pairs={{0,8},{1,33},{2,10},{3,35},{4,12},{5,37},{6,14},{7,39},{8,16},{9,4... | collective-permute-start | bytes 2949128 | tf_op jit(solution)/shard_map/ppermute | solution.py:69
  35.5 14.2 %collective-permute-start.17 = (bf16[4,4,240,128]{3,2,1,0:T(8,128)(2,1)S(1)}, bf16[4,4,240,128]{3,2,1,0:T(8,128)(2,1)S(1)}, u32[]{:S(2)}, u32[]{:S(2)}) collective-permute-start(bf16[4,4,240,128]{3,2,1,0:T(8,128)(2,1)S(1)} %add_c.2), channel_id=1, source_target_pairs={{0,2},{1,7},{2,4},{3,1},{4,6},{5,3},{6,0},{7,5},{8,10},{9,15},{10,... | collective-permute-start | bytes 2949128 | tf_op jit(solution)/shard_map/ppermute | solution.py:69
  42.9 15.4 %collective-permute-start.9 = (bf16[4,4,240,128]{3,2,1,0:T(8,128)(2,1)S(1)}, bf16[4,4,240,128]{3,2,1,0:T(8,128)(2,1)S(1)}, u32[]{:S(2)}, u32[]{:S(2)}) collective-permute-start(bf16[4,4,240,128]{3,2,1,0:T(8,128)(2,1)S(1)} %add_convert_fusion), channel_id=1, source_target_pairs={{0,24},{1,97},{2,26},{3,99},{4,28},{5,101},{6,30},{7,103},{8,0},{9... | collective-permute-start | bytes 2949128 | tf_op jit(solution)/shard_map/ppermute | solution.py:69
  46.9 15.4 %collective-permute-start.6 = (bf16[4,4,240,128]{3,2,1,0:T(8,128)(2,1)S(1)}, bf16[4,4,240,128]{3,2,1,0:T(8,128)(2,1)S(1)}, u32[]{:S(2)}, u32[]{:S(2)}) collective-permute-start(bf16[4,4,240,128]{3,2,1,0:T(8,128)(2,1)S(1)} %add_convert_fusion.2), channel_id=1, source_target_pairs={{0,8},{1,33},{2,10},{3,35},{4,12},{5,37},{6,14},{7,39},{8,16},{9,4... | collective-permute-start | bytes 2949128 | tf_op jit(solution)/shard_map/ppermute | solution.py:69
  50.0 19.2 %collective-permute-start.18 = (bf16[4,4,240,128]{3,2,1,0:T(8,128)(2,1)S(1)}, bf16[4,4,240,128]{3,2,1,0:T(8,128)(2,1)S(1)}, u32[]{:S(2)}, u32[]{:S(2)}) collective-permute-start(bf16[4,4,240,128]{3,2,1,0:T(8,128)(2,1)S(1)} %add_c.3), channel_id=1, source_target_pairs={{0,2},{1,7},{2,4},{3,1},{4,6},{5,3},{6,0},{7,5},{8,10},{9,15},{10,... | collective-permute-start | bytes 2949128 | tf_op jit(solution)/shard_map/ppermute | solution.py:69
  64.3 12.2 %collective-permute-start.10 = (bf16[4,480,128]{2,1,0:T(8,128)(2,1)S(1)}, bf16[4,480,128]{2,1,0:T(8,128)(2,1)S(1)}, u32[]{:S(2)}, u32[]{:S(2)}) collective-permute-start(bf16[4,480,128]{2,1,0:T(8,128)(2,1)S(1)} %get-tuple-element.61), channel_id=1, source_target_pairs={{0,2},{1,9},{2,4},{3,11},{4,6},{5,13},{6,0},{7,15},{8,10},{9,17},{... | collective-permute-start | bytes 1474568 | tf_op jit(solution)/shard_map/ppermute | solution.py:69
  65.9 13.5 %collective-permute-start.11 = (bf16[4,480,128]{2,1,0:T(8,128)(2,1)}, bf16[4,480,128]{2,1,0:T(8,128)(2,1)S(1)}, u32[]{:S(2)}, u32[]{:S(2)}) collective-permute-start(bf16[4,480,128]{2,1,0:T(8,128)(2,1)} %get-tuple-element.62), channel_id=1, source_target_pairs={{0,4},{1,17},{2,6},{3,19},{4,0},{5,21},{6,2},{7,23},{8,12},{9,25},... | collective-permute-start | bytes 1474568 | tf_op jit(solution)/shard_map/ppermute | solution.py:69
  66.8 14.3 %collective-permute-start.12 = (bf16[4,480,128]{2,1,0:T(8,128)(2,1)}, bf16[4,480,128]{2,1,0:T(8,128)(2,1)S(1)}, u32[]{:S(2)}, u32[]{:S(2)}) collective-permute-start(bf16[4,480,128]{2,1,0:T(8,128)(2,1)} %get-tuple-element.63), channel_id=1, source_target_pairs={{0,6},{1,25},{2,0},{3,27},{4,2},{5,29},{6,4},{7,31},{8,14},{9,1},{... | collective-permute-start | bytes 1474568 | tf_op jit(solution)/shard_map/ppermute | solution.py:69
  71.0 11.6 %collective-permute-start.19 = (bf16[4,240,128]{2,1,0:T(8,128)(2,1)}, bf16[4,240,128]{2,1,0:T(8,128)(2,1)S(1)}, u32[]{:S(2)}, u32[]{:S(2)}) collective-permute-start(bf16[4,240,128]{2,1,0:T(8,128)(2,1)} %get-tuple-element.75), channel_id=1, source_target_pairs={{0,32},{1,33},{2,34},{3,35},{4,36},{5,37},{6,38},{7,39},{8,40},{9,... | collective-permute-start | bytes 737288 | tf_op jit(solution)/shard_map/ppermute | solution.py:69
  72.9 10.6 %collective-permute-start.20 = (bf16[4,240,128]{2,1,0:T(8,128)(2,1)}, bf16[4,240,128]{2,1,0:T(8,128)(2,1)S(1)}, u32[]{:S(2)}, u32[]{:S(2)}) collective-permute-start(bf16[4,240,128]{2,1,0:T(8,128)(2,1)} %get-tuple-element.76), channel_id=1, source_target_pairs={{0,64},{1,65},{2,66},{3,67},{4,68},{5,69},{6,70},{7,71},{8,72},{9,... | collective-permute-start | bytes 737288 | tf_op jit(solution)/shard_map/ppermute | solution.py:69
  76.5 7.6 %collective-permute-start.21 = (bf16[4,240,128]{2,1,0:T(8,128)(2,1)}, bf16[4,240,128]{2,1,0:T(8,128)(2,1)S(1)}, u32[]{:S(2)}, u32[]{:S(2)}) collective-permute-start(bf16[4,240,128]{2,1,0:T(8,128)(2,1)} %get-tuple-element.77), channel_id=1, source_target_pairs={{0,96},{1,97},{2,98},{3,99},{4,100},{5,101},{6,102},{7,103},{8,104... | collective-permute-start | bytes 737288 | tf_op jit(solution)/shard_map/ppermute | solution.py:69
  79.4 11.2 %collective-permute-start.25 = (f32[80,384]{1,0:T(8,128)S(1)}, f32[80,384]{1,0:T(8,128)S(1)}, u32[]{:S(2)}, u32[]{:S(2)}) collective-permute-start(f32[80,384]{1,0:T(8,128)S(1)} %constant_dynamic-slice_fusion.1), channel_id=1, source_target_pairs={{0,1},{1,0},{2,3},{3,2},{4,5},{5,4},{6,7},{7,6},{8,9},{9,8},{10,11... | collective-permute-start | bytes 368648 | tf_op jit(solution)/shard_map/ppermute | solution.py:74
  86.0 11.4 %collective-permute-start.13 = (bf16[480,128]{1,0:T(8,128)(2,1)}, bf16[480,128]{1,0:T(8,128)(2,1)S(1)}, u32[]{:S(2)}, u32[]{:S(2)}) collective-permute-start(bf16[480,128]{1,0:T(8,128)(2,1)} %get-tuple-element.65), channel_id=1, source_target_pairs={{0,32},{1,3},{2,34},{3,5},{4,36},{5,7},{6,38},{7,1},{8,40},{9,11},... | collective-permute-start | bytes 368648 | tf_op jit(solution)/shard_map/ppermute | solution.py:69
  86.2 11.1 %collective-permute-start.14 = (bf16[480,128]{1,0:T(8,128)(2,1)}, bf16[480,128]{1,0:T(8,128)(2,1)S(1)}, u32[]{:S(2)}, u32[]{:S(2)}) collective-permute-start(bf16[480,128]{1,0:T(8,128)(2,1)} %get-tuple-element.66), channel_id=1, source_target_pairs={{0,64},{1,5},{2,66},{3,7},{4,68},{5,1},{6,70},{7,3},{8,72},{9,13},... | collective-permute-start | bytes 368648 | tf_op jit(solution)/shard_map/ppermute | solution.py:69
  89.8 7.6 %collective-permute-start.15 = (bf16[480,128]{1,0:T(8,128)(2,1)}, bf16[480,128]{1,0:T(8,128)(2,1)S(1)}, u32[]{:S(2)}, u32[]{:S(2)}) collective-permute-start(bf16[480,128]{1,0:T(8,128)(2,1)} %get-tuple-element.67), channel_id=1, source_target_pairs={{0,96},{1,7},{2,98},{3,1},{4,100},{5,3},{6,102},{7,5},{8,104},{9,1... | collective-permute-start | bytes 368648 | tf_op jit(solution)/shard_map/ppermute | solution.py:69
  101.4 10.5 %collective-permute-start.27 = (f32[288,128]{1,0:T(8,128)S(1)}, f32[288,128]{1,0:T(8,128)S(1)}, u32[]{:S(2)}, u32[]{:S(2)}) collective-permute-start(f32[288,128]{1,0:T(8,128)S(1)} %select_add_fusion.g0), channel_id=1, source_target_pairs={{0,2},{1,3},{2,4},{3,5},{4,6},{5,7},{6,0},{7,1},{8,10},{9,11},{10,... | collective-permute-start | bytes 442376 | tf_op jit(solution)/shard_map/ppermute | solution.py:69
  105.3 8.2 %collective-permute-start.28 = (f32[288,128]{1,0:T(8,128)S(1)}, f32[288,128]{1,0:T(8,128)S(1)}, u32[]{:S(2)}, u32[]{:S(2)}) collective-permute-start(f32[288,128]{1,0:T(8,128)S(1)} %select_add_fusion.g0), channel_id=1, source_target_pairs={{0,4},{1,5},{2,6},{3,7},{4,0},{5,1},{6,2},{7,3},{8,12},{9,13},{10,... | collective-permute-start | bytes 442376 | tf_op jit(solution)/shard_map/ppermute | solution.py:69
  105.3 8.8 %collective-permute-start.29 = (f32[288,128]{1,0:T(8,128)S(1)}, f32[288,128]{1,0:T(8,128)S(1)}, u32[]{:S(2)}, u32[]{:S(2)}) collective-permute-start(f32[288,128]{1,0:T(8,128)S(1)} %select_add_fusion.g0), channel_id=1, source_target_pairs={{0,6},{1,7},{2,0},{3,1},{4,2},{5,3},{6,4},{7,5},{8,14},{9,15},{10,... | collective-permute-start | bytes 442376 | tf_op jit(solution)/shard_map/ppermute | solution.py:69
  107.4 12.3 %collective-permute-start.31 = (f32[80,384]{1,0:T(8,128)S(1)}, f32[80,384]{1,0:T(8,128)S(1)}, u32[]{:S(2)}, u32[]{:S(2)}) collective-permute-start(f32[80,384]{1,0:T(8,128)S(1)} %constant_dynamic-slice_fusion), channel_id=1, source_target_pairs={{0,1},{1,0},{2,3},{3,2},{4,5},{5,4},{6,7},{7,6},{8,9},{9,8},{10,11... | collective-permute-start | bytes 368648 | tf_op jit(solution)/shard_map/ppermute | solution.py:74
  130.3 7.9 %collective-permute-start.38 = (bf16[2,704,128]{2,1,0:T(8,128)(2,1)S(1)}, bf16[2,704,128]{2,1,0:T(8,128)(2,1)S(1)}, u32[]{:S(2)}, u32[]{:S(2)}) collective-permute-start(bf16[2,704,128]{2,1,0:T(8,128)(2,1)S(1)} %pad_maximum_fusion.1.s0), channel_id=1, source_target_pairs={{0,24},{1,97},{2,26},{3,99},{4,28},{5,101},{6,30},{7,103},{8,0},{9... | collective-permute-start | bytes 1081352 | tf_op jit(solution)/shard_map/ppermute | solution.py:69
  133.2 8.7 %collective-permute-start.33 = (bf16[2,704,128]{2,1,0:T(8,128)(2,1)S(1)}, bf16[2,704,128]{2,1,0:T(8,128)(2,1)S(1)}, u32[]{:S(2)}, u32[]{:S(2)}) collective-permute-start(bf16[2,704,128]{2,1,0:T(8,128)(2,1)S(1)} %pad_maximum_fusion.f0), channel_id=1, source_target_pairs={{0,8},{1,33},{2,10},{3,35},{4,12},{5,37},{6,14},{7,39},{8,16},{9,4... | collective-permute-start | bytes 1081352 | tf_op jit(solution)/shard_map/ppermute | solution.py:69
  134.3 11.5 %collective-permute-start.37 = (bf16[2,704,128]{2,1,0:T(8,128)(2,1)S(1)}, bf16[2,704,128]{2,1,0:T(8,128)(2,1)S(1)}, u32[]{:S(2)}, u32[]{:S(2)}) collective-permute-start(bf16[2,704,128]{2,1,0:T(8,128)(2,1)S(1)} %pad_maximum_fusion.1.s0), channel_id=1, source_target_pairs={{0,8},{1,33},{2,10},{3,35},{4,12},{5,37},{6,14},{7,39},{8,16},{9,4... | collective-permute-start | bytes 1081352 | tf_op jit(solution)/shard_map/ppermute | solution.py:69
  135.3 10.5 %collective-permute-start.34 = (bf16[2,704,128]{2,1,0:T(8,128)(2,1)S(1)}, bf16[2,704,128]{2,1,0:T(8,128)(2,1)S(1)}, u32[]{:S(2)}, u32[]{:S(2)}) collective-permute-start(bf16[2,704,128]{2,1,0:T(8,128)(2,1)S(1)} %pad_maximum_fusion.f0), channel_id=1, source_target_pairs={{0,24},{1,97},{2,26},{3,99},{4,28},{5,101},{6,30},{7,103},{8,0},{9... | collective-permute-start | bytes 1081352 | tf_op jit(solution)/shard_map/ppermute | solution.py:69
  138.1 10.4 %collective-permute-start.40 = (bf16[2,704,128]{2,1,0:T(8,128)(2,1)S(1)}, bf16[2,704,128]{2,1,0:T(8,128)(2,1)S(1)}, u32[]{:S(2)}, u32[]{:S(2)}) collective-permute-start(bf16[2,704,128]{2,1,0:T(8,128)(2,1)S(1)} %collective-permute-done.38.s3), channel_id=1, source_target_pairs={{0,24},{1,97},{2,26},{3,99},{4,28},{5,101},{6,30},{7,103},{8,0},{9... | collective-permute-start | bytes 1081352 | tf_op jit(solution)/shard_map/ppermute | solution.py:69
  142.0 8.6 %collective-permute-start.39 = (bf16[2,704,128]{2,1,0:T(8,128)(2,1)S(1)}, bf16[2,704,128]{2,1,0:T(8,128)(2,1)S(1)}, u32[]{:S(2)}, u32[]{:S(2)}) collective-permute-start(bf16[2,704,128]{2,1,0:T(8,128)(2,1)S(1)} %collective-permute-done.33.f1), channel_id=1, source_target_pairs={{0,8},{1,33},{2,10},{3,35},{4,12},{5,37},{6,14},{7,39},{8,16},{9,4... | collective-permute-start | bytes 1081352 | tf_op jit(solution)/shard_map/ppermute | solution.py:69
  (15 other events, 188.8 us)

commit v6 on v5

--- a/solution.py
+++ b/solution.py
@@ -505,9 +505,14 @@
     key_eye = jnp.where(row == column, 1.0, 0.0).astype(f32)[:128, :128]
 
     def product(left, right, exact):
+        if left.shape[0] < left.shape[1]:
+            right = stacked(right, zeros_wide)
         if exact:
             return jnp.dot(left, right, precision=HIGHEST, preferred_element_type=f32)
         return three_products(left, right)
+
+    zeros_wide = jnp.zeros((64, 256), f32)
+    query_gram, query_eye = query_gram[:QH], query_eye[:QH]
 
     def start(gram, eye):
         square = jnp.sum(jnp.sum(gram * eye, axis=1, keepdims=True), axis=0, keepdims=True)
@@ -622,9 +627,9 @@
             yield stack.at[j, rows, :], key_out.at[:, columns(zz, xx, KC, lane)]
 
 
-def assemble_kernel(where, f0, f1, f3, s0, s1, s3, query_out, key_out):
-    for i, stacks in enumerate(((f0, f1, f3), (s0, s1, s3))):
-        for far, stack in zip((0, 1, 3), stacks):
+def assemble_kernel(where, f0, f1, f3, s0, s1, s3, s2, query_out, key_out):
+    for i, stacks in enumerate(((f0, f1, f3), (s0, s1, s3, s2))):
+        for far, stack in zip((0, 1, 3, 2), stacks):
             for source, to in gathered_pieces(where, far, i, stack, query_out, key_out):
                 to[...] = source[...]
 
@@ -636,35 +641,34 @@
     return pl.pallas_call(
         assemble_kernel,
         out_shape=RESULT,
-        in_specs=[SMEM] + [VMEM] * 6,
+        in_specs=[SMEM] + [VMEM] * 7,
         out_specs=(VMEM, VMEM),
         compiler_params=params(16),
         name="assemble",
     )(where, *first, *second)
 
 
-def finish_kernel(where, query_in, key_in, first, second, query_out, key_out, sems):
+def finish_kernel(where, query_in, key_in, first, query_out, key_out, sems):
     copies = []
-    for i, stack in enumerate((first, second)):
-        for source, to in gathered_pieces(where, 2, i, stack, query_out, key_out):
-            copies.append(pltpu.make_async_copy(source, to, sems.at[len(copies)]))
+    for source, to in gathered_pieces(where, 2, 0, first, query_out, key_out):
+        copies.append(pltpu.make_async_copy(source, to, sems.at[len(copies)]))
     for copy in copies:
         copy.start()
     for copy in copies:
         copy.wait()
 
 
-def finish(where, query_out, key_out, first, second):
+def finish(where, query_out, key_out, first):
     return pl.pallas_call(
         finish_kernel,
         out_shape=RESULT,
-        in_specs=[SMEM, HBM, HBM, VMEM, VMEM],
+        in_specs=[SMEM, HBM, HBM, VMEM],
         out_specs=(HBM, HBM),
-        scratch_shapes=[pltpu.SemaphoreType.DMA((20,))],
+        scratch_shapes=[pltpu.SemaphoreType.DMA((10,))],
         input_output_aliases={1: 0, 2: 1},
         compiler_params=params(4),
         name="finish",
-    )(where, *in_hbm(query_out, key_out), first, second)
+    )(where, *in_hbm(query_out, key_out), first)
 
 
 def on_device(grad_query, grad_key, query_weight, key_weight, query_moment, key_moment, max_logits):
@@ -735,9 +739,9 @@
     second_back, first_ahead = along(second, 1), along(first, -1)
     first_far, second_far = along(first_back, 1), along(second_ahead, -1)
     query_out, key_out = assemble(
-        where, (first, first_back, first_ahead), (second, second_back, second_ahead)
-    )
-    query_out, key_out = finish(where, query_out, key_out, first_far, second_far)
+        where, (first, first_back, first_ahead), (second, second_back, second_ahead, second_far)
+    )
+    query_out, key_out = finish(where, query_out, key_out, first_far)
     return (query_out, key_out, new_query_moment, new_key_moment)
 
 

time: 153 us -> 152 us (level)
  transfers between devices with their start and end apart: 41 -> 41, of which waited for: 22 -> 23; matrix products, arithmetic and copies ran while one was open for 1% -> 1% of each run, Pallas kernels for 22% -> 21%
where the time goes in v6:
time: 152 us; the launch traced here: 151 us
  starting transfers between devices  59.8 us (39%)
  waiting for transfers between devices  48 us (32%)
  Pallas kernels  38.8 us (26%)
  between operations  1.81 us (1%)
    ppermute x33, starting transfers between devices, shift(): return lax.ppermute(array, AXES, pairs)  57 us
    ppermute x33, waiting for transfers between devices, shift(): return lax.ppermute(array, AXES, pairs)  45.2 us
    pallas_call x7, Pallas kernels, local(): pl.pallas_call(functools.partial(local_kernel, sum_step, send_step), out_...  20.7 us
    pallas_call x1, Pallas kernels, chain(): pl.pallas_call(chain_kernel, out_shape=out((512, 128), f32), in_specs=[VM...  4.63 us
  transfers between devices with their start and end apart: 41, of which 23 were waited for; matrix products, arithmetic and copies ran while one was open for 1% of the time, Pallas kernels for 21%

profile of v6, /device:TPU:8, one launch (start us, length us, event | category | flops | bytes accessed | tf_op | source)
XLA Modules:
  0.0 151.2 jit_solution(5944659156559615733)
XLA Ops:
  0.7 2.7 %local_sum_None_send_1.1 = bf16[4,4,720,128]{3,2,1,0:T(8,128)(2,1)S(1)} custom-call(s32[4]{0:T(128)S(1)} %pad_add_fusion.where, bf16[4,2,192,6144]{3,2,1,0:T(8,128)(2,1)} %bitcast.12, bf16[4,2,64,4096]{3,2,1,0:T(8,128)(2,1)} %bitcast.19, f32[1,32]{1,0:T(1,128)} %logits.13), custom_call_target="tpu_custom_call" | custom-call | tf_op jit(solution)/shard_map/local_sum_None_send_1/pallas_call | solution.py:288
  3.5 2.7 %local_sum_None_send_2.1 = bf16[4,4,720,128]{3,2,1,0:T(8,128)(2,1)S(1)} custom-call(s32[4]{0:T(128)S(1)} %pad_add_fusion.where, bf16[4,2,192,6144]{3,2,1,0:T(8,128)(2,1)} %bitcast.13, bf16[4,2,64,4096]{3,2,1,0:T(8,128)(2,1)} %bitcast.20, f32[1,32]{1,0:T(1,128)} %logits.13), custom_call_target="tpu_custom_call" | custom-call | tf_op jit(solution)/shard_map/local_sum_None_send_2/pallas_call | solution.py:288
  6.8 2.7 %local_sum_None_send_3.1 = bf16[4,4,720,128]{3,2,1,0:T(8,128)(2,1)S(1)} custom-call(s32[4]{0:T(128)S(1)} %pad_add_fusion.where, bf16[4,2,192,6144]{3,2,1,0:T(8,128)(2,1)} %bitcast.14, bf16[4,2,64,4096]{3,2,1,0:T(8,128)(2,1)} %bitcast.21, f32[1,32]{1,0:T(1,128)} %logits.13), custom_call_target="tpu_custom_call" | custom-call | tf_op jit(solution)/shard_map/local_sum_None_send_3/pallas_call | solution.py:288
  9.6 2.9 %local_sum_1_send_None.1 = (bf16[4,4,240,128]{3,2,1,0:T(8,128)(2,1)S(1)}, bf16[4,4,240,128]{3,2,1,0:T(8,128)(2,1)S(1)}, bf16[4,4,240,128]{3,2,1,0:T(8,128)(2,1)S(1)}) custom-call(s32[4]{0:T(128)S(1)} %pad_add_fusion.where, bf16[4,2,192,6144]{3,2,1,0:T(8,128)(2,1)} %bitcast.15, bf16[4,2,64,4096]{3,2,1,0:T(8,128)(2,1)} %bitcast.22, f32[1,32]{1,0:T(1,128)} %logits.13, ...), custom_call_target="tpu_custom_call" | custom-call | tf_op jit(solution)/shard_map/local_sum_1_send_None/pallas_call | solution.py:288
  12.5 2.8 %collective-permute-start.7 = (bf16[4,4,240,128]{3,2,1,0:T(8,128)(2,1)S(1)}, bf16[4,4,240,128]{3,2,1,0:T(8,128)(2,1)S(1)}, u32[]{:S(2)}, u32[]{:S(2)}) collective-permute-start(bf16[4,4,240,128]{3,2,1,0:T(8,128)(2,1)S(1)} %get-tuple-element.59), channel_id=1, source_target_pairs={{0,24},{1,97},{2,26},{3,99},{4,28},{5,101},{6,30},{7,103},{8,0},{9... | collective-permute-start | bytes 2949128 | tf_op jit(solution)/shard_map/ppermute | solution.py:69
  15.4 3.8 %local_sum_2_send_4.1 = (bf16[4,4,240,128]{3,2,1,0:T(8,128)(2,1)S(1)}, bf16[4,4,240,128]{3,2,1,0:T(8,128)(2,1)S(1)}, bf16[4,4,240,128]{3,2,1,0:T(8,128)(2,1)S(1)}, bf16[4,4,720,128]{3,2,1,0:T(8,128)(2,1)S(1)}) custom-call(s32[4]{0:T(128)S(1)} %pad_add_fusion.where, bf16[4,2,192,6144]{3,2,1,0:T(8,128)(2,1)} %bitcast.16, bf16[4,2,64,4096]{3,2,1,0:T(8,128)(2,1)} %bitcast.23, ...), custom_call_target="tpu_custom_call" | custom-call | tf_op jit(solution)/shard_map/local_sum_2_send_4/pallas_call | solution.py:288
  22.5 4.5 %collective-permute-done.7 = bf16[4,4,240,128]{3,2,1,0:T(8,128)(2,1)S(1)} collective-permute-done((bf16[4,4,240,128]{3,2,1,0:T(8,128)(2,1)S(1)}, bf16[4,4,240,128]{3,2,1,0:T(8,128)(2,1)S(1)}, u32[]{:S(2)}, u32[]{:S(2)}) %collective-permute-start.7) | collective-permute-done | bytes 983072 | tf_op jit(solution)/shard_map/ppermute | solution.py:69
  27.2 3.8 %collective-permute-start.8 = (bf16[4,4,240,128]{3,2,1,0:T(8,128)(2,1)S(1)}, bf16[4,4,240,128]{3,2,1,0:T(8,128)(2,1)S(1)}, u32[]{:S(2)}, u32[]{:S(2)}) collective-permute-start(bf16[4,4,240,128]{3,2,1,0:T(8,128)(2,1)S(1)} %add_convert_fusion.1), channel_id=1, source_target_pairs={{0,24},{1,97},{2,26},{3,99},{4,28},{5,101},{6,30},{7,103},{8,0},{9... | collective-permute-start | bytes 2949128 | tf_op jit(solution)/shard_map/ppermute | solution.py:69
  31.4 2.9 %local_sum_3_send_None.1 = (bf16[4,4,240,128]{3,2,1,0:T(8,128)(2,1)S(1)}, bf16[4,4,240,128]{3,2,1,0:T(8,128)(2,1)S(1)}, bf16[4,4,240,128]{3,2,1,0:T(8,128)(2,1)S(1)}) custom-call(s32[4]{0:T(128)S(1)} %pad_add_fusion.where, bf16[4,2,192,6144]{3,2,1,0:T(8,128)(2,1)} %bitcast.17, bf16[4,2,64,4096]{3,2,1,0:T(8,128)(2,1)} %bitcast.24, f32[1,32]{1,0:T(1,128)} %logits.13, ...), custom_call_target="tpu_custom_call" | custom-call | tf_op jit(solution)/shard_map/local_sum_3_send_None/pallas_call | solution.py:288
  37.1 5.6 %collective-permute-done.8 = bf16[4,4,240,128]{3,2,1,0:T(8,128)(2,1)S(1)} collective-permute-done((bf16[4,4,240,128]{3,2,1,0:T(8,128)(2,1)S(1)}, bf16[4,4,240,128]{3,2,1,0:T(8,128)(2,1)S(1)}, u32[]{:S(2)}, u32[]{:S(2)}) %collective-permute-start.8) | collective-permute-done | bytes 983072 | tf_op jit(solution)/shard_map/ppermute | solution.py:69
  42.9 3.8 %collective-permute-start.9 = (bf16[4,4,240,128]{3,2,1,0:T(8,128)(2,1)S(1)}, bf16[4,4,240,128]{3,2,1,0:T(8,128)(2,1)S(1)}, u32[]{:S(2)}, u32[]{:S(2)}) collective-permute-start(bf16[4,4,240,128]{3,2,1,0:T(8,128)(2,1)S(1)} %add_convert_fusion), channel_id=1, source_target_pairs={{0,24},{1,97},{2,26},{3,99},{4,28},{5,101},{6,30},{7,103},{8,0},{9... | collective-permute-start | bytes 2949128 | tf_op jit(solution)/shard_map/ppermute | solution.py:69
  47.0 2.6 %collective-permute-done.17.second = bf16[4,4,240,128]{3,2,1,0:T(8,128)(2,1)S(1)} collective-permute-done((bf16[4,4,240,128]{3,2,1,0:T(8,128)(2,1)S(1)}, bf16[4,4,240,128]{3,2,1,0:T(8,128)(2,1)S(1)}, u32[]{:S(2)}, u32[]{:S(2)}) %collective-permute-start.17) | collective-permute-done | bytes 983072 | tf_op jit(solution)/shard_map/ppermute | solution.py:69
  51.6 2.9 %local_sum_4_send_None.1 = (bf16[4,4,240,128]{3,2,1,0:T(8,128)(2,1)S(1)}, bf16[4,4,240,128]{3,2,1,0:T(8,128)(2,1)S(1)}, bf16[4,4,240,128]{3,2,1,0:T(8,128)(2,1)S(1)}) custom-call(s32[4]{0:T(128)S(1)} %pad_add_fusion.where, bf16[4,2,192,6144]{3,2,1,0:T(8,128)(2,1)} %bitcast.18, bf16[4,2,64,4096]{3,2,1,0:T(8,128)(2,1)} %bitcast.25, f32[1,32]{1,0:T(1,128)} %logits.13, ...), custom_call_target="tpu_custom_call" | custom-call | tf_op jit(solution)/shard_map/local_sum_4_send_None/pallas_call | solution.py:288
  54.6 3.7 %collective-permute-done.9.m1 = bf16[4,4,240,128]{3,2,1,0:T(8,128)(2,1)S(1)} collective-permute-done((bf16[4,4,240,128]{3,2,1,0:T(8,128)(2,1)S(1)}, bf16[4,4,240,128]{3,2,1,0:T(8,128)(2,1)S(1)}, u32[]{:S(2)}, u32[]{:S(2)}) %collective-permute-start.9) | collective-permute-done | bytes 983072 | tf_op jit(solution)/shard_map/ppermute | solution.py:69
  58.3 4.0 %collective-permute-done.6.p1 = bf16[4,4,240,128]{3,2,1,0:T(8,128)(2,1)S(1)} collective-permute-done((bf16[4,4,240,128]{3,2,1,0:T(8,128)(2,1)S(1)}, bf16[4,4,240,128]{3,2,1,0:T(8,128)(2,1)S(1)}, u32[]{:S(2)}, u32[]{:S(2)}) %collective-permute-start.6) | collective-permute-done | bytes 983072 | tf_op jit(solution)/shard_map/ppermute | solution.py:69
  62.3 2.0 %split_ab.1 = (bf16[4,480,128]{2,1,0:T(8,128)(2,1)S(1)}, bf16[4,480,128]{2,1,0:T(8,128)(2,1)S(1)}, bf16[4,480,128]{2,1,0:T(8,128)(2,1)}, bf16[4,480,128]{2,1,0:T(8,128)(2,1)}) custom-call(s32[4]{0:T(128)S(1)} %pad_add_fusion.where, bf16[4,4,240,128]{3,2,1,0:T(8,128)(2,1)S(1)} %get-tuple-element.52.p0, bf16[4,4,240,128]{3,2,1,0:T(8,128)(2,1)S(1)} %get-tuple-element.53.m0, ...), custom_call_target="tpu_custom_call" | custom-call | tf_op jit(solution)/shard_map/split_ab/pallas_call | solution.py:337
  66.8 2.4 %collective-permute-start.12 = (bf16[4,480,128]{2,1,0:T(8,128)(2,1)}, bf16[4,480,128]{2,1,0:T(8,128)(2,1)S(1)}, u32[]{:S(2)}, u32[]{:S(2)}) collective-permute-start(bf16[4,480,128]{2,1,0:T(8,128)(2,1)} %get-tuple-element.63), channel_id=1, source_target_pairs={{0,6},{1,25},{2,0},{3,27},{4,2},{5,29},{6,4},{7,31},{8,14},{9,1},{... | collective-permute-start | bytes 1474568 | tf_op jit(solution)/shard_map/ppermute | solution.py:69
  72.9 3.6 %collective-permute-start.20 = (bf16[4,240,128]{2,1,0:T(8,128)(2,1)}, bf16[4,240,128]{2,1,0:T(8,128)(2,1)S(1)}, u32[]{:S(2)}, u32[]{:S(2)}) collective-permute-start(bf16[4,240,128]{2,1,0:T(8,128)(2,1)} %get-tuple-element.76), channel_id=1, source_target_pairs={{0,64},{1,65},{2,66},{3,67},{4,68},{5,69},{6,70},{7,71},{8,72},{9,... | collective-permute-start | bytes 737288 | tf_op jit(solution)/shard_map/ppermute | solution.py:69
  86.2 3.6 %collective-permute-start.14 = (bf16[480,128]{1,0:T(8,128)(2,1)}, bf16[480,128]{1,0:T(8,128)(2,1)S(1)}, u32[]{:S(2)}, u32[]{:S(2)}) collective-permute-start(bf16[480,128]{1,0:T(8,128)(2,1)} %get-tuple-element.66), channel_id=1, source_target_pairs={{0,64},{1,5},{2,66},{3,7},{4,68},{5,1},{6,70},{7,3},{8,72},{9,13},... | collective-permute-start | bytes 368648 | tf_op jit(solution)/shard_map/ppermute | solution.py:69
  91.4 2.3 %collective-permute-start.24 = (bf16[240,128]{1,0:T(8,128)(2,1)S(1)}, bf16[240,128]{1,0:T(8,128)(2,1)S(1)}, u32[]{:S(2)}, u32[]{:S(2)}) collective-permute-start(bf16[240,128]{1,0:T(8,128)(2,1)S(1)} %get-tuple-element.81), channel_id=1, source_target_pairs={{0,24},{1,25},{2,26},{3,27},{4,28},{5,29},{6,30},{7,31},{8,0},{9,1... | collective-permute-start | bytes 184328 | tf_op jit(solution)/shard_map/ppermute | solution.py:69
  93.7 2.5 %collective-permute-done.23.c2 = bf16[240,128]{1,0:T(8,128)(2,1)S(1)} collective-permute-done((bf16[240,128]{1,0:T(8,128)(2,1)S(1)}, bf16[240,128]{1,0:T(8,128)(2,1)S(1)}, u32[]{:S(2)}, u32[]{:S(2)}) %collective-permute-start.23) | collective-permute-done | bytes 61472 | tf_op jit(solution)/shard_map/ppermute | solution.py:69
  101.4 3.9 %collective-permute-start.27 = (f32[288,128]{1,0:T(8,128)S(1)}, f32[288,128]{1,0:T(8,128)S(1)}, u32[]{:S(2)}, u32[]{:S(2)}) collective-permute-start(f32[288,128]{1,0:T(8,128)S(1)} %select_add_fusion.g0), channel_id=1, source_target_pairs={{0,2},{1,3},{2,4},{3,5},{4,6},{5,7},{6,0},{7,1},{8,10},{9,11},{10,... | collective-permute-start | bytes 442376 | tf_op jit(solution)/shard_map/ppermute | solution.py:69
  105.3 2.2 %collective-permute-start.29 = (f32[288,128]{1,0:T(8,128)S(1)}, f32[288,128]{1,0:T(8,128)S(1)}, u32[]{:S(2)}, u32[]{:S(2)}) collective-permute-start(f32[288,128]{1,0:T(8,128)S(1)} %select_add_fusion.g0), channel_id=1, source_target_pairs={{0,6},{1,7},{2,0},{3,1},{4,2},{5,3},{6,4},{7,5},{8,14},{9,15},{10,... | collective-permute-start | bytes 442376 | tf_op jit(solution)/shard_map/ppermute | solution.py:69
  107.5 4.3 %collective-permute-done.27.g1 = f32[288,128]{1,0:T(8,128)S(1)} collective-permute-done((f32[288,128]{1,0:T(8,128)S(1)}, f32[288,128]{1,0:T(8,128)S(1)}, u32[]{:S(2)}, u32[]{:S(2)}) %collective-permute-start.27) | collective-permute-done | bytes 147488 | tf_op jit(solution)/shard_map/ppermute | solution.py:69
  114.0 4.6 %newton_schulz_polynomial.1.own = f32[512,128]{1,0:T(8,128)S(1)} custom-call(f32[288,128]{1,0:T(8,128)S(1)} %select_add_fusion.g0, f32[288,128]{1,0:T(8,128)S(1)} %collective-permute-done.27.g1, f32[288,128]{1,0:T(8,128)S(1)} %collective-permute-done.28.g2, f32[288,128]{1,0:T(8,128)S(1)} %collective-permute-done.29.g3), custom_call_target="tpu_custom_call" | custom-call | tf_op jit(solution)/shard_map/newton_schulz_polynomial/pallas_call | solution.py:543
  122.3 2.9 %collective-permute-start.35 = (bf16[704,128]{1,0:T(8,128)(2,1)S(1)}, bf16[704,128]{1,0:T(8,128)(2,1)S(1)}, u32[]{:S(2)}, u32[]{:S(2)}) collective-permute-start(bf16[704,128]{1,0:T(8,128)(2,1)S(1)} %update.1), channel_id=1, source_target_pairs={{0,64},{1,17},{2,66},{3,19},{4,68},{5,21},{6,70},{7,23},{8,72},{9,... | collective-permute-start | bytes 540680 | tf_op jit(solution)/shard_map/ppermute | solution.py:69
  127.0 2.4 %collective-permute-done.35 = bf16[704,128]{1,0:T(8,128)(2,1)S(1)} collective-permute-done((bf16[704,128]{1,0:T(8,128)(2,1)S(1)}, bf16[704,128]{1,0:T(8,128)(2,1)S(1)}, u32[]{:S(2)}, u32[]{:S(2)}) %collective-permute-start.35) | collective-permute-done | bytes 180256 | tf_op jit(solution)/shard_map/ppermute | solution.py:69
  129.3 2.9 %collective-permute-start.38 = (bf16[2,704,128]{2,1,0:T(8,128)(2,1)S(1)}, bf16[2,704,128]{2,1,0:T(8,128)(2,1)S(1)}, u32[]{:S(2)}, u32[]{:S(2)}) collective-permute-start(bf16[2,704,128]{2,1,0:T(8,128)(2,1)S(1)} %pad_maximum_fusion.1.s0), channel_id=1, source_target_pairs={{0,24},{1,97},{2,26},{3,99},{4,28},{5,101},{6,30},{7,103},{8,0},{9... | collective-permute-start | bytes 1081352 | tf_op jit(solution)/shard_map/ppermute | solution.py:69
  134.3 2.2 %collective-permute-start.34 = (bf16[2,704,128]{2,1,0:T(8,128)(2,1)S(1)}, bf16[2,704,128]{2,1,0:T(8,128)(2,1)S(1)}, u32[]{:S(2)}, u32[]{:S(2)}) collective-permute-start(bf16[2,704,128]{2,1,0:T(8,128)(2,1)S(1)} %pad_maximum_fusion.f0), channel_id=1, source_target_pairs={{0,24},{1,97},{2,26},{3,99},{4,28},{5,101},{6,30},{7,103},{8,0},{9... | collective-permute-start | bytes 1081352 | tf_op jit(solution)/shard_map/ppermute | solution.py:69
  137.2 3.7 %collective-permute-start.39 = (bf16[2,704,128]{2,1,0:T(8,128)(2,1)S(1)}, bf16[2,704,128]{2,1,0:T(8,128)(2,1)S(1)}, u32[]{:S(2)}, u32[]{:S(2)}) collective-permute-start(bf16[2,704,128]{2,1,0:T(8,128)(2,1)S(1)} %collective-permute-done.38.s3), channel_id=1, source_target_pairs={{0,24},{1,97},{2,26},{3,99},{4,28},{5,101},{6,30},{7,103},{8,0},{9... | collective-permute-start | bytes 1081352 | tf_op jit(solution)/shard_map/ppermute | solution.py:69
  141.0 3.9 %collective-permute-done.37.s1 = bf16[2,704,128]{2,1,0:T(8,128)(2,1)S(1)} collective-permute-done((bf16[2,704,128]{2,1,0:T(8,128)(2,1)S(1)}, bf16[2,704,128]{2,1,0:T(8,128)(2,1)S(1)}, u32[]{:S(2)}, u32[]{:S(2)}) %collective-permute-start.37) | collective-permute-done | bytes 360480 | tf_op jit(solution)/shard_map/ppermute | solution.py:69
  146.2 2.8 %assemble.1 = (bf16[192,6144]{1,0:T(8,128)(2,1)}, bf16[64,4096]{1,0:T(8,128)(2,1)}) custom-call(s32[4]{0:T(128)S(1)} %pad_add_fusion.where, bf16[2,704,128]{2,1,0:T(8,128)(2,1)S(1)} %pad_maximum_fusion.f0, bf16[2,704,128]{2,1,0:T(8,128)(2,1)S(1)} %collective-permute-done.33.f1, bf16[2,704,128]{2,1,0:T(8,128)(2,1)S(1)} %collective-permute-done.34.f3, ...), custom_call_target="tpu_custom_call" | custom-call | tf_op jit(solution)/shard_map/assemble/pallas_call | solution.py:641
  (95 shorter events, 45.9 us)
Async XLA Ops:
  6.2 9.1 %collective-permute-start.1 = (bf16[4,4,720,128]{3,2,1,0:T(8,128)(2,1)S(1)}, bf16[4,4,720,128]{3,2,1,0:T(8,128)(2,1)S(1)}, u32[]{:S(2)}, u32[]{:S(2)}) collective-permute-start(bf16[4,4,720,128]{3,2,1,0:T(8,128)(2,1)S(1)} %local_sum_None_send_2.1), channel_id=1, source_target_pairs={{0,1},{1,0},{2,3},{3,2},{4,5},{5,4},{6,7},{7,6},{8,9},{9,8},{10,11... | collective-permute-start | bytes 8847368 | tf_op jit(solution)/shard_map/ppermute | solution.py:74
  9.5 21.9 %collective-permute-start.3 = (bf16[4,4,720,128]{3,2,1,0:T(8,128)(2,1)S(1)}, bf16[4,4,720,128]{3,2,1,0:T(8,128)(2,1)S(1)}, u32[]{:S(2)}, u32[]{:S(2)}) collective-permute-start(bf16[4,4,720,128]{3,2,1,0:T(8,128)(2,1)S(1)} %local_sum_None_send_3.1), channel_id=1, source_target_pairs={{0,1},{1,0},{2,3},{3,2},{4,5},{5,4},{6,7},{7,6},{8,9},{9,8},{10,11... | collective-permute-start | bytes 8847368 | tf_op jit(solution)/shard_map/ppermute | solution.py:74
  12.5 14.4 %collective-permute-start.7 = (bf16[4,4,240,128]{3,2,1,0:T(8,128)(2,1)S(1)}, bf16[4,4,240,128]{3,2,1,0:T(8,128)(2,1)S(1)}, u32[]{:S(2)}, u32[]{:S(2)}) collective-permute-start(bf16[4,4,240,128]{3,2,1,0:T(8,128)(2,1)S(1)} %get-tuple-element.59), channel_id=1, source_target_pairs={{0,24},{1,97},{2,26},{3,99},{4,28},{5,101},{6,30},{7,103},{8,0},{9... | collective-permute-start | bytes 2949128 | tf_op jit(solution)/shard_map/ppermute | solution.py:69
  15.4 15.6 %collective-permute-start.4 = (bf16[4,4,240,128]{3,2,1,0:T(8,128)(2,1)S(1)}, bf16[4,4,240,128]{3,2,1,0:T(8,128)(2,1)S(1)}, u32[]{:S(2)}, u32[]{:S(2)}) collective-permute-start(bf16[4,4,240,128]{3,2,1,0:T(8,128)(2,1)S(1)} %get-tuple-element.48), channel_id=1, source_target_pairs={{0,8},{1,33},{2,10},{3,35},{4,12},{5,37},{6,14},{7,39},{8,16},{9,4... | collective-permute-start | bytes 2949128 | tf_op jit(solution)/shard_map/ppermute | solution.py:69
  19.2 32.4 %collective-permute-start.2 = (bf16[4,4,720,128]{3,2,1,0:T(8,128)(2,1)S(1)}, bf16[4,4,720,128]{3,2,1,0:T(8,128)(2,1)S(1)}, u32[]{:S(2)}, u32[]{:S(2)}) collective-permute-start(bf16[4,4,720,128]{3,2,1,0:T(8,128)(2,1)S(1)} %get-tuple-element.51), channel_id=1, source_target_pairs={{0,1},{1,0},{2,3},{3,2},{4,5},{5,4},{6,7},{7,6},{8,9},{9,8},{10,11... | collective-permute-start | bytes 8847368 | tf_op jit(solution)/shard_map/ppermute | solution.py:74
  20.9 14.1 %collective-permute-start.16 = (bf16[4,4,240,128]{3,2,1,0:T(8,128)(2,1)S(1)}, bf16[4,4,240,128]{3,2,1,0:T(8,128)(2,1)S(1)}, u32[]{:S(2)}, u32[]{:S(2)}) collective-permute-start(bf16[4,4,240,128]{3,2,1,0:T(8,128)(2,1)S(1)} %get-tuple-element.73), channel_id=1, source_target_pairs={{0,2},{1,7},{2,4},{3,1},{4,6},{5,3},{6,0},{7,5},{8,10},{9,15},{10,... | collective-permute-start | bytes 2949128 | tf_op jit(solution)/shard_map/ppermute | solution.py:69
  27.2 15.4 %collective-permute-start.8 = (bf16[4,4,240,128]{3,2,1,0:T(8,128)(2,1)S(1)}, bf16[4,4,240,128]{3,2,1,0:T(8,128)(2,1)S(1)}, u32[]{:S(2)}, u32[]{:S(2)}) collective-permute-start(bf16[4,4,240,128]{3,2,1,0:T(8,128)(2,1)S(1)} %add_convert_fusion.1), channel_id=1, source_target_pairs={{0,24},{1,97},{2,26},{3,99},{4,28},{5,101},{6,30},{7,103},{8,0},{9... | collective-permute-start | bytes 2949128 | tf_op jit(solution)/shard_map/ppermute | solution.py:69
  31.3 15.4 %collective-permute-start.5 = (bf16[4,4,240,128]{3,2,1,0:T(8,128)(2,1)S(1)}, bf16[4,4,240,128]{3,2,1,0:T(8,128)(2,1)S(1)}, u32[]{:S(2)}, u32[]{:S(2)}) collective-permute-start(bf16[4,4,240,128]{3,2,1,0:T(8,128)(2,1)S(1)} %add_convert_fusion.3), channel_id=1, source_target_pairs={{0,8},{1,33},{2,10},{3,35},{4,12},{5,37},{6,14},{7,39},{8,16},{9,4... | collective-permute-start | bytes 2949128 | tf_op jit(solution)/shard_map/ppermute | solution.py:69
  35.5 14.2 %collective-permute-start.17 = (bf16[4,4,240,128]{3,2,1,0:T(8,128)(2,1)S(1)}, bf16[4,4,240,128]{3,2,1,0:T(8,128)(2,1)S(1)}, u32[]{:S(2)}, u32[]{:S(2)}) collective-permute-start(bf16[4,4,240,128]{3,2,1,0:T(8,128)(2,1)S(1)} %add_c.2), channel_id=1, source_target_pairs={{0,2},{1,7},{2,4},{3,1},{4,6},{5,3},{6,0},{7,5},{8,10},{9,15},{10,... | collective-permute-start | bytes 2949128 | tf_op jit(solution)/shard_map/ppermute | solution.py:69
  42.9 15.4 %collective-permute-start.9 = (bf16[4,4,240,128]{3,2,1,0:T(8,128)(2,1)S(1)}, bf16[4,4,240,128]{3,2,1,0:T(8,128)(2,1)S(1)}, u32[]{:S(2)}, u32[]{:S(2)}) collective-permute-start(bf16[4,4,240,128]{3,2,1,0:T(8,128)(2,1)S(1)} %add_convert_fusion), channel_id=1, source_target_pairs={{0,24},{1,97},{2,26},{3,99},{4,28},{5,101},{6,30},{7,103},{8,0},{9... | collective-permute-start | bytes 2949128 | tf_op jit(solution)/shard_map/ppermute | solution.py:69
  46.9 15.4 %collective-permute-start.6 = (bf16[4,4,240,128]{3,2,1,0:T(8,128)(2,1)S(1)}, bf16[4,4,240,128]{3,2,1,0:T(8,128)(2,1)S(1)}, u32[]{:S(2)}, u32[]{:S(2)}) collective-permute-start(bf16[4,4,240,128]{3,2,1,0:T(8,128)(2,1)S(1)} %add_convert_fusion.2), channel_id=1, source_target_pairs={{0,8},{1,33},{2,10},{3,35},{4,12},{5,37},{6,14},{7,39},{8,16},{9,4... | collective-permute-start | bytes 2949128 | tf_op jit(solution)/shard_map/ppermute | solution.py:69
  50.0 19.2 %collective-permute-start.18 = (bf16[4,4,240,128]{3,2,1,0:T(8,128)(2,1)S(1)}, bf16[4,4,240,128]{3,2,1,0:T(8,128)(2,1)S(1)}, u32[]{:S(2)}, u32[]{:S(2)}) collective-permute-start(bf16[4,4,240,128]{3,2,1,0:T(8,128)(2,1)S(1)} %add_c.3), channel_id=1, source_target_pairs={{0,2},{1,7},{2,4},{3,1},{4,6},{5,3},{6,0},{7,5},{8,10},{9,15},{10,... | collective-permute-start | bytes 2949128 | tf_op jit(solution)/shard_map/ppermute | solution.py:69
  64.3 12.2 %collective-permute-start.10 = (bf16[4,480,128]{2,1,0:T(8,128)(2,1)S(1)}, bf16[4,480,128]{2,1,0:T(8,128)(2,1)S(1)}, u32[]{:S(2)}, u32[]{:S(2)}) collective-permute-start(bf16[4,480,128]{2,1,0:T(8,128)(2,1)S(1)} %get-tuple-element.61), channel_id=1, source_target_pairs={{0,2},{1,9},{2,4},{3,11},{4,6},{5,13},{6,0},{7,15},{8,10},{9,17},{... | collective-permute-start | bytes 1474568 | tf_op jit(solution)/shard_map/ppermute | solution.py:69
  65.9 13.5 %collective-permute-start.11 = (bf16[4,480,128]{2,1,0:T(8,128)(2,1)}, bf16[4,480,128]{2,1,0:T(8,128)(2,1)S(1)}, u32[]{:S(2)}, u32[]{:S(2)}) collective-permute-start(bf16[4,480,128]{2,1,0:T(8,128)(2,1)} %get-tuple-element.62), channel_id=1, source_target_pairs={{0,4},{1,17},{2,6},{3,19},{4,0},{5,21},{6,2},{7,23},{8,12},{9,25},... | collective-permute-start | bytes 1474568 | tf_op jit(solution)/shard_map/ppermute | solution.py:69
  66.8 14.3 %collective-permute-start.12 = (bf16[4,480,128]{2,1,0:T(8,128)(2,1)}, bf16[4,480,128]{2,1,0:T(8,128)(2,1)S(1)}, u32[]{:S(2)}, u32[]{:S(2)}) collective-permute-start(bf16[4,480,128]{2,1,0:T(8,128)(2,1)} %get-tuple-element.63), channel_id=1, source_target_pairs={{0,6},{1,25},{2,0},{3,27},{4,2},{5,29},{6,4},{7,31},{8,14},{9,1},{... | collective-permute-start | bytes 1474568 | tf_op jit(solution)/shard_map/ppermute | solution.py:69
  71.0 11.6 %collective-permute-start.19 = (bf16[4,240,128]{2,1,0:T(8,128)(2,1)}, bf16[4,240,128]{2,1,0:T(8,128)(2,1)S(1)}, u32[]{:S(2)}, u32[]{:S(2)}) collective-permute-start(bf16[4,240,128]{2,1,0:T(8,128)(2,1)} %get-tuple-element.75), channel_id=1, source_target_pairs={{0,32},{1,33},{2,34},{3,35},{4,36},{5,37},{6,38},{7,39},{8,40},{9,... | collective-permute-start | bytes 737288 | tf_op jit(solution)/shard_map/ppermute | solution.py:69
  72.9 10.6 %collective-permute-start.20 = (bf16[4,240,128]{2,1,0:T(8,128)(2,1)}, bf16[4,240,128]{2,1,0:T(8,128)(2,1)S(1)}, u32[]{:S(2)}, u32[]{:S(2)}) collective-permute-start(bf16[4,240,128]{2,1,0:T(8,128)(2,1)} %get-tuple-element.76), channel_id=1, source_target_pairs={{0,64},{1,65},{2,66},{3,67},{4,68},{5,69},{6,70},{7,71},{8,72},{9,... | collective-permute-start | bytes 737288 | tf_op jit(solution)/shard_map/ppermute | solution.py:69
  76.5 7.6 %collective-permute-start.21 = (bf16[4,240,128]{2,1,0:T(8,128)(2,1)}, bf16[4,240,128]{2,1,0:T(8,128)(2,1)S(1)}, u32[]{:S(2)}, u32[]{:S(2)}) collective-permute-start(bf16[4,240,128]{2,1,0:T(8,128)(2,1)} %get-tuple-element.77), channel_id=1, source_target_pairs={{0,96},{1,97},{2,98},{3,99},{4,100},{5,101},{6,102},{7,103},{8,104... | collective-permute-start | bytes 737288 | tf_op jit(solution)/shard_map/ppermute | solution.py:69
  79.4 11.2 %collective-permute-start.25 = (f32[80,384]{1,0:T(8,128)S(1)}, f32[80,384]{1,0:T(8,128)S(1)}, u32[]{:S(2)}, u32[]{:S(2)}) collective-permute-start(f32[80,384]{1,0:T(8,128)S(1)} %constant_dynamic-slice_fusion.1), channel_id=1, source_target_pairs={{0,1},{1,0},{2,3},{3,2},{4,5},{5,4},{6,7},{7,6},{8,9},{9,8},{10,11... | collective-permute-start | bytes 368648 | tf_op jit(solution)/shard_map/ppermute | solution.py:74
  86.0 11.4 %collective-permute-start.13 = (bf16[480,128]{1,0:T(8,128)(2,1)}, bf16[480,128]{1,0:T(8,128)(2,1)S(1)}, u32[]{:S(2)}, u32[]{:S(2)}) collective-permute-start(bf16[480,128]{1,0:T(8,128)(2,1)} %get-tuple-element.65), channel_id=1, source_target_pairs={{0,32},{1,3},{2,34},{3,5},{4,36},{5,7},{6,38},{7,1},{8,40},{9,11},... | collective-permute-start | bytes 368648 | tf_op jit(solution)/shard_map/ppermute | solution.py:69
  86.2 11.1 %collective-permute-start.14 = (bf16[480,128]{1,0:T(8,128)(2,1)}, bf16[480,128]{1,0:T(8,128)(2,1)S(1)}, u32[]{:S(2)}, u32[]{:S(2)}) collective-permute-start(bf16[480,128]{1,0:T(8,128)(2,1)} %get-tuple-element.66), channel_id=1, source_target_pairs={{0,64},{1,5},{2,66},{3,7},{4,68},{5,1},{6,70},{7,3},{8,72},{9,13},... | collective-permute-start | bytes 368648 | tf_op jit(solution)/shard_map/ppermute | solution.py:69
  89.8 7.6 %collective-permute-start.15 = (bf16[480,128]{1,0:T(8,128)(2,1)}, bf16[480,128]{1,0:T(8,128)(2,1)S(1)}, u32[]{:S(2)}, u32[]{:S(2)}) collective-permute-start(bf16[480,128]{1,0:T(8,128)(2,1)} %get-tuple-element.67), channel_id=1, source_target_pairs={{0,96},{1,7},{2,98},{3,1},{4,100},{5,3},{6,102},{7,5},{8,104},{9,1... | collective-permute-start | bytes 368648 | tf_op jit(solution)/shard_map/ppermute | solution.py:69
  101.4 10.5 %collective-permute-start.27 = (f32[288,128]{1,0:T(8,128)S(1)}, f32[288,128]{1,0:T(8,128)S(1)}, u32[]{:S(2)}, u32[]{:S(2)}) collective-permute-start(f32[288,128]{1,0:T(8,128)S(1)} %select_add_fusion.g0), channel_id=1, source_target_pairs={{0,2},{1,3},{2,4},{3,5},{4,6},{5,7},{6,0},{7,1},{8,10},{9,11},{10,... | collective-permute-start | bytes 442376 | tf_op jit(solution)/shard_map/ppermute | solution.py:69
  105.3 8.2 %collective-permute-start.28 = (f32[288,128]{1,0:T(8,128)S(1)}, f32[288,128]{1,0:T(8,128)S(1)}, u32[]{:S(2)}, u32[]{:S(2)}) collective-permute-start(f32[288,128]{1,0:T(8,128)S(1)} %select_add_fusion.g0), channel_id=1, source_target_pairs={{0,4},{1,5},{2,6},{3,7},{4,0},{5,1},{6,2},{7,3},{8,12},{9,13},{10,... | collective-permute-start | bytes 442376 | tf_op jit(solution)/shard_map/ppermute | solution.py:69
  105.3 8.8 %collective-permute-start.29 = (f32[288,128]{1,0:T(8,128)S(1)}, f32[288,128]{1,0:T(8,128)S(1)}, u32[]{:S(2)}, u32[]{:S(2)}) collective-permute-start(f32[288,128]{1,0:T(8,128)S(1)} %select_add_fusion.g0), channel_id=1, source_target_pairs={{0,6},{1,7},{2,0},{3,1},{4,2},{5,3},{6,4},{7,5},{8,14},{9,15},{10,... | collective-permute-start | bytes 442376 | tf_op jit(solution)/shard_map/ppermute | solution.py:69
  107.4 11.3 %collective-permute-start.31 = (f32[80,384]{1,0:T(8,128)S(1)}, f32[80,384]{1,0:T(8,128)S(1)}, u32[]{:S(2)}, u32[]{:S(2)}) collective-permute-start(f32[80,384]{1,0:T(8,128)S(1)} %constant_dynamic-slice_fusion), channel_id=1, source_target_pairs={{0,1},{1,0},{2,3},{3,2},{4,5},{5,4},{6,7},{7,6},{8,9},{9,8},{10,11... | collective-permute-start | bytes 368648 | tf_op jit(solution)/shard_map/ppermute | solution.py:74
  129.3 7.9 %collective-permute-start.38 = (bf16[2,704,128]{2,1,0:T(8,128)(2,1)S(1)}, bf16[2,704,128]{2,1,0:T(8,128)(2,1)S(1)}, u32[]{:S(2)}, u32[]{:S(2)}) collective-permute-start(bf16[2,704,128]{2,1,0:T(8,128)(2,1)S(1)} %pad_maximum_fusion.1.s0), channel_id=1, source_target_pairs={{0,24},{1,97},{2,26},{3,99},{4,28},{5,101},{6,30},{7,103},{8,0},{9... | collective-permute-start | bytes 1081352 | tf_op jit(solution)/shard_map/ppermute | solution.py:69
  132.3 8.7 %collective-permute-start.33 = (bf16[2,704,128]{2,1,0:T(8,128)(2,1)S(1)}, bf16[2,704,128]{2,1,0:T(8,128)(2,1)S(1)}, u32[]{:S(2)}, u32[]{:S(2)}) collective-permute-start(bf16[2,704,128]{2,1,0:T(8,128)(2,1)S(1)} %pad_maximum_fusion.f0), channel_id=1, source_target_pairs={{0,8},{1,33},{2,10},{3,35},{4,12},{5,37},{6,14},{7,39},{8,16},{9,4... | collective-permute-start | bytes 1081352 | tf_op jit(solution)/shard_map/ppermute | solution.py:69
  133.4 11.5 %collective-permute-start.37 = (bf16[2,704,128]{2,1,0:T(8,128)(2,1)S(1)}, bf16[2,704,128]{2,1,0:T(8,128)(2,1)S(1)}, u32[]{:S(2)}, u32[]{:S(2)}) collective-permute-start(bf16[2,704,128]{2,1,0:T(8,128)(2,1)S(1)} %pad_maximum_fusion.1.s0), channel_id=1, source_target_pairs={{0,8},{1,33},{2,10},{3,35},{4,12},{5,37},{6,14},{7,39},{8,16},{9,4... | collective-permute-start | bytes 1081352 | tf_op jit(solution)/shard_map/ppermute | solution.py:69
  134.3 10.5 %collective-permute-start.34 = (bf16[2,704,128]{2,1,0:T(8,128)(2,1)S(1)}, bf16[2,704,128]{2,1,0:T(8,128)(2,1)S(1)}, u32[]{:S(2)}, u32[]{:S(2)}) collective-permute-start(bf16[2,704,128]{2,1,0:T(8,128)(2,1)S(1)} %pad_maximum_fusion.f0), channel_id=1, source_target_pairs={{0,24},{1,97},{2,26},{3,99},{4,28},{5,101},{6,30},{7,103},{8,0},{9... | collective-permute-start | bytes 1081352 | tf_op jit(solution)/shard_map/ppermute | solution.py:69
  137.2 9.0 %collective-permute-start.39 = (bf16[2,704,128]{2,1,0:T(8,128)(2,1)S(1)}, bf16[2,704,128]{2,1,0:T(8,128)(2,1)S(1)}, u32[]{:S(2)}, u32[]{:S(2)}) collective-permute-start(bf16[2,704,128]{2,1,0:T(8,128)(2,1)S(1)} %collective-permute-done.38.s3), channel_id=1, source_target_pairs={{0,24},{1,97},{2,26},{3,99},{4,28},{5,101},{6,30},{7,103},{8,0},{9... | collective-permute-start | bytes 1081352 | tf_op jit(solution)/shard_map/ppermute | solution.py:69
  141.0 8.6 %collective-permute-start.40 = (bf16[2,704,128]{2,1,0:T(8,128)(2,1)S(1)}, bf16[2,704,128]{2,1,0:T(8,128)(2,1)S(1)}, u32[]{:S(2)}, u32[]{:S(2)}) collective-permute-start(bf16[2,704,128]{2,1,0:T(8,128)(2,1)S(1)} %collective-permute-done.33.f1), channel_id=1, source_target_pairs={{0,8},{1,33},{2,10},{3,35},{4,12},{5,37},{6,14},{7,39},{8,16},{9,4... | collective-permute-start | bytes 1081352 | tf_op jit(solution)/shard_map/ppermute | solution.py:69
  (15 other events, 187.5 us)
